TPU v7x, 128 devices: a whole 4x4x4 slice. The times are simulated.
128 devices in a mesh: tx: 8 (over z, core), ty: 16 (over y, x).
Axes of the slice: x: 4, y: 4, z: 4, core: 2. Of those that a mesh axis runs over, the one named last changes fastest.
Arguments:
- adjoint_start: float32 [4, 4, 1024, 4096], P(None, None, 'tx', 'ty'), may hold values from -6 to 6
- mixing_h: float32 [4, 1024, 4096], P(None, 'tx', 'ty'), may hold values from 0.02 to 0.12
- mixing_v: float32 [3, 1024, 4096], P(None, 'tx', 'ty'), may hold values from 0.05 to 0.2
- courant: float32 [2, 4, 1024, 4096], P(None, None, 'tx', 'ty'), may hold values from -0.15 to 0.15
- coriolis: float32 [1024, 4096], P('tx', 'ty'), may hold values from -0.3 to 0.3
- misfit: float32 [2, 8, 524288], P(None, None, ('tx', 'ty')), may hold values from -6 to 6
- owner: int32 [2, 524288, 1], P(None, ('tx', 'ty')), may hold values from 0 to 127; in each aligned block of 4096 rows (0 to 4095, 4096 to 8191, ..., all dimensions but the last counted through in order) at most 64 rows name the same one
- column: int32 [2, 524288], P(None, ('tx', 'ty')), may hold values from 0 to 32767
Outputs:
- adjoint_end: float32 [4, 4, 1024, 4096], P(None, None, 'tx', 'ty')
Inputs may be any that keep to these rules, and one draw needn't show every extreme that they name: `owner`: among the records of one device for one step, no tile is named more than 64 times, and in every draw some such block names one tile exactly 64 times.
All inputs are finite; a program needn't handle non-finite values.
Results may differ from a plain program's by a relative error of at most 0.0003.
Values sent between devices are 32-bit elements; how exact they have to be, the bound alone decides.
No kernel may reach another device: no remote copies, remote signals or barrier semaphores. Data moves between devices by JAX's collectives and lax.ppermute only.
A program may use at most 128 MiB of HBM per device.

v0:
```python
import math

import jax
import jax.numpy as jnp
from jax import lax
from jax.sharding import PartitionSpec as P

CA = 128
CB = 256
LEV = 4
STEPS = 2
CAP = 64


def with_halo(cells, sides, width):
    for axis, dim in sides:
        count = lax.axis_size(axis)
        ends = count - 1
        head = lax.slice_in_dim(cells, 0, width, axis=dim)
        tail = lax.slice_in_dim(cells, cells.shape[dim] - width, cells.shape[dim], axis=dim)
        cells = jnp.concatenate(
            [
                lax.ppermute(tail, axis, [(i, (i + 1) % count) for i in range(ends)]),
                cells,
                lax.ppermute(head, axis, [((i + 1) % count, i) for i in range(ends)]),
            ],
            axis=dim,
        )
    return cells


def advance(padded, adjoint, mixing_h, mixing_v, courant, coriolis, forcing):
    upper_row = padded[:, :, 2:, 1:-1]
    lower_row = padded[:, :, :-2, 1:-1]
    right_col = padded[:, :, 1:-1, 2:]
    left_col = padded[:, :, 1:-1, :-2]
    laplacian = upper_row + lower_row + right_col + left_col - 4.0 * adjoint
    transport = 0.5 * courant[0] * (upper_row - lower_row) + 0.5 * courant[1] * (
        right_col - left_col
    )
    vertical_flux = mixing_v * (adjoint[:, 1:] - adjoint[:, :-1])
    vertical = jnp.pad(vertical_flux, ((0, 0), (0, 1), (0, 0), (0, 0))) - jnp.pad(
        vertical_flux, ((0, 0), (1, 0), (0, 0), (0, 0))
    )
    updated = adjoint + mixing_h * laplacian + transport + vertical
    rotation = coriolis * jnp.stack([adjoint[3], -adjoint[2]])
    return updated + jnp.concatenate([forcing, rotation], axis=0)


def slot_numbers(target, devices):
    record_count = target.shape[0]
    block_len = math.gcd(record_count, 1024)
    block_count = record_count // block_len
    position = jnp.arange(block_len)
    earlier = (position[:, None] > position[None, :]).astype(jnp.bfloat16)
    tiles = jnp.arange(devices, dtype=jnp.int32)

    def advance_block(counts, block_target):
        onehot = (block_target[:, None] == tiles[None, :]).astype(jnp.bfloat16)
        before = jnp.dot(earlier, onehot, preferred_element_type=jnp.float32)
        weights = onehot.astype(jnp.float32)
        slot_list = jnp.sum((before + counts[None, :]) * weights, axis=1)
        return (counts + jnp.sum(weights, axis=0), slot_list)

    counts, slot_list = lax.scan(
        advance_block, jnp.zeros((devices,), jnp.float32), target.reshape(block_count, block_len)
    )
    return slot_list.reshape(record_count).astype(jnp.int32)


def fill_send(values, target, slot_list, column_ids, devices):
    stacked = jnp.concatenate([values, column_ids.astype(jnp.float32)[None, :]], axis=0)
    slot_hot = (slot_list[None, :] == jnp.arange(CAP, dtype=jnp.int32)[:, None]).astype(jnp.float32)
    tile_hot = (target[:, None] == jnp.arange(devices, dtype=jnp.int32)[None, :]).astype(
        jnp.float32
    )
    spread = stacked[:, None, :] * slot_hot[None, :, :]
    buffer = jnp.einsum("kcr,rd->kdc", spread, tile_hot, precision=lax.Precision.HIGHEST)
    send_vals = buffer[: 2 * LEV].reshape(2 * LEV, devices * CAP)
    send_ids = buffer[2 * LEV].reshape(devices * CAP).astype(jnp.int32)
    return (send_vals, send_ids)


def place_records(values, column_ids):
    slot_count = column_ids.shape[0]
    block_len = math.gcd(slot_count, 1024)
    block_count = slot_count // block_len
    value_blocks = values.reshape(2 * LEV, block_count, block_len).transpose(1, 0, 2)
    id_blocks = column_ids.reshape(block_count, block_len)
    row_range = jnp.arange(CA, dtype=jnp.int32)
    col_range = jnp.arange(CB, dtype=jnp.int32)

    def add_block(total, pieces):
        block_vals, block_ids = pieces
        row_hot = (block_ids[None, :] // CB == row_range[:, None]).astype(jnp.float32)
        col_hot = (block_ids[:, None] % CB == col_range[None, :]).astype(jnp.float32)
        spread = (block_vals[:, None, :] * row_hot[None, :, :]).reshape(2 * LEV * CA, block_len)
        return (
            total
            + jnp.dot(
                spread, col_hot, precision=lax.Precision.HIGHEST, preferred_element_type=jnp.float32
            ),
            None,
        )

    total, unused = lax.scan(
        add_block, jnp.zeros((2 * LEV * CA, CB), jnp.float32), (value_blocks, id_blocks)
    )
    return total.reshape(2, LEV, CA, CB)


def deliver(record_vals, owner, column):
    tiles_x = lax.axis_size("tx")
    tiles_y = lax.axis_size("ty")
    devices = tiles_x * tiles_y
    step_count = record_vals.shape[0]
    target = owner[:, :, 0]
    slot_list = slot_numbers(target[0], devices)
    one_vals, one_ids = fill_send(record_vals[0], target[0], slot_list, column[0], devices)
    send_list = [one_vals]
    ids_list = [one_ids]
    send_vals = jnp.stack(send_list)
    send_ids = jnp.stack(ids_list)
    arrived_vals, arrived_ids = (
        lax.all_to_all(
            send_vals.reshape(step_count, 2 * LEV, devices, CAP),
            ("tx", "ty"),
            split_axis=2,
            concat_axis=2,
            tiled=True,
        ),
        lax.all_to_all(
            send_ids.reshape(step_count, 1, devices, CAP),
            ("tx", "ty"),
            split_axis=2,
            concat_axis=2,
            tiled=True,
        ),
    )
    arrived_vals = arrived_vals.reshape(step_count, 2 * LEV, devices * CAP)
    arrived_ids = arrived_ids.reshape(step_count, devices * CAP)
    placed = [place_records(arrived_vals[0], arrived_ids[0])]
    return jnp.stack(placed)


def local(adjoint_start, mixing_h, mixing_v, courant, coriolis, misfit, owner, column):
    adjoint = adjoint_start
    for step_index in range(STEPS):
        forcing = deliver(
            misfit[step_index : step_index + 1],
            owner[step_index : step_index + 1],
            column[step_index : step_index + 1],
        )[0]
        padded = with_halo(adjoint, (("tx", 2), ("ty", 3)), 1)
        adjoint = advance(padded, adjoint, mixing_h, mixing_v, courant, coriolis, forcing)
    return adjoint


def solution(mesh):
    return jax.shard_map(
        local,
        mesh=mesh,
        in_specs=(
            P(None, None, "tx", "ty"),
            P(None, "tx", "ty"),
            P(None, "tx", "ty"),
            P(None, None, "tx", "ty"),
            P("tx", "ty"),
            P(None, None, ("tx", "ty")),
            P(None, ("tx", "ty"), None),
            P(None, ("tx", "ty")),
        ),
        out_specs=P(None, None, "tx", "ty"),
        check_vma=False,
    )
```

profile of v0, /device:TPU:9, one launch (start us, length us, event | category | flops | bytes accessed | tf_op | source)
XLA Modules:
  0.0 232.1 jit_solution(2226040363877881090)
XLA Ops:
  1.6 4.1 %collective-permute-start.1 = (f32[4,4,1,256]{3,2,1,0:T(1,128)}, f32[4,4,1,256]{3,2,1,0:T(1,128)S(1)}, u32[]{:S(2)}, u32[]{:S(2)}) collective-permute-start(f32[4,4,1,256]{3,2,1,0:T(1,128)} %get-tuple-element.383), channel_id=1, source_target_pairs={{0,16},{16,32},{32,48},{48,64},{64,80},{80,96},{96,112},{1,17},{17... | collective-permute-start | bytes 49160 | tf_op jit(solution)/shard_map/ppermute | solution.py:23
  9.9 3.6 %while.52 = (s32[]{:T(128)}, f32[128]{0:T(128)S(1)}, f32[4,1024]{1,0:T(4,128)S(1)}, s32[4,1024]{1,0:T(4,128)S(1)}, s32[]{:T(128)}, /*index=5*/s32[]{:T(128)}) while((s32[]{:T(128)}, f32[128]{0:T(128)S(1)}, f32[4,1024]{1,0:T(4,128)S(1)}, s32[4,1024]{1,0:T(4,128)S(1)}, s32[]{:T(128)}, /*index=5*/s32[]{:T(128)}) %tuple.120), condition=%wide.region_3.4_spmd.clone, body=%wide.region_0.3_spmd.clone.sunk | while | flops 271973504 | bytes 31839 | solution.py:65
  14.4 4.9 %fusion.69 = f32[9,128,64]{1,2,0:T(8,128)S(1)} fusion(f32[64,4096]{1,0:T(8,128)S(1)} %fusion.81, f32[9,4096]{1,0:T(8,128)S(1)} %get-tuple-element.395, s32[4096]{0:T(1024)S(1)} %bitcast.143), kind=kOutput, calls=%fused_computation.103 | convolution fusion | flops 3626762240 | bytes 1507328 | tf_op jit(solution)/shard_map/kcr,rd->kdc/dot_general | solution.py:78
  20.0 10.8 %all-to-all-start.1 = ((s32[1,1,128,64]{3,1,0,2:T(1,128)}), s32[1,1,128,64]{3,1,0,2:T(1,128)}, u32[]{:S(2)}, u32[]{:S(2)}) async-start(s32[1,1,128,64]{3,1,0,2:T(1,128)} %copy.46), calls=%async_computation.1 | async-start | bytes 131072 | tf_op jit(solution)/shard_map/all_to_all | solution.py:132
  32.2 8.6 %while.54 = (s32[]{:T(128)}, f32[128]{0:T(128)S(1)}, f32[4,1024]{1,0:T(4,128)}, s32[4,1024]{1,0:T(4,128)S(1)}, s32[]{:T(128)}, /*index=5*/s32[]{:T(128)}) while((s32[]{:T(128)}, f32[128]{0:T(128)S(1)}, f32[4,1024]{1,0:T(4,128)}, s32[4,1024]{1,0:T(4,128)S(1)}, s32[]{:T(128)}, /*index=5*/s32[]{:T(128)}) %tuple.126), condition=%wide.region_9.10_spmd.clone, body=%wide.region_6.9_spmd.clone.sunk | while | flops 271973504 | bytes 31839 | solution.py:65
  45.4 4.9 %fusion.74 = f32[9,128,64]{1,2,0:T(8,128)S(1)} fusion(f32[64,4096]{1,0:T(8,128)S(1)} %fusion.82, f32[9,4096]{1,0:T(8,128)S(1)} %copy-done.7, s32[4096]{0:T(1024)S(1)} %bitcast.142), kind=kOutput, calls=%fused_computation.104 | convolution fusion | flops 3626762240 | bytes 1507328 | tf_op jit(solution)/shard_map/kcr,rd->kdc/dot_general | solution.py:78
  54.3 9.8 %all-to-all-start.3 = ((s32[1,1,128,64]{3,1,0,2:T(1,128)}), s32[1,1,128,64]{3,1,0,2:T(1,128)S(1)}, u32[]{:S(2)}, u32[]{:S(2)}) async-start(s32[1,1,128,64]{3,1,0,2:T(1,128)} %copy.54), calls=%async_computation.3 | async-start | bytes 131072 | tf_op jit(solution)/shard_map/all_to_all | solution.py:132
  66.5 6.1 %all-to-all-done.3 = s32[1,1,128,64]{3,1,0,2:T(1,128)S(1)} async-done(((s32[1,1,128,64]{3,1,0,2:T(1,128)}), s32[1,1,128,64]{3,1,0,2:T(1,128)S(1)}, u32[]{:S(2)}, u32[]{:S(2)}) %all-to-all-start.3) | async-done | bytes 32800 | tf_op jit(solution)/shard_map/all_to_all | solution.py:132
  73.2 5.5 %all-to-all-start = ((f32[128,1,512]{2,1,0:T(1,128)}), f32[128,1,512]{2,1,0:T(1,128)S(1)}, u32[]{:S(2)}, u32[]{:S(2)}) async-start(f32[128,1,512]{2,1,0:T(1,128)} %reshape.253), calls=%async_computation | async-start | bytes 524288 | tf_op jit(solution)/shard_map/all_to_all | solution.py:125
  83.2 3.1 %collective-permute-start.3 = (f32[4,4,130,1]{2,1,3,0:T(4,128)}, f32[4,4,130,1]{2,1,3,0:T(4,128)}, u32[]{:S(2)}, u32[]{:S(2)}) collective-permute-start(f32[4,4,130,1]{2,1,3,0:T(4,128)} %copy.42), channel_id=1, source_target_pairs={{0,1},{1,2},{2,3},{3,4},{4,5},{5,6},{6,7},{7,8},{8,9},{9,10},{10,1... | collective-permute-start | bytes 24968 | tf_op jit(solution)/shard_map/ppermute | solution.py:23
  86.2 4.3 %collective-permute-start.2 = (f32[4,4,130,1]{2,1,3,0:T(4,128)}, f32[4,4,130,1]{2,1,3,0:T(4,128)}, u32[]{:S(2)}, u32[]{:S(2)}) collective-permute-start(f32[4,4,130,1]{2,1,3,0:T(4,128)} %copy.40), channel_id=1, source_target_pairs={{1,0},{2,1},{3,2},{4,3},{5,4},{6,5},{7,6},{8,7},{9,8},{10,9},{11,1... | collective-permute-start | bytes 24968 | tf_op jit(solution)/shard_map/ppermute | solution.py:25
  100.5 12.4 %all-to-all-start.2 = ((f32[128,1,512]{2,1,0:T(1,128)}), f32[128,1,512]{2,1,0:T(1,128)}, u32[]{:S(2)}, u32[]{:S(2)}) async-start(f32[128,1,512]{2,1,0:T(1,128)} %reshape.255), calls=%async_computation.2 | async-start | bytes 524288 | tf_op jit(solution)/shard_map/all_to_all | solution.py:125
  115.2 32.7 %while.53 = (s32[]{:T(128)}, f32[1024,256]{1,0:T(8,128)S(1)}, f32[8,8,1024]{2,0,1:T(8,128)S(1)}, s32[8,1024]{1,0:T(8,128)}, s32[]{:T(128)}, /*index=5*/s32[]{:T(128)}) while((s32[]{:T(128)}, f32[1024,256]{1,0:T(8,128)S(1)}, f32[8,8,1024]{2,0,1:T(8,128)S(1)}, s32[8,1024]{1,0:T(8,128)}, s32[]{:T(128)}, /*index=5*/s32[]{:T(128)}) %tuple.133), condition=%wide.region_5.6_spmd.clone, body=%wide.region_4.5_spmd.clone.sunk | while | flops 3223349248 | bytes 11726943 | solution.py:106
  116.6 2.6 %convolution_add_fusion.4 = f32[1024,256]{1,0:T(8,128)S(1)} fusion(f32[1024,1024]{1,0:T(8,128)S(1)} %bitcast.118, f32[1024,256]{1,0:T(8,128)S(1)} %get-tuple-element.538, s32[1024]{0:T(1024)S(1)} %add_select_fusion.4, pred[]{:T(512)S(6)} %compare.31), kind=kOutput, calls=%fused_computation.22.clone.1 | convolution fusion | flops 3222011904 | bytes 6295553 | tf_op jit(solution)/shard_map/while/body/eval_jaxpr/dot_general | solution.py:100
  120.7 2.6 %convolution_add_fusion.4 = f32[1024,256]{1,0:T(8,128)S(1)} fusion(f32[1024,1024]{1,0:T(8,128)S(1)} %bitcast.118, f32[1024,256]{1,0:T(8,128)S(1)} %get-tuple-element.538, s32[1024]{0:T(1024)S(1)} %add_select_fusion.4, pred[]{:T(512)S(6)} %compare.31), kind=kOutput, calls=%fused_computation.22.clone.1 | convolution fusion | flops 3222011904 | bytes 6295553 | tf_op jit(solution)/shard_map/while/body/eval_jaxpr/dot_general | solution.py:100
  124.8 2.6 %convolution_add_fusion.4 = f32[1024,256]{1,0:T(8,128)S(1)} fusion(f32[1024,1024]{1,0:T(8,128)S(1)} %bitcast.118, f32[1024,256]{1,0:T(8,128)S(1)} %get-tuple-element.538, s32[1024]{0:T(1024)S(1)} %add_select_fusion.4, pred[]{:T(512)S(6)} %compare.31), kind=kOutput, calls=%fused_computation.22.clone.1 | convolution fusion | flops 3222011904 | bytes 6295553 | tf_op jit(solution)/shard_map/while/body/eval_jaxpr/dot_general | solution.py:100
  128.9 2.6 %convolution_add_fusion.4 = f32[1024,256]{1,0:T(8,128)S(1)} fusion(f32[1024,1024]{1,0:T(8,128)S(1)} %bitcast.118, f32[1024,256]{1,0:T(8,128)S(1)} %get-tuple-element.538, s32[1024]{0:T(1024)S(1)} %add_select_fusion.4, pred[]{:T(512)S(6)} %compare.31), kind=kOutput, calls=%fused_computation.22.clone.1 | convolution fusion | flops 3222011904 | bytes 6295553 | tf_op jit(solution)/shard_map/while/body/eval_jaxpr/dot_general | solution.py:100
  133.0 2.6 %convolution_add_fusion.4 = f32[1024,256]{1,0:T(8,128)S(1)} fusion(f32[1024,1024]{1,0:T(8,128)S(1)} %bitcast.118, f32[1024,256]{1,0:T(8,128)S(1)} %get-tuple-element.538, s32[1024]{0:T(1024)S(1)} %add_select_fusion.4, pred[]{:T(512)S(6)} %compare.31), kind=kOutput, calls=%fused_computation.22.clone.1 | convolution fusion | flops 3222011904 | bytes 6295553 | tf_op jit(solution)/shard_map/while/body/eval_jaxpr/dot_general | solution.py:100
  137.0 2.6 %convolution_add_fusion.4 = f32[1024,256]{1,0:T(8,128)S(1)} fusion(f32[1024,1024]{1,0:T(8,128)S(1)} %bitcast.118, f32[1024,256]{1,0:T(8,128)S(1)} %get-tuple-element.538, s32[1024]{0:T(1024)S(1)} %add_select_fusion.4, pred[]{:T(512)S(6)} %compare.31), kind=kOutput, calls=%fused_computation.22.clone.1 | convolution fusion | flops 3222011904 | bytes 6295553 | tf_op jit(solution)/shard_map/while/body/eval_jaxpr/dot_general | solution.py:100
  141.1 2.6 %convolution_add_fusion.4 = f32[1024,256]{1,0:T(8,128)S(1)} fusion(f32[1024,1024]{1,0:T(8,128)S(1)} %bitcast.118, f32[1024,256]{1,0:T(8,128)S(1)} %get-tuple-element.538, s32[1024]{0:T(1024)S(1)} %add_select_fusion.4, pred[]{:T(512)S(6)} %compare.31), kind=kOutput, calls=%fused_computation.22.clone.1 | convolution fusion | flops 3222011904 | bytes 6295553 | tf_op jit(solution)/shard_map/while/body/eval_jaxpr/dot_general | solution.py:100
  145.2 2.6 %convolution_add_fusion.4 = f32[1024,256]{1,0:T(8,128)S(1)} fusion(f32[1024,1024]{1,0:T(8,128)S(1)} %bitcast.118, f32[1024,256]{1,0:T(8,128)S(1)} %get-tuple-element.538, s32[1024]{0:T(1024)S(1)} %add_select_fusion.4, pred[]{:T(512)S(6)} %compare.31), kind=kOutput, calls=%fused_computation.22.clone.1 | convolution fusion | flops 3222011904 | bytes 6295553 | tf_op jit(solution)/shard_map/while/body/eval_jaxpr/dot_general | solution.py:100
  148.8 9.0 %maximum_add_fusion = f32[4,4,128,256]{3,2,1,0:T(8,128)S(1)} fusion(f32[2,4,128,256]{3,2,1,0:T(8,128)} %maximum_multiply_fusion, f32[2,4,128,256]{3,2,1,0:T(8,128)} %bitcast.121, f32[4,3,128,256]{3,2,1,0:T(8,128)} %subtract_multiply_fusion, f32[4,4,128,256]{3,2,1,0:T(8,128)} %param.16, f32[4,4,1,256]{3,2,1,0:T(1,128)} %collective-permute-done, ...), kind=kLoop, calls=%fused_computation.94 | loop fusion | flops 13107200 | bytes 9486592 | tf_op jit(solution)/shard_map/add | solution.py:47
  165.6 32.7 %while.55 = (s32[]{:T(128)}, f32[1024,256]{1,0:T(8,128)S(1)}, f32[8,8,1024]{2,0,1:T(8,128)S(1)}, s32[8,1024]{1,0:T(8,128)}, s32[]{:T(128)}, /*index=5*/s32[]{:T(128)}) while((s32[]{:T(128)}, f32[1024,256]{1,0:T(8,128)S(1)}, f32[8,8,1024]{2,0,1:T(8,128)S(1)}, s32[8,1024]{1,0:T(8,128)}, s32[]{:T(128)}, ...), condition=%wide.region_11.12_spmd.clone, body=%wide.region_10.11_spmd.clone.sunk | while | flops 3223349248 | bytes 11726943 | solution.py:106
  167.0 2.6 %convolution_add_fusion.5 = f32[1024,256]{1,0:T(8,128)S(1)} fusion(f32[1024,1024]{1,0:T(8,128)S(1)} %bitcast.119, f32[1024,256]{1,0:T(8,128)S(1)} %get-tuple-element.574, s32[1024]{0:T(1024)S(1)} %add_select_fusion.5, pred[]{:T(512)S(6)} %compare.33), kind=kOutput, calls=%fused_computation.52.clone.1 | convolution fusion | flops 3222011904 | bytes 6295553 | tf_op jit(solution)/shard_map/while/body/eval_jaxpr/dot_general | solution.py:100
  171.1 2.6 %convolution_add_fusion.5 = f32[1024,256]{1,0:T(8,128)S(1)} fusion(f32[1024,1024]{1,0:T(8,128)S(1)} %bitcast.119, f32[1024,256]{1,0:T(8,128)S(1)} %get-tuple-element.574, s32[1024]{0:T(1024)S(1)} %add_select_fusion.5, pred[]{:T(512)S(6)} %compare.33), kind=kOutput, calls=%fused_computation.52.clone.1 | convolution fusion | flops 3222011904 | bytes 6295553 | tf_op jit(solution)/shard_map/while/body/eval_jaxpr/dot_general | solution.py:100
  175.2 2.6 %convolution_add_fusion.5 = f32[1024,256]{1,0:T(8,128)S(1)} fusion(f32[1024,1024]{1,0:T(8,128)S(1)} %bitcast.119, f32[1024,256]{1,0:T(8,128)S(1)} %get-tuple-element.574, s32[1024]{0:T(1024)S(1)} %add_select_fusion.5, pred[]{:T(512)S(6)} %compare.33), kind=kOutput, calls=%fused_computation.52.clone.1 | convolution fusion | flops 3222011904 | bytes 6295553 | tf_op jit(solution)/shard_map/while/body/eval_jaxpr/dot_general | solution.py:100
  179.3 2.6 %convolution_add_fusion.5 = f32[1024,256]{1,0:T(8,128)S(1)} fusion(f32[1024,1024]{1,0:T(8,128)S(1)} %bitcast.119, f32[1024,256]{1,0:T(8,128)S(1)} %get-tuple-element.574, s32[1024]{0:T(1024)S(1)} %add_select_fusion.5, pred[]{:T(512)S(6)} %compare.33), kind=kOutput, calls=%fused_computation.52.clone.1 | convolution fusion | flops 3222011904 | bytes 6295553 | tf_op jit(solution)/shard_map/while/body/eval_jaxpr/dot_general | solution.py:100
  183.4 2.6 %convolution_add_fusion.5 = f32[1024,256]{1,0:T(8,128)S(1)} fusion(f32[1024,1024]{1,0:T(8,128)S(1)} %bitcast.119, f32[1024,256]{1,0:T(8,128)S(1)} %get-tuple-element.574, s32[1024]{0:T(1024)S(1)} %add_select_fusion.5, pred[]{:T(512)S(6)} %compare.33), kind=kOutput, calls=%fused_computation.52.clone.1 | convolution fusion | flops 3222011904 | bytes 6295553 | tf_op jit(solution)/shard_map/while/body/eval_jaxpr/dot_general | solution.py:100
  198.3 3.5 %collective-permute-start.5 = (f32[4,4,1,256]{3,2,1,0:T(1,128)S(1)}, f32[4,4,1,256]{3,2,1,0:T(1,128)S(1)}, u32[]{:S(2)}, u32[]{:S(2)}) collective-permute-start(f32[4,4,1,256]{3,2,1,0:T(1,128)S(1)} %get-tuple-element.379), channel_id=1, source_target_pairs={{0,16},{16,32},{32,48},{48,64},{64,80},{80,96},{96,112},{1,17},{17... | collective-permute-start | bytes 49160 | tf_op jit(solution)/shard_map/ppermute | solution.py:23
  212.5 3.1 %collective-permute-start.7 = (f32[4,4,130,1]{2,1,3,0:T(4,128)S(1)}, f32[4,4,130,1]{2,1,3,0:T(4,128)S(1)}, u32[]{:S(2)}, u32[]{:S(2)}) collective-permute-start(f32[4,4,130,1]{2,1,3,0:T(4,128)S(1)} %copy.50), channel_id=1, source_target_pairs={{0,1},{1,2},{2,3},{3,4},{4,5},{5,6},{6,7},{7,8},{8,9},{9,10},{10,1... | collective-permute-start | bytes 24968 | tf_op jit(solution)/shard_map/ppermute | solution.py:23
  215.7 4.5 %collective-permute-start.6 = (f32[4,4,130,1]{2,1,3,0:T(4,128)S(1)}, f32[4,4,130,1]{2,1,3,0:T(4,128)S(1)}, u32[]{:S(2)}, u32[]{:S(2)}) collective-permute-start(f32[4,4,130,1]{2,1,3,0:T(4,128)S(1)} %copy.48), channel_id=1, source_target_pairs={{1,0},{2,1},{3,2},{4,3},{5,4},{6,5},{7,6},{8,7},{9,8},{10,9},{11,1... | collective-permute-start | bytes 24968 | tf_op jit(solution)/shard_map/ppermute | solution.py:25
  225.3 6.8 %maximum_add_fusion.1 = f32[4,4,128,256]{3,2,1,0:T(8,128)} fusion(f32[2,4,128,256]{3,2,1,0:T(8,128)} %maximum_multiply_fusion.1, f32[2,4,128,256]{3,2,1,0:T(8,128)S(1)} %bitcast.120, f32[4,3,128,256]{3,2,1,0:T(8,128)} %fusion.68, f32[4,4,128,256]{3,2,1,0:T(8,128)S(1)} %maximum_add_fusion, f32[4,4,1,256]{3,2,1,0:T(1,128)S(1)} %collective-permute-done.4, ...), kind=kLoop, calls=%fused_computation.95 | loop fusion | flops 13107200 | bytes 9486592 | tf_op jit(solution)/shard_map/add | solution.py:47
  (239 shorter events, 103.6 us)
Async XLA Ops:
  1.6 62.5 %collective-permute-start.1 = (f32[4,4,1,256]{3,2,1,0:T(1,128)}, f32[4,4,1,256]{3,2,1,0:T(1,128)S(1)}, u32[]{:S(2)}, u32[]{:S(2)}) collective-permute-start(f32[4,4,1,256]{3,2,1,0:T(1,128)} %get-tuple-element.383), channel_id=1, source_target_pairs={{0,16},{16,32},{32,48},{48,64},{64,80},{80,96},{96,112},{1,17},{17... | collective-permute-start | bytes 49160 | tf_op jit(solution)/shard_map/ppermute | solution.py:23
  5.7 58.4 %collective-permute-start = (f32[4,4,1,256]{3,2,1,0:T(1,128)}, f32[4,4,1,256]{3,2,1,0:T(1,128)}, u32[]{:S(2)}, u32[]{:S(2)}) collective-permute-start(f32[4,4,1,256]{3,2,1,0:T(1,128)} %get-tuple-element.384), channel_id=1, source_target_pairs={{16,0},{32,16},{48,32},{64,48},{80,64},{96,80},{112,96},{17,1},{33... | collective-permute-start | bytes 49160 | tf_op jit(solution)/shard_map/ppermute | solution.py:25
  9.9 3.6 %copy-start.8 = (f32[2,8,4096]{2,1,0:T(8,128)S(1)}, f32[2,8,4096]{2,1,0:T(8,128)}, u32[]{:S(2)}) copy-start(f32[2,8,4096]{2,1,0:T(8,128)} %param.21) | copy-start | bytes 786436
  14.4 17.1 %copy-start.1 = (f32[4,4,128,256]{3,2,1,0:T(8,128)S(1)}, f32[4,4,128,256]{3,2,1,0:T(8,128)}, u32[]{:S(2)}) copy-start(f32[4,4,128,256]{3,2,1,0:T(8,128)} %param.16) | copy-start | bytes 6291460
  20.0 34.3 %all-to-all-start.1 = ((s32[1,1,128,64]{3,1,0,2:T(1,128)}), s32[1,1,128,64]{3,1,0,2:T(1,128)}, u32[]{:S(2)}, u32[]{:S(2)}) async-start(s32[1,1,128,64]{3,1,0,2:T(1,128)} %copy.46), calls=%async_computation.1 | async-start | bytes 131072 | tf_op jit(solution)/shard_map/all_to_all | solution.py:132
  40.8 3.2 %copy-start.2 = (f32[3,128,256]{2,1,0:T(8,128)S(1)}, f32[3,128,256]{2,1,0:T(8,128)}, u32[]{:S(2)}) copy-start(f32[3,128,256]{2,1,0:T(8,128)} %param.18) | copy-start | bytes 1179652
  44.0 1.4 copy-start.7
  44.0 1.4 copy-start.11
  45.4 4.9 %copy-start.3 = (f32[128,256]{1,0:T(8,128)S(1)}, f32[128,256]{1,0:T(8,128)}, u32[]{:S(2)}) copy-start(f32[128,256]{1,0:T(8,128)} %param.20) | copy-start | bytes 393220
  50.3 1.1 copy-start.5
  54.3 18.3 %all-to-all-start.3 = ((s32[1,1,128,64]{3,1,0,2:T(1,128)}), s32[1,1,128,64]{3,1,0,2:T(1,128)S(1)}, u32[]{:S(2)}, u32[]{:S(2)}) async-start(s32[1,1,128,64]{3,1,0,2:T(1,128)} %copy.54), calls=%async_computation.3 | async-start | bytes 131072 | tf_op jit(solution)/shard_map/all_to_all | solution.py:132
  72.6 0.6 copy-start.9
  73.2 27.3 %all-to-all-start = ((f32[128,1,512]{2,1,0:T(1,128)}), f32[128,1,512]{2,1,0:T(1,128)S(1)}, u32[]{:S(2)}, u32[]{:S(2)}) async-start(f32[128,1,512]{2,1,0:T(1,128)} %reshape.253), calls=%async_computation | async-start | bytes 524288 | tf_op jit(solution)/shard_map/all_to_all | solution.py:125
  80.7 9.8 %copy-start.6 = (f32[9,128,64]{1,2,0:T(8,128)S(1)}, f32[9,128,64]{1,2,0:T(8,128)}, u32[]{:S(2)}) copy-start(f32[9,128,64]{1,2,0:T(8,128)} %copy-done.5) | copy-start | bytes 884740
  83.2 10.9 %collective-permute-start.3 = (f32[4,4,130,1]{2,1,3,0:T(4,128)}, f32[4,4,130,1]{2,1,3,0:T(4,128)}, u32[]{:S(2)}, u32[]{:S(2)}) collective-permute-start(f32[4,4,130,1]{2,1,3,0:T(4,128)} %copy.42), channel_id=1, source_target_pairs={{0,1},{1,2},{2,3},{3,4},{4,5},{5,6},{6,7},{7,8},{8,9},{9,10},{10,1... | collective-permute-start | bytes 24968 | tf_op jit(solution)/shard_map/ppermute | solution.py:23
  86.2 5.7 %collective-permute-start.2 = (f32[4,4,130,1]{2,1,3,0:T(4,128)}, f32[4,4,130,1]{2,1,3,0:T(4,128)}, u32[]{:S(2)}, u32[]{:S(2)}) collective-permute-start(f32[4,4,130,1]{2,1,3,0:T(4,128)} %copy.40), channel_id=1, source_target_pairs={{1,0},{2,1},{3,2},{4,3},{5,4},{6,5},{7,6},{8,7},{9,8},{10,9},{11,1... | collective-permute-start | bytes 24968 | tf_op jit(solution)/shard_map/ppermute | solution.py:25
  90.9 8.2 %copy-start.10 = (s32[1,1,128,64]{3,1,0,2:T(1,128)S(1)}, s32[1,1,128,64]{3,1,0,2:T(1,128)}, u32[]{:S(2)}) copy-start(s32[1,1,128,64]{3,1,0,2:T(1,128)} %copy-done.9) | copy-start | bytes 98308
  100.5 58.7 %all-to-all-start.2 = ((f32[128,1,512]{2,1,0:T(1,128)}), f32[128,1,512]{2,1,0:T(1,128)}, u32[]{:S(2)}, u32[]{:S(2)}) async-start(f32[128,1,512]{2,1,0:T(1,128)} %reshape.255), calls=%async_computation.2 | async-start | bytes 524288 | tf_op jit(solution)/shard_map/all_to_all | solution.py:125
  147.9 1.0 copy-start
  198.3 6.5 %collective-permute-start.5 = (f32[4,4,1,256]{3,2,1,0:T(1,128)S(1)}, f32[4,4,1,256]{3,2,1,0:T(1,128)S(1)}, u32[]{:S(2)}, u32[]{:S(2)}) collective-permute-start(f32[4,4,1,256]{3,2,1,0:T(1,128)S(1)} %get-tuple-element.379), channel_id=1, source_target_pairs={{0,16},{16,32},{32,48},{48,64},{64,80},{80,96},{96,112},{1,17},{17... | collective-permute-start | bytes 49160 | tf_op jit(solution)/shard_map/ppermute | solution.py:23
  201.8 5.1 %collective-permute-start.4 = (f32[4,4,1,256]{3,2,1,0:T(1,128)S(1)}, f32[4,4,1,256]{3,2,1,0:T(1,128)S(1)}, u32[]{:S(2)}, u32[]{:S(2)}) collective-permute-start(f32[4,4,1,256]{3,2,1,0:T(1,128)S(1)} %get-tuple-element.380), channel_id=1, source_target_pairs={{16,0},{32,16},{48,32},{64,48},{80,64},{96,80},{112,96},{17,1},{33... | collective-permute-start | bytes 49160 | tf_op jit(solution)/shard_map/ppermute | solution.py:25
  208.8 11.4 %copy-start.4 = (f32[128,256]{1,0:T(8,128)S(1)}, f32[128,256]{1,0:T(8,128)}, u32[]{:S(2)}) copy-start(f32[128,256]{1,0:T(8,128)} %param.20) | copy-start | bytes 393220
  212.5 11.4 %collective-permute-start.7 = (f32[4,4,130,1]{2,1,3,0:T(4,128)S(1)}, f32[4,4,130,1]{2,1,3,0:T(4,128)S(1)}, u32[]{:S(2)}, u32[]{:S(2)}) collective-permute-start(f32[4,4,130,1]{2,1,3,0:T(4,128)S(1)} %copy.50), channel_id=1, source_target_pairs={{0,1},{1,2},{2,3},{3,4},{4,5},{5,6},{6,7},{7,8},{8,9},{9,10},{10,1... | collective-permute-start | bytes 24968 | tf_op jit(solution)/shard_map/ppermute | solution.py:23
  215.7 6.8 %collective-permute-start.6 = (f32[4,4,130,1]{2,1,3,0:T(4,128)S(1)}, f32[4,4,130,1]{2,1,3,0:T(4,128)S(1)}, u32[]{:S(2)}, u32[]{:S(2)}) collective-permute-start(f32[4,4,130,1]{2,1,3,0:T(4,128)S(1)} %copy.48), channel_id=1, source_target_pairs={{1,0},{2,1},{3,2},{4,3},{5,4},{6,5},{7,6},{8,7},{9,8},{10,9},{11,1... | collective-permute-start | bytes 24968 | tf_op jit(solution)/shard_map/ppermute | solution.py:25
where the time goes:
time: 235 us; the launch traced here: 232 us
  starting transfers between devices  64.9 us (28%)
  other arithmetic  59.4 us (25%)
  matrix products  56.6 us (24%)
  local copies, waits for them, and re-layouts  41.3 us (18%)
  waiting for transfers between devices  8.21 us (3%)
    dot_general x16, matrix products, add_block(): jnp.dot(spread, col_hot, precision=lax.Precision.HIGHEST, preferred_eleme...  41.9 us
    all_to_all x2, starting transfers between devices, deliver(): lax.all_to_all(send_ids.reshape(step_count, 1, devices, CAP), ('tx', 'ty'...  20.5 us
    all_to_all x2, starting transfers between devices, deliver(): lax.all_to_all(send_vals.reshape(step_count, 2 * LEV, devices, CAP), ('tx...  17.9 us
    add x2, other arithmetic, advance(): return updated + jnp.concatenate([forcing, rotation], axis=0)  15.8 us
    ppermute x4, starting transfers between devices, with_halo(): lax.ppermute(tail, axis, [(i, (i + 1) % count) for i in range(ends)])  13.8 us
    ppermute x4, starting transfers between devices, with_halo(): lax.ppermute(head, axis, [((i + 1) % count, i) for i in range(ends)])  12.7 us
    select_n x16, other arithmetic, add_block(): block_ids[None, :] // CB == row_range[:, None]  12.6 us
    dot_general x2, matrix products, fill_send(): jnp.einsum('kcr,rd->kdc', spread, tile_hot, precision=lax.Precision.HIGHEST)  9.71 us
  transfers between devices with their start and end apart: 12, of which 2 were waited for; matrix products, arithmetic and copies ran while one was open for 44% of the time, Pallas kernels for 0%

commit v1 on v0

v1 whole, which is shorter than its diff:
```python
import functools
import jax
import jax.numpy as jnp
from jax import lax
from jax.experimental import pallas as pl
from jax.experimental.pallas import tpu as pltpu
from jax.sharding import PartitionSpec as P

CA, CB, LEV, STEPS, CAP = 128, 256, 4, 2, 64
VALS = 2 * LEV
WORDS = VALS + 1
CHUNK = 256
BF = jnp.bfloat16
NT = (((1,), (1,)), ((), ()))


def halves(x):
    top = x.astype(BF)
    return top, (x - top.astype(jnp.float32)).astype(BF)


def pack_kernel(devices, span, owner_ref, column_ref, misfit_ref, out_ref, acc_ref, place_ref):
    records = owner_ref.shape[2]
    groups = devices // 4
    r = lax.broadcasted_iota(jnp.int32, (CHUNK, CHUNK), 0)
    c = lax.broadcasted_iota(jnp.int32, (CHUNK, CHUNK), 1)
    earlier = (r < c).astype(jnp.float32).astype(BF)
    tiles = lax.broadcasted_iota(jnp.int32, (devices, CHUNK), 0)

    counts = [jnp.zeros((devices, 1), jnp.float32)] * STEPS
    for i in range(records // CHUNK):
        at = pl.ds(i * CHUNK, CHUNK)
        for t in range(STEPS):
            target = owner_ref[t, :, at]
            hot = tiles == target
            ones = hot.astype(jnp.float32)
            before = jnp.dot(ones.astype(BF), earlier, preferred_element_type=jnp.float32)
            slot = jnp.sum(jnp.where(hot, before + counts[t], 0.0), axis=0, keepdims=True)
            counts[t] = counts[t] + before[:, CHUNK - 1 :] + ones[:, CHUNK - 1 :]
            place_ref[t, :, at] = (target & 3) * CAP + slot.astype(jnp.int32)

    acc_ref[...] = jnp.zeros_like(acc_ref)
    group_row = lax.broadcasted_iota(jnp.int32, (groups, span), 0)
    place_row = lax.broadcasted_iota(jnp.int32, (CHUNK, span), 0)

    def body(i, carry):
        at = pl.ds(pl.multiple_of(i * span, span), span)
        for t in range(STEPS):
            group_hot = (group_row == (owner_ref[t, :, at] >> 2)).astype(jnp.float32).astype(BF)
            place_hot = (place_row == place_ref[t, :, at]).astype(jnp.float32).astype(BF)
            cell = column_ref[t : t + 1, at]
            high, low = halves(misfit_ref[t, :, at])
            row = (cell - (cell & (CB - 1))).astype(jnp.float32).astype(BF)
            col = ((cell & (CB - 1)) + 1).astype(jnp.float32).astype(BF)
            lhs_h = jnp.concatenate([group_hot * high[k : k + 1] for k in range(VALS)] + [group_hot * row], axis=0)
            lhs_l = jnp.concatenate([group_hot * low[k : k + 1] for k in range(VALS)] + [group_hot * col], axis=0)
            lhs = jnp.concatenate([lhs_h, lhs_l], axis=1)
            rhs = jnp.concatenate([place_hot, place_hot], axis=1)
            acc_ref[t] += lax.dot_general(lhs, rhs, NT, preferred_element_type=jnp.float32)
        return carry

    lax.fori_loop(0, records // span, body, 0)
    left = lax.broadcasted_iota(jnp.int32, (groups, 128), 1) < CAP
    for k in range(WORDS):
        for j in range(2):
            a = acc_ref[0, pl.ds(k * groups, groups), pl.ds(j * 128, 128)]
            b = acc_ref[1, pl.ds(k * groups, groups), pl.ds(j * 128, 128)]
            out_ref[pl.ds(2 * j * WORDS + k, groups, stride=4 * WORDS), :] = jnp.where(left, a, pltpu.roll(b, CAP, 1))
            out_ref[pl.ds((2 * j + 1) * WORDS + k, groups, stride=4 * WORDS), :] = jnp.where(left, pltpu.roll(a, CAP, 1), b)


def pack(owner, column, misfit, devices, span=512):
    return pl.pallas_call(
        functools.partial(pack_kernel, devices, span),
        out_shape=jax.ShapeDtypeStruct((devices * WORDS, 128), jnp.float32),
        in_specs=[pl.BlockSpec(memory_space=pltpu.VMEM)] * 3,
        out_specs=pl.BlockSpec(memory_space=pltpu.VMEM),
        scratch_shapes=[pltpu.VMEM((STEPS, WORDS * devices // 4, CHUNK), jnp.float32), pltpu.VMEM((STEPS, 1, 4096), jnp.int32)],
        compiler_params=pltpu.CompilerParams(vmem_limit_bytes=48 << 20),
        name="pack",
    )(owner, column, misfit)


def exchange(keys, span, reach):
    sub = lax.broadcasted_iota(jnp.int32, (8, 128), 0)
    count = len(keys)
    keys = list(keys)
    if reach < count:
        for v in range(count):
            w = v ^ reach
            if v > w:
                continue
            low, high = jnp.minimum(keys[v], keys[w]), jnp.maximum(keys[v], keys[w])
            if span < count:
                keys[v], keys[w] = (high, low) if v & span else (low, high)
            elif span < 8 * count:
                down = (sub & (span // count)) != 0
                keys[v], keys[w] = jnp.where(down, high, low), jnp.where(down, low, high)
            else:
                keys[v], keys[w] = low, high
        return keys
    step = reach // count
    upper = (sub & step) != 0
    if span < 8 * count:
        upper = upper != ((sub & (span // count)) != 0)
    for v in range(count):
        other = jnp.where((sub & step) != 0, pltpu.roll(keys[v], step, 0), pltpu.roll(keys[v], 8 - step, 0))
        keys[v] = jnp.where(upper, jnp.maximum(keys[v], other), jnp.minimum(keys[v], other))
    return keys


def sort_rows(keys):
    span = 2
    while span <= 8 * len(keys):
        reach = span // 2
        while reach:
            keys = exchange(keys, span, reach)
            reach //= 2
        span *= 2
    return keys


def order_kernel(got_ref, high_ref, low_ref, cell_ref):
    lanes = lax.broadcasted_iota(jnp.int32, (128, 128), 1)
    left = lanes < CAP

    def list_of(k):
        a = got_ref[pl.ds(k, 64, stride=WORDS), :]
        b = got_ref[pl.ds(64 * WORDS + k, 64, stride=WORDS), :]
        first = jnp.where(left[:64], a, pltpu.roll(b, CAP, 1))
        second = jnp.where(left[:64], pltpu.roll(a, CAP, 1), b)
        return jnp.concatenate([first, second], axis=0)

    ids = list_of(VALS).astype(jnp.int32)
    slot = lanes & (CAP - 1)
    spread = ((slot & 1) << 5) | ((slot & 2) << 3) | ((slot & 4) << 1) | ((slot & 8) >> 1) | ((slot & 16) >> 3) | ((slot & 32) >> 5)
    idle = ((spread << 1) | (lanes >> 6)) << 8
    key = (jnp.where(ids > 0, ids - 1, idle) << 7) | lanes
    turned = key.astype(jnp.float32).T
    keys = sort_rows([turned[8 * v : 8 * v + 8] for v in range(16)])
    keys = jnp.concatenate(keys, axis=0).astype(jnp.int32)
    source = (keys & 127).astype(jnp.float32).T.astype(jnp.int32)

    def place(ref, k, x):
        for v in range(0, 16, 2):
            a, b = x[8 * v : 8 * v + 8], x[8 * v + 8 : 8 * v + 16]
            g, h = v // 4, (v // 2) % 2
            l8 = left[:8]
            ref[0, k, pl.ds(8 * g, 8), pl.ds(128 * h, 128)] = jnp.where(l8, a, pltpu.roll(b, CAP, 1))
            ref[1, k, pl.ds(8 * g, 8), pl.ds(128 * h, 128)] = jnp.where(l8, pltpu.roll(a, CAP, 1), b)

    place(cell_ref, 0, (keys >> 7).astype(jnp.float32))
    for k in range(VALS):
        moved = jnp.take_along_axis(list_of(k), source, axis=1).T
        top = moved.astype(BF).astype(jnp.float32)
        place(high_ref, k, top)
        place(low_ref, k, moved - top)


def bounds_of(cell_ref, edge_ref):
    chunk = lax.broadcasted_iota(jnp.int32, (32, 128), 0)
    lane = lax.broadcasted_iota(jnp.int32, (32, 128), 1)
    lines = []
    for t in range(STEPS):
        row = cell_ref[t, 0].astype(jnp.int32) >> 8
        least = jnp.min(jnp.minimum(row[:, :128], row[:, 128:]).astype(jnp.float32), axis=1, keepdims=True)
        most = jnp.max(jnp.maximum(row[:, :128], row[:, 128:]).astype(jnp.float32), axis=1, keepdims=True)
        lines += [jnp.sum(jnp.where(chunk == lane, e, 0.0), axis=0, keepdims=True) for e in (least, most)]
    edge_ref[...] = jnp.concatenate(lines + [jnp.zeros((4, 128), jnp.float32)], axis=0).astype(jnp.int32)


def products(t, i, base, window, keep, high_ref, low_ref, cell_ref):
    row_iota = lax.broadcasted_iota(jnp.int32, (window, CHUNK), 0) + base
    col_iota = lax.broadcasted_iota(jnp.int32, (CB, CHUNK), 0)
    cell = cell_ref[t, 0, pl.ds(i, 1), :].astype(jnp.int32)
    col_hot = (col_iota == (cell & (CB - 1))).astype(jnp.float32).astype(BF)
    hit = row_iota == (cell >> 8)
    if keep is not None:
        hit = hit & (row_iota >= keep)
    row_hot = hit.astype(jnp.float32).astype(BF)
    lhs = jnp.concatenate([row_hot * ref[t, k, pl.ds(i, 1), :].astype(BF) for ref in (high_ref, low_ref) for k in range(VALS)], axis=0)
    out = lax.dot_general(lhs, col_hot, NT, preferred_element_type=jnp.float32)
    return out[: VALS * window] + out[VALS * window :]


def spread_step(t, window, unroll, high_ref, low_ref, cell_ref, edge_ref, acc_ref):
    def gain(base, out):
        for k in range(VALS):
            acc_ref[k, pl.ds(base, window), :] += out[k * window : (k + 1) * window]

    def first(i):
        return pl.multiple_of(jnp.minimum((edge_ref[2 * t, i] >> 3) << 3, CA - window), 8)

    def body(j, carry):
        chunks = [j * unroll + u for u in range(unroll)]
        bases = [first(i) for i in chunks]
        outs = [products(t, i, base, window, None, high_ref, low_ref, cell_ref) for i, base in zip(chunks, bases)]
        for base, out in zip(bases, outs):
            gain(base, out)
        return carry

    lax.fori_loop(0, 32 // unroll, body, 0)

    def rest(i, carry):
        def more(start):
            base = pl.multiple_of(jnp.minimum(start, CA - window), 8)
            gain(base, products(t, i, base, window, start, high_ref, low_ref, cell_ref))
            return start + window

        lax.while_loop(lambda start: start <= edge_ref[2 * t + 1, i], more, first(i) + window)
        return carry

    lax.fori_loop(0, 32, rest, 0)


FIELDS = 4
PLANES = FIELDS * LEV


def edge_lines(plane, top_ref, bottom_ref, left_ref, right_ref):
    lane = lax.broadcasted_iota(jnp.int32, (CA, 128), 1)
    picked = jnp.zeros((CA, 128), jnp.float32)
    for p in range(PLANES):
        top_ref[p : p + 1, :] = plane(p, pl.ds(0, 8), pl.ds(0, CB))[:1]
        bottom_ref[p : p + 1, :] = plane(p, pl.ds(CA - 8, 8), pl.ds(0, CB))[7:]
        picked = jnp.where(lane == p, plane(p, pl.ds(0, CA), pl.ds(0, 128))[:, :1], picked)
        picked = jnp.where(lane == PLANES + p, plane(p, pl.ds(0, CA), pl.ds(CB - 128, 128))[:, 127:], picked)
    lines = picked.T
    left_ref[...] = lines[:PLANES]
    right_ref[...] = lines[PLANES : 2 * PLANES]


EDGES = (
    jax.ShapeDtypeStruct((PLANES, CB), jnp.float32),
    jax.ShapeDtypeStruct((PLANES, CB), jnp.float32),
    jax.ShapeDtypeStruct((PLANES, CA), jnp.float32),
    jax.ShapeDtypeStruct((PLANES, CA), jnp.float32),
)
WHOLE = pl.BlockSpec(memory_space=pltpu.VMEM)
ANYWHERE = pl.BlockSpec(memory_space=pl.ANY)
PARAMS = pltpu.CompilerParams(vmem_limit_bytes=48 << 20)


def first_edges_kernel(state_ref, after_ref, *edge_refs):
    edge_lines(lambda p, rows, cols: state_ref[p, rows, cols], *edge_refs)


def first_edges(state, after):
    return pl.pallas_call(
        first_edges_kernel,
        out_shape=EDGES,
        in_specs=[WHOLE, ANYWHERE],
        out_specs=[WHOLE] * 4,
        compiler_params=PARAMS,
        name="first_edges",
    )(state, after)


def trade(edges):
    top, bottom, left, right = edges

    def moved(x, axis, forward):
        ends = lax.axis_size(axis) - 1
        pairs = [(i, i + 1) if forward else (i + 1, i) for i in range(ends)]
        return lax.ppermute(x, axis, pairs)

    return moved(bottom, "tx", True), moved(top, "tx", False), moved(right, "ty", True), moved(left, "ty", False)


def step_kernel(forced, ts_ref, uv_ref, before_ref, after_ref, prior_ref, next_ref, mix_h_ref, mix_v_ref, courant_ref, turn_ref, *rest):
    forcing_ref, out_ref, state_ref, column_ref, sem = rest if forced else (None, *rest)
    half = PLANES // 2
    loads = [
        pltpu.make_async_copy(ts_ref.at[pl.ds(0, half)], state_ref.at[pl.ds(0, half), pl.ds(8, CA)], sem.at[0]),
        pltpu.make_async_copy(uv_ref.at[pl.ds(half, half)], state_ref.at[pl.ds(half, half), pl.ds(8, CA)], sem.at[1]),
    ]
    for load in loads:
        load.start()
    for p in range(PLANES):
        state_ref[p, 0:8, :] = jnp.broadcast_to(before_ref[p : p + 1, :], (8, CB))
        state_ref[p, CA + 8 : CA + 16, :] = jnp.broadcast_to(after_ref[p : p + 1, :], (8, CB))
    column_ref[...] = jnp.concatenate([prior_ref[...], next_ref[...], jnp.zeros((128 - 2 * PLANES, CA), jnp.float32)], axis=0).T
    for load in loads:
        load.wait()
    sub = lax.broadcasted_iota(jnp.int32, (8, CB), 0)
    lane = lax.broadcasted_iota(jnp.int32, (8, CB), 1)

    def strip(i, carry):
        at = pl.multiple_of(i * 8, 8)
        rows = pl.ds(at, 8)
        sides = column_ref[rows, :]
        turn = turn_ref[rows, :]
        mix_v = [mix_v_ref[k, rows, :] for k in range(LEV - 1)]
        centre = [state_ref[p, pl.ds(at + 8, 8), :] for p in range(PLANES)]
        for k in range(LEV):
            mix_h = mix_h_ref[k, rows, :]
            c0 = 0.5 * courant_ref[0, k, rows, :]
            c1 = 0.5 * courant_ref[1, k, rows, :]
            for f in range(FIELDS):
                p = f * LEV + k
                a = centre[p]
                below = state_ref[p, rows, :]
                above = state_ref[p, pl.ds(at + 16, 8), :]
                up = jnp.where(sub == 7, pltpu.roll(above, 7, 0), pltpu.roll(a, 7, 0))
                down = jnp.where(sub == 0, pltpu.roll(below, 1, 0), pltpu.roll(a, 1, 0))
                right = jnp.where(lane == CB - 1, sides[:, PLANES + p : PLANES + p + 1], pltpu.roll(a, CB - 1, 1))
                left = jnp.where(lane == 0, sides[:, p : p + 1], pltpu.roll(a, 1, 1))
                new = a + mix_h * (up + down + right + left - 4.0 * a) + c0 * (up - down) + c1 * (right - left)
                if k < LEV - 1:
                    new = new + mix_v[k] * (centre[p + 1] - a)
                if k > 0:
                    new = new - mix_v[k - 1] * (a - centre[p - 1])
                if f == 2:
                    new = new + turn * centre[p + LEV]
                if f == 3:
                    new = new - turn * centre[p - LEV]
                if forced and f < 2:
                    new = new + forcing_ref[p, rows, :]
                out_ref[p, rows, :] = new
        return carry

    lax.fori_loop(0, CA // 8, strip, 0)


def step(ts, uv, halos, coefficients, forcing=None):
    extra = () if forcing is None else (forcing,)
    return pl.pallas_call(
        functools.partial(step_kernel, forcing is not None),
        out_shape=jax.ShapeDtypeStruct((PLANES, CA, CB), jnp.float32),
        in_specs=[ANYWHERE] * 2 + [WHOLE] * (8 + len(extra)),
        out_specs=WHOLE,
        scratch_shapes=[pltpu.VMEM((PLANES, CA + 16, CB), jnp.float32), pltpu.VMEM((CA, 128), jnp.float32), pltpu.SemaphoreType.DMA((2,))],
        compiler_params=PARAMS,
        name="advance",
    )(ts, uv, *halos, *coefficients, *extra)


LISTS = (
    jax.ShapeDtypeStruct((STEPS, VALS, 32, CHUNK), jnp.float32),
    jax.ShapeDtypeStruct((STEPS, VALS, 32, CHUNK), jnp.float32),
    jax.ShapeDtypeStruct((STEPS, 1, 32, CHUNK), jnp.float32),
    jax.ShapeDtypeStruct((8, 128), jnp.int32),
)
WINDOW, UNROLL = 40, 8


def first_records_kernel(got_ref, still_ref, ts_ref, high_ref, low_ref, cell_ref, edge_ref, top_ref, bottom_ref, left_ref, right_ref, smem_ref, sem):
    order_kernel(got_ref, high_ref, low_ref, cell_ref)
    bounds_of(cell_ref, edge_ref)
    copy = pltpu.make_async_copy(edge_ref, smem_ref, sem)
    copy.start()
    ts_ref[...] = still_ref[: PLANES // 2]
    copy.wait()
    spread_step(0, WINDOW, UNROLL, high_ref, low_ref, cell_ref, smem_ref, ts_ref)
    half = PLANES // 2
    edge_lines(lambda p, rows, cols: (ts_ref if p < half else still_ref)[p, rows, cols], top_ref, bottom_ref, left_ref, right_ref)


def first_records(got, still):
    out = pl.pallas_call(
        first_records_kernel,
        out_shape=(jax.ShapeDtypeStruct((PLANES // 2, CA, CB), jnp.float32),) + LISTS + EDGES,
        in_specs=[WHOLE] * 2,
        out_specs=[WHOLE] * 9,
        scratch_shapes=[pltpu.SMEM((8, 128), jnp.int32), pltpu.SemaphoreType.DMA(())],
        compiler_params=PARAMS,
        name="first_records",
    )(got, still)
    return out[0], out[1:5], out[5:]


def second_records_kernel(high_ref, low_ref, cell_ref, edge_ref, out_ref):
    out_ref[...] = jnp.zeros_like(out_ref)
    spread_step(1, WINDOW, UNROLL, high_ref, low_ref, cell_ref, edge_ref, out_ref)


def second_records(lists):
    return pl.pallas_call(
        second_records_kernel,
        out_shape=jax.ShapeDtypeStruct((PLANES // 2, CA, CB), jnp.float32),
        in_specs=[WHOLE] * 3 + [pl.BlockSpec(memory_space=pltpu.SMEM)],
        out_specs=WHOLE,
        compiler_params=PARAMS,
        name="second_records",
    )(*lists)


def local(adjoint_start, mixing_h, mixing_v, courant, coriolis, misfit, owner, column):
    devices = lax.axis_size("tx") * lax.axis_size("ty")
    state = adjoint_start.reshape(PLANES, CA, CB)
    coefficients = (mixing_h, mixing_v, courant, coriolis)
    sent = pack(owner.transpose(0, 2, 1), column, misfit, devices, 1024)
    got = lax.all_to_all(sent.reshape(devices, 1, WORDS * 128), ("tx", "ty"), split_axis=0, concat_axis=0, tiled=True)
    still = step(state, state, trade(first_edges(state, sent)), coefficients)
    ts, lists, edges = first_records(got.reshape(devices * WORDS, 128), still)
    halos = trade(edges)
    forcing = second_records(lists)
    return step(ts, still, halos, coefficients, forcing).reshape(FIELDS, LEV, CA, CB)


def solution(mesh):
    return jax.shard_map(
        local,
        mesh=mesh,
        in_specs=(
            P(None, None, "tx", "ty"),
            P(None, "tx", "ty"),
            P(None, "tx", "ty"),
            P(None, None, "tx", "ty"),
            P("tx", "ty"),
            P(None, None, ("tx", "ty")),
            P(None, ("tx", "ty"), None),
            P(None, ("tx", "ty")),
        ),
        out_specs=P(None, None, "tx", "ty"),
        check_vma=False,
    )
```

time: 235 us -> 75.8 us (0.32)
  the two profiles are of different devices: /device:TPU:9 before, /device:TPU:17 now
where the time goes in v1:
time: 75.8 us; the launch traced here: 75.4 us
  starting transfers between devices  38.6 us (51%)
  Pallas kernels  33.1 us (44%)
  local copies, waits for them, and re-layouts  2.65 us (3%)
  waiting for transfers between devices  0.78 us (1%)
    ppermute x8, starting transfers between devices, moved(): return lax.ppermute(x, axis, pairs)  27.5 us
    all_to_all x1, starting transfers between devices, local(): lax.all_to_all(sent.reshape(devices, 1, WORDS * 128), ('tx', 'ty'), split...  11.1 us
    pallas_call x2, Pallas kernels, step(): pl.pallas_call(functools.partial(step_kernel, forcing is not None), out_s...  11 us
    pallas_call x1, Pallas kernels, first_records(): pl.pallas_call(first_records_kernel, out_shape=(jax.ShapeDtypeStruct((PLA...  9.81 us
    pallas_call x1, Pallas kernels, pack(): pl.pallas_call(functools.partial(pack_kernel, devices, span), out_shape=j...  5.98 us
    pallas_call x1, Pallas kernels, second_records(): pl.pallas_call(second_records_kernel, out_shape=jax.ShapeDtypeStruct((PLA...  5.65 us
    unnamed x22, local copies, waits for them, and re-layouts  2.65 us
  transfers between devices with their start and end apart: 9, of which 1 were waited for; matrix products, arithmetic and copies ran while one was open for 0% of the time, Pallas kernels for 15%

profile of v1, /device:TPU:17, one launch (start us, length us, event | category | flops | bytes accessed | tf_op | source)
XLA Modules:
  0.0 75.4 jit_solution(8710682882758165629)
XLA Ops:
  0.0 1.1 %copy-done.8 = f32[2,8,4096]{2,1,0:T(8,128)S(1)} copy-done((f32[2,8,4096]{2,1,0:T(8,128)S(1)}, f32[2,8,4096]{2,1,0:T(8,128)}, u32[]{:S(2)}) %copy-start.8) | copy-done | bytes 262168
  1.1 0.8 %copy-done.9 = s32[2,4096,1]{1,2,0:T(1,128)S(1)} copy-done((s32[2,4096,1]{1,2,0:T(1,128)S(1)}, s32[2,4096,1]{1,2,0:T(1,128)}, u32[]{:S(2)}) %copy-start.9) | copy-done | bytes 32792
  1.9 0.8 %copy-done.10 = s32[2,4096]{1,0:T(2,128)S(1)} copy-done((s32[2,4096]{1,0:T(2,128)S(1)}, s32[2,4096]{1,0:T(2,128)}, u32[]{:S(2)}) %copy-start.10) | copy-done | bytes 32792
  2.6 6.0 %pack.1.after_ref = f32[1152,128]{1,0:T(8,128)} custom-call(s32[2,1,4096]{2,1,0:T(1,128)S(1)} %bitcast.8, s32[2,4096]{1,0:T(2,128)S(1)} %copy-done.10, f32[2,8,4096]{2,1,0:T(8,128)S(1)} %copy-done.8), custom_call_target="tpu_custom_call" | custom-call | tf_op jit(solution)/shard_map/pack/pallas_call | solution.py:73
  8.6 11.1 %all-to-all-start = ((f32[128,1,1152]{2,1,0:T(1,128)}), f32[128,1,1152]{2,1,0:T(1,128)}, u32[]{:S(2)}, u32[]{:S(2)}) async-start(f32[128,1,1152]{2,1,0:T(1,128)} %bitcast.1), calls=%async_computation | async-start | bytes 1179648 | tf_op jit(solution)/shard_map/all_to_all | solution.py:393
  19.7 0.0 copy-start.3
  19.7 0.0 copy-start.6
  19.7 0.0 copy-done
  19.7 0.7 first_edges.1
  20.4 3.6 %collective-permute-start = (f32[16,256]{1,0:T(8,128)S(1)}, f32[16,256]{1,0:T(8,128)S(1)}, u32[]{:S(2)}, u32[]{:S(2)}) collective-permute-start(f32[16,256]{1,0:T(8,128)S(1)} %get-tuple-element.18), channel_id=1, source_target_pairs={{0,16},{16,32},{32,48},{48,64},{64,80},{80,96},{96,112},{1,17},{17... | collective-permute-start | bytes 49160 | tf_op jit(solution)/shard_map/ppermute | solution.py:265
  24.0 1.9 %collective-permute-start.1 = (f32[16,256]{1,0:T(8,128)S(1)}, f32[16,256]{1,0:T(8,128)S(1)}, u32[]{:S(2)}, u32[]{:S(2)}) collective-permute-start(f32[16,256]{1,0:T(8,128)S(1)} %get-tuple-element.19), channel_id=1, source_target_pairs={{16,0},{32,16},{48,32},{64,48},{80,64},{96,80},{112,96},{17,1},{33... | collective-permute-start | bytes 49160 | tf_op jit(solution)/shard_map/ppermute | solution.py:265
  25.9 3.1 %collective-permute-start.2 = (f32[16,128]{1,0:T(8,128)S(1)}, f32[16,128]{1,0:T(8,128)S(1)}, u32[]{:S(2)}, u32[]{:S(2)}) collective-permute-start(f32[16,128]{1,0:T(8,128)S(1)} %get-tuple-element.20), channel_id=1, source_target_pairs={{0,1},{1,2},{2,3},{3,4},{4,5},{5,6},{6,7},{7,8},{8,9},{9,10},{10,1... | collective-permute-start | bytes 24584 | tf_op jit(solution)/shard_map/ppermute | solution.py:265
  29.0 4.3 %collective-permute-start.3 = (f32[16,128]{1,0:T(8,128)S(1)}, f32[16,128]{1,0:T(8,128)S(1)}, u32[]{:S(2)}, u32[]{:S(2)}) collective-permute-start(f32[16,128]{1,0:T(8,128)S(1)} %get-tuple-element.21), channel_id=1, source_target_pairs={{1,0},{2,1},{3,2},{4,3},{5,4},{6,5},{7,6},{8,7},{9,8},{10,9},{11,1... | collective-permute-start | bytes 24584 | tf_op jit(solution)/shard_map/ppermute | solution.py:265
  33.3 0.0 collective-permute-done.2.prior_ref
  33.3 0.8 %collective-permute-done.3.next_ref = f32[16,128]{1,0:T(8,128)S(1)} collective-permute-done((f32[16,128]{1,0:T(8,128)S(1)}, f32[16,128]{1,0:T(8,128)S(1)}, u32[]{:S(2)}, u32[]{:S(2)}) %collective-permute-start.3) | collective-permute-done | bytes 8224 | tf_op jit(solution)/shard_map/ppermute | solution.py:265
  34.1 0.0 collective-permute-done.before_ref
  34.1 0.0 collective-permute-done.1.after_ref
  34.1 5.0 %advance.2.still_ref.uv_ref = f32[16,128,256]{2,1,0:T(8,128)S(1)} custom-call(f32[16,128,256]{2,1,0:T(8,128)} %bitcast.5, f32[16,128,256]{2,1,0:T(8,128)} %bitcast.6, f32[16,256]{1,0:T(8,128)S(1)} %collective-permute-done.before_ref, f32[16,256]{1,0:T(8,128)S(1)} %collective-permute-done.1.after_ref, f32[16,128]{1,0:T(8,128)S(1)} %collective-permute-done.2.prior_ref, ...), custom_call_target="tpu_custom_call" | custom-call | tf_op jit(solution)/shard_map/advance/pallas_call | solution.py:327
  39.1 0.0 all-to-all-done
  39.1 0.0 copy-start.4
  39.1 0.0 copy-start.7
  39.1 9.8 %first_records.1 = (f32[8,128,256]{2,1,0:T(8,128)S(1)}, f32[2,8,32,256]{3,2,1,0:T(8,128)S(1)}, f32[2,8,32,256]{3,2,1,0:T(8,128)S(1)}, f32[2,1,32,256]{3,2,1,0:T(...) custom-call(f32[1152,128]{1,0:T(8,128)} %bitcast.2.got_ref, ...), custom_call_target="tpu_custom_call" | custom-call | tf_op jit(solution)/shard_map/first_records/pallas_call | solution.py:360
  49.0 4.8 %collective-permute-start.4 = (f32[16,256]{1,0:T(8,128)S(1)}, f32[16,256]{1,0:T(8,128)S(1)}, u32[]{:S(2)}, u32[]{:S(2)}) collective-permute-start(f32[16,256]{1,0:T(8,128)S(1)} %get-tuple-element.23), channel_id=1, source_target_pairs={{0,16},{16,32},{32,48},{48,64},{64,80},{80,96},{96,112},{1,17},{17... | collective-permute-start | bytes 49160 | tf_op jit(solution)/shard_map/ppermute | solution.py:265
  53.8 1.9 %collective-permute-start.5 = (f32[16,256]{1,0:T(8,128)S(1)}, f32[16,256]{1,0:T(8,128)S(1)}, u32[]{:S(2)}, u32[]{:S(2)}) collective-permute-start(f32[16,256]{1,0:T(8,128)S(1)} %get-tuple-element.24), channel_id=1, source_target_pairs={{16,0},{32,16},{48,32},{64,48},{80,64},{96,80},{112,96},{17,1},{33... | collective-permute-start | bytes 49160 | tf_op jit(solution)/shard_map/ppermute | solution.py:265
  55.7 2.7 %collective-permute-start.6 = (f32[16,128]{1,0:T(8,128)S(1)}, f32[16,128]{1,0:T(8,128)S(1)}, u32[]{:S(2)}, u32[]{:S(2)}) collective-permute-start(f32[16,128]{1,0:T(8,128)S(1)} %get-tuple-element.25), channel_id=1, source_target_pairs={{0,1},{1,2},{2,3},{3,4},{4,5},{5,6},{6,7},{7,8},{8,9},{9,10},{10,1... | collective-permute-start | bytes 24584 | tf_op jit(solution)/shard_map/ppermute | solution.py:265
  58.4 5.2 %collective-permute-start.7 = (f32[16,128]{1,0:T(8,128)S(1)}, f32[16,128]{1,0:T(8,128)S(1)}, u32[]{:S(2)}, u32[]{:S(2)}) collective-permute-start(f32[16,128]{1,0:T(8,128)S(1)} %get-tuple-element.26), channel_id=1, source_target_pairs={{1,0},{2,1},{3,2},{4,3},{5,4},{6,5},{7,6},{8,7},{9,8},{10,9},{11,1... | collective-permute-start | bytes 24584 | tf_op jit(solution)/shard_map/ppermute | solution.py:265
  63.6 5.6 %second_records.1.rest_0_ = f32[8,128,256]{2,1,0:T(8,128)S(1)} custom-call(f32[2,8,32,256]{3,2,1,0:T(8,128)S(1)} %get-tuple-element.27.high_ref, f32[2,8,32,256]{3,2,1,0:T(8,128)S(1)} %get-tuple-element.28.low_ref, f32[2,1,32,256]{3,2,1,0:T(8,128)S(1)} %get-tuple-element.29.cell_ref, s32[8,128]{1,0:T(8,128)S(1)} %get-tuple-element.30.edge_ref), custom_call_target="tpu_custom_call" | custom-call | tf_op jit(solution)/shard_map/second_records/pallas_call | solution.py:378
  69.3 0.0 collective-permute-done.6.prior_ref
  69.3 0.0 collective-permute-done.7.next_ref
  69.3 0.0 collective-permute-done.4.before_ref
  69.3 0.0 collective-permute-done.5.after_ref
  69.4 6.0 %advance.3 = f32[16,128,256]{2,1,0:T(8,128)} custom-call(f32[8,128,256]{2,1,0:T(8,128)S(1)} %get-tuple-element.22.ts_ref, f32[16,128,256]{2,1,0:T(8,128)} %copy-done.1, f32[16,256]{1,0:T(8,128)S(1)} %collective-permute-done.4.before_ref, f32[16,256]{1,0:T(8,128)S(1)} %collective-permute-done.5.after_ref, f32[16,128]{1,0:T(8,128)S(1)} %collective-permute-done.6.prior_ref, ...), custom_call_target="tpu_custom_call" | custom-call | tf_op jit(solution)/shard_map/advance/pallas_call | solution.py:327
  (14 shorter events, 0.0 us)
Async XLA Ops:
  0.0 19.7 %copy-start = (f32[4,4,128,256]{3,2,1,0:T(8,128)S(1)}, f32[4,4,128,256]{3,2,1,0:T(8,128)}, u32[]{:S(2)}) copy-start(f32[4,4,128,256]{3,2,1,0:T(8,128)} %param.8) | copy-start | bytes 6291460
  0.0 1.1 %copy-start.8 = (f32[2,8,4096]{2,1,0:T(8,128)S(1)}, f32[2,8,4096]{2,1,0:T(8,128)}, u32[]{:S(2)}) copy-start(f32[2,8,4096]{2,1,0:T(8,128)} %misfit_ref.1) | copy-start | bytes 786436
  1.1 0.8 %copy-start.9 = (s32[2,4096,1]{1,2,0:T(1,128)S(1)}, s32[2,4096,1]{1,2,0:T(1,128)}, u32[]{:S(2)}) copy-start(s32[2,4096,1]{1,2,0:T(1,128)} %param.14) | copy-start | bytes 98308
  1.9 0.8 %copy-start.10 = (s32[2,4096]{1,0:T(2,128)S(1)}, s32[2,4096]{1,0:T(2,128)}, u32[]{:S(2)}) copy-start(s32[2,4096]{1,0:T(2,128)} %column_ref.1) | copy-start | bytes 98308
  8.6 25.5 %copy-start.2 = (f32[2,4,128,256]{3,2,1,0:T(8,128)S(1)}, f32[2,4,128,256]{3,2,1,0:T(8,128)}, u32[]{:S(2)}) copy-start(f32[2,4,128,256]{3,2,1,0:T(8,128)} %courant_ref.3) | copy-start | bytes 3145732
  8.6 25.5 %copy-start.5 = (f32[3,128,256]{2,1,0:T(8,128)S(1)}, f32[3,128,256]{2,1,0:T(8,128)}, u32[]{:S(2)}) copy-start(f32[3,128,256]{2,1,0:T(8,128)} %mix_v_ref.3) | copy-start | bytes 1179652
  8.6 30.5 %all-to-all-start = ((f32[128,1,1152]{2,1,0:T(1,128)}), f32[128,1,1152]{2,1,0:T(1,128)}, u32[]{:S(2)}, u32[]{:S(2)}) async-start(f32[128,1,1152]{2,1,0:T(1,128)} %bitcast.1), calls=%async_computation | async-start | bytes 1179648 | tf_op jit(solution)/shard_map/all_to_all | solution.py:393
  19.7 14.5 %copy-start.3 = (f32[4,128,256]{2,1,0:T(8,128)S(1)}, f32[4,128,256]{2,1,0:T(8,128)}, u32[]{:S(2)}) copy-start(f32[4,128,256]{2,1,0:T(8,128)} %mix_h_ref.3) | copy-start | bytes 1572868
  19.7 14.5 %copy-start.6 = (f32[128,256]{1,0:T(8,128)S(1)}, f32[128,256]{1,0:T(8,128)}, u32[]{:S(2)}) copy-start(f32[128,256]{1,0:T(8,128)} %turn_ref.3) | copy-start | bytes 393220
  20.4 13.7 %collective-permute-start = (f32[16,256]{1,0:T(8,128)S(1)}, f32[16,256]{1,0:T(8,128)S(1)}, u32[]{:S(2)}, u32[]{:S(2)}) collective-permute-start(f32[16,256]{1,0:T(8,128)S(1)} %get-tuple-element.18), channel_id=1, source_target_pairs={{0,16},{16,32},{32,48},{48,64},{64,80},{80,96},{96,112},{1,17},{17... | collective-permute-start | bytes 49160 | tf_op jit(solution)/shard_map/ppermute | solution.py:265
  24.0 10.1 %collective-permute-start.1 = (f32[16,256]{1,0:T(8,128)S(1)}, f32[16,256]{1,0:T(8,128)S(1)}, u32[]{:S(2)}, u32[]{:S(2)}) collective-permute-start(f32[16,256]{1,0:T(8,128)S(1)} %get-tuple-element.19), channel_id=1, source_target_pairs={{16,0},{32,16},{48,32},{64,48},{80,64},{96,80},{112,96},{17,1},{33... | collective-permute-start | bytes 49160 | tf_op jit(solution)/shard_map/ppermute | solution.py:265
  25.9 7.4 %collective-permute-start.2 = (f32[16,128]{1,0:T(8,128)S(1)}, f32[16,128]{1,0:T(8,128)S(1)}, u32[]{:S(2)}, u32[]{:S(2)}) collective-permute-start(f32[16,128]{1,0:T(8,128)S(1)} %get-tuple-element.20), channel_id=1, source_target_pairs={{0,1},{1,2},{2,3},{3,4},{4,5},{5,6},{6,7},{7,8},{8,9},{9,10},{10,1... | collective-permute-start | bytes 24584 | tf_op jit(solution)/shard_map/ppermute | solution.py:265
  29.0 5.1 %collective-permute-start.3 = (f32[16,128]{1,0:T(8,128)S(1)}, f32[16,128]{1,0:T(8,128)S(1)}, u32[]{:S(2)}, u32[]{:S(2)}) collective-permute-start(f32[16,128]{1,0:T(8,128)S(1)} %get-tuple-element.21), channel_id=1, source_target_pairs={{1,0},{2,1},{3,2},{4,3},{5,4},{6,5},{7,6},{8,7},{9,8},{10,9},{11,1... | collective-permute-start | bytes 24584 | tf_op jit(solution)/shard_map/ppermute | solution.py:265
  39.1 30.2 %copy-start.1 = (f32[16,128,256]{2,1,0:T(8,128)}, f32[16,128,256]{2,1,0:T(8,128)S(1)}, u32[]{:S(2)}) copy-start(f32[16,128,256]{2,1,0:T(8,128)S(1)} %advance.2.still_ref.uv_ref) | copy-start | bytes 6291460
  39.1 30.2 %copy-start.4 = (f32[4,128,256]{2,1,0:T(8,128)S(1)}, f32[4,128,256]{2,1,0:T(8,128)}, u32[]{:S(2)}) copy-start(f32[4,128,256]{2,1,0:T(8,128)} %mix_h_ref.3) | copy-start | bytes 1572868
  39.1 30.2 %copy-start.7 = (f32[128,256]{1,0:T(8,128)S(1)}, f32[128,256]{1,0:T(8,128)}, u32[]{:S(2)}) copy-start(f32[128,256]{1,0:T(8,128)} %turn_ref.3) | copy-start | bytes 393220
  49.0 20.4 %collective-permute-start.4 = (f32[16,256]{1,0:T(8,128)S(1)}, f32[16,256]{1,0:T(8,128)S(1)}, u32[]{:S(2)}, u32[]{:S(2)}) collective-permute-start(f32[16,256]{1,0:T(8,128)S(1)} %get-tuple-element.23), channel_id=1, source_target_pairs={{0,16},{16,32},{32,48},{48,64},{64,80},{80,96},{96,112},{1,17},{17... | collective-permute-start | bytes 49160 | tf_op jit(solution)/shard_map/ppermute | solution.py:265
  53.8 15.6 %collective-permute-start.5 = (f32[16,256]{1,0:T(8,128)S(1)}, f32[16,256]{1,0:T(8,128)S(1)}, u32[]{:S(2)}, u32[]{:S(2)}) collective-permute-start(f32[16,256]{1,0:T(8,128)S(1)} %get-tuple-element.24), channel_id=1, source_target_pairs={{16,0},{32,16},{48,32},{64,48},{80,64},{96,80},{112,96},{17,1},{33... | collective-permute-start | bytes 49160 | tf_op jit(solution)/shard_map/ppermute | solution.py:265
  55.7 13.6 %collective-permute-start.6 = (f32[16,128]{1,0:T(8,128)S(1)}, f32[16,128]{1,0:T(8,128)S(1)}, u32[]{:S(2)}, u32[]{:S(2)}) collective-permute-start(f32[16,128]{1,0:T(8,128)S(1)} %get-tuple-element.25), channel_id=1, source_target_pairs={{0,1},{1,2},{2,3},{3,4},{4,5},{5,6},{6,7},{7,8},{8,9},{9,10},{10,1... | collective-permute-start | bytes 24584 | tf_op jit(solution)/shard_map/ppermute | solution.py:265
  58.4 10.9 %collective-permute-start.7 = (f32[16,128]{1,0:T(8,128)S(1)}, f32[16,128]{1,0:T(8,128)S(1)}, u32[]{:S(2)}, u32[]{:S(2)}) collective-permute-start(f32[16,128]{1,0:T(8,128)S(1)} %get-tuple-element.26), channel_id=1, source_target_pairs={{1,0},{2,1},{3,2},{4,3},{5,4},{6,5},{7,6},{8,7},{9,8},{10,9},{11,1... | collective-permute-start | bytes 24584 | tf_op jit(solution)/shard_map/ppermute | solution.py:265

commit v2 on v1

--- a/solution.py
+++ b/solution.py
@@ -12,6 +12,9 @@
 CHUNK = 256
 BF = jnp.bfloat16
 NT = (((1,), (1,)), ((), ()))
+WHOLE = pl.BlockSpec(memory_space=pltpu.VMEM)
+ANYWHERE = pl.BlockSpec(memory_space=pl.ANY)
+PARAMS = pltpu.CompilerParams(vmem_limit_bytes=48 << 20)
 
 
 def halves(x):
@@ -19,16 +22,13 @@
     return top, (x - top.astype(jnp.float32)).astype(BF)
 
 
-def pack_kernel(devices, span, owner_ref, column_ref, misfit_ref, out_ref, acc_ref, place_ref):
-    records = owner_ref.shape[2]
-    groups = devices // 4
+def slots_kernel(devices, owner_ref, place_ref):
     r = lax.broadcasted_iota(jnp.int32, (CHUNK, CHUNK), 0)
     c = lax.broadcasted_iota(jnp.int32, (CHUNK, CHUNK), 1)
     earlier = (r < c).astype(jnp.float32).astype(BF)
     tiles = lax.broadcasted_iota(jnp.int32, (devices, CHUNK), 0)
-
     counts = [jnp.zeros((devices, 1), jnp.float32)] * STEPS
-    for i in range(records // CHUNK):
+    for i in range(owner_ref.shape[2] // CHUNK):
         at = pl.ds(i * CHUNK, CHUNK)
         for t in range(STEPS):
             target = owner_ref[t, :, at]
@@ -39,46 +39,78 @@
             counts[t] = counts[t] + before[:, CHUNK - 1 :] + ones[:, CHUNK - 1 :]
             place_ref[t, :, at] = (target & 3) * CAP + slot.astype(jnp.int32)
 
-    acc_ref[...] = jnp.zeros_like(acc_ref)
+
+def slots(owner, devices):
+    return pl.pallas_call(
+        functools.partial(slots_kernel, devices),
+        out_shape=jax.ShapeDtypeStruct(owner.shape, jnp.int32),
+        in_specs=[WHOLE],
+        out_specs=WHOLE,
+        compiler_params=PARAMS,
+        name="slots",
+    )(owner)
+
+
+def gather_step(t, span, owner_ref, place_ref, column_ref, misfit_ref, acc_ref):
+    groups = acc_ref.shape[0] // WORDS
     group_row = lax.broadcasted_iota(jnp.int32, (groups, span), 0)
     place_row = lax.broadcasted_iota(jnp.int32, (CHUNK, span), 0)
 
+    def part(i):
+        at = pl.ds(pl.multiple_of(i * span, span), span)
+        group_hot = (group_row == (owner_ref[t, :, at] >> 2)).astype(jnp.float32).astype(BF)
+        place_hot = (place_row == place_ref[t, :, at]).astype(jnp.float32).astype(BF)
+        cell = column_ref[t : t + 1, at]
+        high, low = halves(misfit_ref[t, :, at])
+        row = (cell - (cell & (CB - 1))).astype(jnp.float32).astype(BF)
+        col = ((cell & (CB - 1)) + 1).astype(jnp.float32).astype(BF)
+        lhs_h = jnp.concatenate([group_hot * high[k : k + 1] for k in range(VALS)] + [group_hot * row], axis=0)
+        lhs_l = jnp.concatenate([group_hot * low[k : k + 1] for k in range(VALS)] + [group_hot * col], axis=0)
+        lhs = jnp.concatenate([lhs_h, lhs_l], axis=1)
+        rhs = jnp.concatenate([place_hot, place_hot], axis=1)
+        return lax.dot_general(lhs, rhs, NT, preferred_element_type=jnp.float32)
+
+    acc_ref[...] = part(0)
+
     def body(i, carry):
-        at = pl.ds(pl.multiple_of(i * span, span), span)
-        for t in range(STEPS):
-            group_hot = (group_row == (owner_ref[t, :, at] >> 2)).astype(jnp.float32).astype(BF)
-            place_hot = (place_row == place_ref[t, :, at]).astype(jnp.float32).astype(BF)
-            cell = column_ref[t : t + 1, at]
-            high, low = halves(misfit_ref[t, :, at])
-            row = (cell - (cell & (CB - 1))).astype(jnp.float32).astype(BF)
-            col = ((cell & (CB - 1)) + 1).astype(jnp.float32).astype(BF)
-            lhs_h = jnp.concatenate([group_hot * high[k : k + 1] for k in range(VALS)] + [group_hot * row], axis=0)
-            lhs_l = jnp.concatenate([group_hot * low[k : k + 1] for k in range(VALS)] + [group_hot * col], axis=0)
-            lhs = jnp.concatenate([lhs_h, lhs_l], axis=1)
-            rhs = jnp.concatenate([place_hot, place_hot], axis=1)
-            acc_ref[t] += lax.dot_general(lhs, rhs, NT, preferred_element_type=jnp.float32)
+        acc_ref[...] += part(i)
         return carry
 
-    lax.fori_loop(0, records // span, body, 0)
+    lax.fori_loop(1, owner_ref.shape[2] // span, body, 0)
+
+
+def gather_first_kernel(span, owner_ref, place_ref, column_ref, misfit_ref, out_ref):
+    gather_step(0, span, owner_ref, place_ref, column_ref, misfit_ref, out_ref)
+
+
+def gather_second_kernel(span, owner_ref, place_ref, column_ref, misfit_ref, first_ref, out_ref, acc_ref):
+    gather_step(1, span, owner_ref, place_ref, column_ref, misfit_ref, acc_ref)
+    groups = acc_ref.shape[0] // WORDS
     left = lax.broadcasted_iota(jnp.int32, (groups, 128), 1) < CAP
     for k in range(WORDS):
         for j in range(2):
-            a = acc_ref[0, pl.ds(k * groups, groups), pl.ds(j * 128, 128)]
-            b = acc_ref[1, pl.ds(k * groups, groups), pl.ds(j * 128, 128)]
+            a = first_ref[pl.ds(k * groups, groups), pl.ds(j * 128, 128)]
+            b = acc_ref[pl.ds(k * groups, groups), pl.ds(j * 128, 128)]
             out_ref[pl.ds(2 * j * WORDS + k, groups, stride=4 * WORDS), :] = jnp.where(left, a, pltpu.roll(b, CAP, 1))
             out_ref[pl.ds((2 * j + 1) * WORDS + k, groups, stride=4 * WORDS), :] = jnp.where(left, pltpu.roll(a, CAP, 1), b)
 
 
-def pack(owner, column, misfit, devices, span=512):
+def gather(records, devices, first=None, span=1024):
+    rows = WORDS * devices // 4
+    if first is None:
+        kernel, shape, extra, scratch, name = gather_first_kernel, (rows, CHUNK), (), [], "gather_first"
+    else:
+        kernel, shape, extra, name = gather_second_kernel, (devices * WORDS, 128), (first,), "gather_second"
+        scratch = [pltpu.VMEM((rows, CHUNK), jnp.float32)]
     return pl.pallas_call(
-        functools.partial(pack_kernel, devices, span),
-        out_shape=jax.ShapeDtypeStruct((devices * WORDS, 128), jnp.float32),
-        in_specs=[pl.BlockSpec(memory_space=pltpu.VMEM)] * 3,
-        out_specs=pl.BlockSpec(memory_space=pltpu.VMEM),
-        scratch_shapes=[pltpu.VMEM((STEPS, WORDS * devices // 4, CHUNK), jnp.float32), pltpu.VMEM((STEPS, 1, 4096), jnp.int32)],
-        compiler_params=pltpu.CompilerParams(vmem_limit_bytes=48 << 20),
-        name="pack",
-    )(owner, column, misfit)
+        functools.partial(kernel, span),
+        out_shape=jax.ShapeDtypeStruct(shape, jnp.float32),
+        in_specs=[WHOLE] * (4 + len(extra)),
+        out_specs=WHOLE,
+        scratch_shapes=scratch,
+        compiler_params=PARAMS,
+        name=name,
+    )(*records, *extra)
 
 
 def exchange(keys, span, reach):
@@ -183,7 +215,7 @@
     return out[: VALS * window] + out[VALS * window :]
 
 
-def spread_step(t, window, unroll, high_ref, low_ref, cell_ref, edge_ref, acc_ref):
+def spread_step(t, chunks_from, chunks_to, window, unroll, high_ref, low_ref, cell_ref, edge_ref, acc_ref):
     def gain(base, out):
         for k in range(VALS):
             acc_ref[k, pl.ds(base, window), :] += out[k * window : (k + 1) * window]
@@ -199,7 +231,7 @@
             gain(base, out)
         return carry
 
-    lax.fori_loop(0, 32 // unroll, body, 0)
+    lax.fori_loop(chunks_from // unroll, chunks_to // unroll, body, 0)
 
     def rest(i, carry):
         def more(start):
@@ -210,7 +242,7 @@
         lax.while_loop(lambda start: start <= edge_ref[2 * t + 1, i], more, first(i) + window)
         return carry
 
-    lax.fori_loop(0, 32, rest, 0)
+    lax.fori_loop(chunks_from, chunks_to, rest, 0)
 
 
 FIELDS = 4
@@ -236,35 +268,31 @@
     jax.ShapeDtypeStruct((PLANES, CA), jnp.float32),
     jax.ShapeDtypeStruct((PLANES, CA), jnp.float32),
 )
-WHOLE = pl.BlockSpec(memory_space=pltpu.VMEM)
-ANYWHERE = pl.BlockSpec(memory_space=pl.ANY)
-PARAMS = pltpu.CompilerParams(vmem_limit_bytes=48 << 20)
-
-
-def first_edges_kernel(state_ref, after_ref, *edge_refs):
+
+
+def first_edges_kernel(state_ref, *edge_refs):
     edge_lines(lambda p, rows, cols: state_ref[p, rows, cols], *edge_refs)
 
 
-def first_edges(state, after):
+def first_edges(state):
     return pl.pallas_call(
         first_edges_kernel,
         out_shape=EDGES,
-        in_specs=[WHOLE, ANYWHERE],
+        in_specs=[WHOLE],
         out_specs=[WHOLE] * 4,
         compiler_params=PARAMS,
         name="first_edges",
-    )(state, after)
-
-
-def trade(edges):
-    top, bottom, left, right = edges
-
-    def moved(x, axis, forward):
-        ends = lax.axis_size(axis) - 1
-        pairs = [(i, i + 1) if forward else (i + 1, i) for i in range(ends)]
-        return lax.ppermute(x, axis, pairs)
-
-    return moved(bottom, "tx", True), moved(top, "tx", False), moved(right, "ty", True), moved(left, "ty", False)
+    )(state)
+
+
+def moved(x, axis, forward):
+    count = lax.axis_size(axis)
+    pairs = [(i, (i + 1) % count) if forward else ((i + 1) % count, i) for i in range(count)]
+    return lax.ppermute(x, axis, pairs)
+
+
+def after(x, *others):
+    return lax.optimization_barrier((x, *others))
 
 
 def step_kernel(forced, ts_ref, uv_ref, before_ref, after_ref, prior_ref, next_ref, mix_h_ref, mix_v_ref, courant_ref, turn_ref, *rest):
@@ -276,10 +304,18 @@
     ]
     for load in loads:
         load.start()
+    tx, ty = lax.axis_index("tx"), lax.axis_index("ty")
+
+    def inside(ref, there):
+        return jnp.where(there, ref[...], 0.0)
+
+    before = inside(before_ref, tx > 0)
+    after = inside(after_ref, tx < lax.axis_size("tx") - 1)
     for p in range(PLANES):
-        state_ref[p, 0:8, :] = jnp.broadcast_to(before_ref[p : p + 1, :], (8, CB))
-        state_ref[p, CA + 8 : CA + 16, :] = jnp.broadcast_to(after_ref[p : p + 1, :], (8, CB))
-    column_ref[...] = jnp.concatenate([prior_ref[...], next_ref[...], jnp.zeros((128 - 2 * PLANES, CA), jnp.float32)], axis=0).T
+        state_ref[p, 0:8, :] = jnp.broadcast_to(before[p : p + 1, :], (8, CB))
+        state_ref[p, CA + 8 : CA + 16, :] = jnp.broadcast_to(after[p : p + 1, :], (8, CB))
+    sides = [inside(prior_ref, ty > 0), inside(next_ref, ty < lax.axis_size("ty") - 1)]
+    column_ref[...] = jnp.concatenate(sides + [jnp.zeros((128 - 2 * PLANES, CA), jnp.float32)], axis=0).T
     for load in loads:
         load.wait()
     sub = lax.broadcasted_iota(jnp.int32, (8, CB), 0)
@@ -351,7 +387,7 @@
     copy.start()
     ts_ref[...] = still_ref[: PLANES // 2]
     copy.wait()
-    spread_step(0, WINDOW, UNROLL, high_ref, low_ref, cell_ref, smem_ref, ts_ref)
+    spread_step(0, 0, 32, WINDOW, UNROLL, high_ref, low_ref, cell_ref, smem_ref, ts_ref)
     half = PLANES // 2
     edge_lines(lambda p, rows, cols: (ts_ref if p < half else still_ref)[p, rows, cols], top_ref, bottom_ref, left_ref, right_ref)
 
@@ -369,33 +405,51 @@
     return out[0], out[1:5], out[5:]
 
 
-def second_records_kernel(high_ref, low_ref, cell_ref, edge_ref, out_ref):
-    out_ref[...] = jnp.zeros_like(out_ref)
-    spread_step(1, WINDOW, UNROLL, high_ref, low_ref, cell_ref, edge_ref, out_ref)
-
-
-def second_records(lists):
+def second_records_kernel(part, high_ref, low_ref, cell_ref, edge_ref, *rest):
+    out_ref = rest[-1]
+    out_ref[...] = rest[0][...] if part else jnp.zeros_like(out_ref)
+    spread_step(1, 16 * part, 16 * part + 16, WINDOW, UNROLL, high_ref, low_ref, cell_ref, edge_ref, out_ref)
+
+
+def second_records(lists, part, earlier=()):
     return pl.pallas_call(
-        second_records_kernel,
+        functools.partial(second_records_kernel, part),
         out_shape=jax.ShapeDtypeStruct((PLANES // 2, CA, CB), jnp.float32),
-        in_specs=[WHOLE] * 3 + [pl.BlockSpec(memory_space=pltpu.SMEM)],
+        in_specs=[WHOLE] * 3 + [pl.BlockSpec(memory_space=pltpu.SMEM)] + [WHOLE] * len(earlier),
         out_specs=WHOLE,
+        input_output_aliases={4: 0} if earlier else {},
         compiler_params=PARAMS,
         name="second_records",
-    )(*lists)
+    )(*lists, *earlier)
 
 
 def local(adjoint_start, mixing_h, mixing_v, courant, coriolis, misfit, owner, column):
     devices = lax.axis_size("tx") * lax.axis_size("ty")
     state = adjoint_start.reshape(PLANES, CA, CB)
     coefficients = (mixing_h, mixing_v, courant, coriolis)
-    sent = pack(owner.transpose(0, 2, 1), column, misfit, devices, 1024)
+    owner = owner.transpose(0, 2, 1)
+    top, bottom, left, right = first_edges(state)
+    places = slots(owner, devices)
+    right, places = after(right, places)
+    prior = moved(right, "ty", True)
+    records = (owner, places, column, misfit)
+    first = gather(records, devices)
+    left, top, bottom, first = after(left, top, bottom, first)
+    next_ = moved(left, "ty", False)
+    sent = gather(records, devices, first)
+    top, bottom, sent = after(top, bottom, sent)
+    halos = moved(bottom, "tx", True), moved(top, "tx", False), prior, next_
     got = lax.all_to_all(sent.reshape(devices, 1, WORDS * 128), ("tx", "ty"), split_axis=0, concat_axis=0, tiled=True)
-    still = step(state, state, trade(first_edges(state, sent)), coefficients)
-    ts, lists, edges = first_records(got.reshape(devices * WORDS, 128), still)
-    halos = trade(edges)
-    forcing = second_records(lists)
-    return step(ts, still, halos, coefficients, forcing).reshape(FIELDS, LEV, CA, CB)
+    still = step(state, state, halos, coefficients)
+
+    ts, lists, (top, bottom, left, right) = first_records(got.reshape(devices * WORDS, 128), still)
+    before, after_ = moved(bottom, "tx", True), moved(top, "tx", False)
+    prior = moved(right, "ty", True)
+    forcing = second_records(lists, 0)
+    left, forcing = after(left, forcing)
+    next_ = moved(left, "ty", False)
+    forcing = second_records(lists, 1, (forcing,))
+    return step(ts, still, (before, after_, prior, next_), coefficients, forcing).reshape(FIELDS, LEV, CA, CB)
 
 
 def solution(mesh):

time: 75.8 us -> 68.8 us (0.908)
  the two profiles are of different devices: /device:TPU:17 before, /device:TPU:0 now
where the time goes in v2:
time: 68.8 us; the launch traced here: 68.5 us
  Pallas kernels  34 us (49%)
  starting transfers between devices  28.3 us (41%)
  local copies, waits for them, and re-layouts  3.62 us (5%)
  waiting for transfers between devices  2.32 us (3%)
    ppermute x8, starting transfers between devices, moved(): return lax.ppermute(x, axis, pairs)  16.7 us
    all_to_all x1, starting transfers between devices, local(): lax.all_to_all(sent.reshape(devices, 1, WORDS * 128), ('tx', 'ty'), split...  11.6 us
    pallas_call x2, Pallas kernels, step(): pl.pallas_call(functools.partial(step_kernel, forcing is not None), out_s...  11 us
    pallas_call x1, Pallas kernels, first_records(): pl.pallas_call(first_records_kernel, out_shape=(jax.ShapeDtypeStruct((PLA...  9.61 us
    pallas_call x2, Pallas kernels, second_records(): pl.pallas_call(functools.partial(second_records_kernel, part), out_shape=...  6.06 us
    pallas_call x2, Pallas kernels, gather(): pl.pallas_call(functools.partial(kernel, span), out_shape=jax.ShapeDtypeS...  5.15 us
    unnamed x22, local copies, waits for them, and re-layouts  3.62 us
    ppermute x8, waiting for transfers between devices, moved(): return lax.ppermute(x, axis, pairs)  2.32 us
  transfers between devices with their start and end apart: 9, of which 1 were waited for; matrix products, arithmetic and copies ran while one was open for 0% of the time, Pallas kernels for 16%

profile of v2, /device:TPU:0, one launch (start us, length us, event | category | flops | bytes accessed | tf_op | source)
XLA Modules:
  0.0 68.5 jit_solution(1969182552949639925)
XLA Ops:
  0.0 1.6 %copy-done = f32[4,4,128,256]{3,2,1,0:T(8,128)S(1)} copy-done((f32[4,4,128,256]{3,2,1,0:T(8,128)S(1)}, f32[4,4,128,256]{3,2,1,0:T(8,128)}, u32[]{:S(2)}) %copy-start) | copy-done | bytes 2097176
  1.6 0.7 %first_edges.1 = (f32[16,256]{1,0:T(8,128)S(1)}, f32[16,256]{1,0:T(8,128)S(1)}, f32[16,128]{1,0:T(8,128)S(1)}, f32[16,128]{1,0:T(8,128)S(1)}) custom-call(f32[16,128,256]{2,1,0:T(8,128)S(1)} %bitcast.7), custom_call_target="tpu_custom_call" | custom-call | tf_op jit(solution)/shard_map/first_edges/pallas_call | solution.py:278
  2.3 0.1 copy-done.9
  2.4 1.5 %slots.1.place_ref = s32[2,1,4096]{2,1,0:T(1,128)S(1)} custom-call(s32[2,1,4096]{2,1,0:T(1,128)S(1)} %bitcast.8), custom_call_target="tpu_custom_call" | custom-call | tf_op jit(solution)/shard_map/slots/pallas_call | solution.py:44
  3.9 2.1 %gather_first.1.first_ref = f32[288,256]{1,0:T(8,128)S(1)} custom-call(s32[2,1,4096]{2,1,0:T(1,128)S(1)} %bitcast.9, s32[2,1,4096]{2,1,0:T(1,128)S(1)} %slots.1.place_ref, s32[2,4096]{1,0:T(2,128)S(1)} %copy-done.10, f32[2,8,4096]{2,1,0:T(8,128)S(1)} %copy-done.6), custom_call_target="tpu_custom_call" | custom-call | tf_op jit(solution)/shard_map/gather_first/pallas_call | solution.py:105
  5.9 3.1 %gather_second.1 = f32[1152,128]{1,0:T(8,128)} custom-call(s32[2,1,4096]{2,1,0:T(1,128)S(1)} %bitcast.10, s32[2,1,4096]{2,1,0:T(1,128)S(1)} %slots.1.place_ref, s32[2,4096]{1,0:T(2,128)S(1)} %copy-done.10, f32[2,8,4096]{2,1,0:T(8,128)S(1)} %copy-done.6, f32[288,256]{1,0:T(8,128)S(1)} %gather_first.1.first_ref), custom_call_target="tpu_custom_call" | custom-call | tf_op jit(solution)/shard_map/gather_second/pallas_call | solution.py:105
  9.0 11.6 %all-to-all-start = ((f32[128,1,1152]{2,1,0:T(1,128)}), f32[128,1,1152]{2,1,0:T(1,128)}, u32[]{:S(2)}, u32[]{:S(2)}) async-start(f32[128,1,1152]{2,1,0:T(1,128)} %bitcast.2), calls=%async_computation | async-start | bytes 1179648 | tf_op jit(solution)/shard_map/all_to_all | solution.py:442
  20.6 0.0 collective-permute-start
  20.7 2.9 %collective-permute-start.1 = (f32[16,256]{1,0:T(8,128)S(1)}, f32[16,256]{1,0:T(8,128)S(1)}, u32[]{:S(2)}, u32[]{:S(2)}) collective-permute-start(f32[16,256]{1,0:T(8,128)S(1)} %get-tuple-element.39), channel_id=1, source_target_pairs={{16,0},{32,16},{48,32},{64,48},{80,64},{96,80},{112,96},{0,112},{1... | collective-permute-start | bytes 49160 | tf_op jit(solution)/shard_map/ppermute | solution.py:291
  23.6 1.1 %collective-permute-start.2 = (f32[16,128]{1,0:T(8,128)S(1)}, f32[16,128]{1,0:T(8,128)S(1)}, u32[]{:S(2)}, u32[]{:S(2)}) collective-permute-start(f32[16,128]{1,0:T(8,128)S(1)} %get-tuple-element.40), channel_id=1, source_target_pairs={{0,1},{1,2},{2,3},{3,4},{4,5},{5,6},{6,7},{7,8},{8,9},{9,10},{10,1... | collective-permute-start | bytes 24584 | tf_op jit(solution)/shard_map/ppermute | solution.py:291
  24.7 4.3 %collective-permute-start.3 = (f32[16,128]{1,0:T(8,128)S(1)}, f32[16,128]{1,0:T(8,128)S(1)}, u32[]{:S(2)}, u32[]{:S(2)}) collective-permute-start(f32[16,128]{1,0:T(8,128)S(1)} %get-tuple-element.41), channel_id=1, source_target_pairs={{1,0},{2,1},{3,2},{4,3},{5,4},{6,5},{7,6},{8,7},{9,8},{10,9},{11,1... | collective-permute-start | bytes 24584 | tf_op jit(solution)/shard_map/ppermute | solution.py:291
  29.0 2.3 %collective-permute-done.2.prior_ref = f32[16,128]{1,0:T(8,128)S(1)} collective-permute-done((f32[16,128]{1,0:T(8,128)S(1)}, f32[16,128]{1,0:T(8,128)S(1)}, u32[]{:S(2)}, u32[]{:S(2)}) %collective-permute-start.2) | collective-permute-done | bytes 8224 | tf_op jit(solution)/shard_map/ppermute | solution.py:291
  31.3 0.0 collective-permute-done.3.next_ref
  31.3 0.0 collective-permute-done.before_ref
  31.3 0.0 collective-permute-done.1.after_ref
  31.3 0.0 copy-start.3
  31.3 1.0 %copy-done.3 = f32[4,128,256]{2,1,0:T(8,128)S(1)} copy-done((f32[4,128,256]{2,1,0:T(8,128)S(1)}, f32[4,128,256]{2,1,0:T(8,128)}, u32[]{:S(2)}) %copy-start.3) | copy-done | bytes 524312
  32.3 0.9 %copy-done.7 = f32[128,256]{1,0:T(8,128)S(1)} copy-done((f32[128,256]{1,0:T(8,128)S(1)}, f32[128,256]{1,0:T(8,128)}, u32[]{:S(2)}) %copy-start.7) | copy-done | bytes 131096
  33.2 5.0 %advance.2.still_ref.uv_ref = f32[16,128,256]{2,1,0:T(8,128)S(1)} custom-call(f32[16,128,256]{2,1,0:T(8,128)} %bitcast.5, f32[16,128,256]{2,1,0:T(8,128)} %bitcast.6, f32[16,256]{1,0:T(8,128)S(1)} %collective-permute-done.before_ref, f32[16,256]{1,0:T(8,128)S(1)} %collective-permute-done.1.after_ref, f32[16,128]{1,0:T(8,128)S(1)} %collective-permute-done.2.prior_ref, ...), custom_call_target="tpu_custom_call" | custom-call | tf_op jit(solution)/shard_map/advance/pallas_call | solution.py:363
  38.2 0.0 all-to-all-done
  38.2 9.6 %first_records.1 = (f32[8,128,256]{2,1,0:T(8,128)S(1)}, f32[2,8,32,256]{3,2,1,0:T(8,128)S(1)}, f32[2,8,32,256]{3,2,1,0:T(8,128)S(1)}, f32[2,1,32,256]{3,2,1,0:T(...) custom-call(f32[1152,128]{1,0:T(8,128)} %bitcast.3.got_ref, ...), custom_call_target="tpu_custom_call" | custom-call | tf_op jit(solution)/shard_map/first_records/pallas_call | solution.py:396
  47.9 0.0 collective-permute-start.4
  47.9 2.9 %collective-permute-start.5 = (f32[16,256]{1,0:T(8,128)S(1)}, f32[16,256]{1,0:T(8,128)S(1)}, u32[]{:S(2)}, u32[]{:S(2)}) collective-permute-start(f32[16,256]{1,0:T(8,128)S(1)} %get-tuple-element.44), channel_id=1, source_target_pairs={{16,0},{32,16},{48,32},{64,48},{80,64},{96,80},{112,96},{0,112},{1... | collective-permute-start | bytes 49160 | tf_op jit(solution)/shard_map/ppermute | solution.py:291
  50.8 0.0 collective-permute-start.6
  50.8 3.0 %second_records.2.rest_0_ = f32[8,128,256]{2,1,0:T(8,128)S(1)} custom-call(f32[2,8,32,256]{3,2,1,0:T(8,128)S(1)} %get-tuple-element.47.high_ref, f32[2,8,32,256]{3,2,1,0:T(8,128)S(1)} %get-tuple-element.48.low_ref, f32[2,1,32,256]{3,2,1,0:T(8,128)S(1)} %get-tuple-element.49.cell_ref, s32[8,128]{1,0:T(8,128)S(1)} %get-tuple-element.50.edge_ref), custom_call_target="tpu_custom_call" | custom-call | tf_op jit(solution)/shard_map/second_records/pallas_call | solution.py:415
  53.9 0.0 copy-start.4
  53.9 0.0 copy-start.8
  53.9 5.4 %collective-permute-start.7 = (f32[16,128]{1,0:T(8,128)S(1)}, f32[16,128]{1,0:T(8,128)S(1)}, u32[]{:S(2)}, u32[]{:S(2)}) collective-permute-start(f32[16,128]{1,0:T(8,128)S(1)} %get-tuple-element.51), channel_id=1, source_target_pairs={{1,0},{2,1},{3,2},{4,3},{5,4},{6,5},{7,6},{8,7},{9,8},{10,9},{11,1... | collective-permute-start | bytes 24584 | tf_op jit(solution)/shard_map/ppermute | solution.py:291
  59.3 3.0 %second_records.3.rest_0_ = f32[8,128,256]{2,1,0:T(8,128)S(1)} custom-call(f32[2,8,32,256]{3,2,1,0:T(8,128)S(1)} %get-tuple-element.47.high_ref, f32[2,8,32,256]{3,2,1,0:T(8,128)S(1)} %get-tuple-element.48.low_ref, f32[2,1,32,256]{3,2,1,0:T(8,128)S(1)} %get-tuple-element.49.cell_ref, ...), custom_call_target="tpu_custom_call", output_to_operand_aliasing={{}: (4, {})} | custom-call | tf_op jit(solution)/shard_map/second_records/pallas_call | solution.py:415
  62.4 0.0 collective-permute-done.6.prior_ref
  62.4 0.0 collective-permute-done.4.before_ref
  62.4 6.1 %advance.3 = f32[16,128,256]{2,1,0:T(8,128)} custom-call(f32[8,128,256]{2,1,0:T(8,128)S(1)} %get-tuple-element.42.ts_ref, f32[16,128,256]{2,1,0:T(8,128)} %copy-done.1, f32[16,256]{1,0:T(8,128)S(1)} %collective-permute-done.4.before_ref, f32[16,256]{1,0:T(8,128)S(1)} %collective-permute-done.5.after_ref, f32[16,128]{1,0:T(8,128)S(1)} %collective-permute-done.6.prior_ref, ...), custom_call_target="tpu_custom_call" | custom-call | tf_op jit(solution)/shard_map/advance/pallas_call | solution.py:363
  (17 shorter events, 0.0 us)
Async XLA Ops:
  0.0 1.6 %copy-start = (f32[4,4,128,256]{3,2,1,0:T(8,128)S(1)}, f32[4,4,128,256]{3,2,1,0:T(8,128)}, u32[]{:S(2)}) copy-start(f32[4,4,128,256]{3,2,1,0:T(8,128)} %param.8) | copy-start | bytes 6291460
  1.6 0.8 %copy-start.9 = (s32[2,4096,1]{1,2,0:T(1,128)S(1)}, s32[2,4096,1]{1,2,0:T(1,128)}, u32[]{:S(2)}) copy-start(s32[2,4096,1]{1,2,0:T(1,128)} %param.14) | copy-start | bytes 98308
  1.6 2.3 %copy-start.6 = (f32[2,8,4096]{2,1,0:T(8,128)S(1)}, f32[2,8,4096]{2,1,0:T(8,128)}, u32[]{:S(2)}) copy-start(f32[2,8,4096]{2,1,0:T(8,128)} %misfit_ref.3) | copy-start | bytes 786436
  1.6 2.3 %copy-start.10 = (s32[2,4096]{1,0:T(2,128)S(1)}, s32[2,4096]{1,0:T(2,128)}, u32[]{:S(2)}) copy-start(s32[2,4096]{1,0:T(2,128)} %column_ref.3) | copy-start | bytes 98308
  2.3 29.0 %copy-start.2 = (f32[2,4,128,256]{3,2,1,0:T(8,128)S(1)}, f32[2,4,128,256]{3,2,1,0:T(8,128)}, u32[]{:S(2)}) copy-start(f32[2,4,128,256]{3,2,1,0:T(8,128)} %courant_ref.3) | copy-start | bytes 3145732
  2.3 29.0 %copy-start.5 = (f32[3,128,256]{2,1,0:T(8,128)S(1)}, f32[3,128,256]{2,1,0:T(8,128)}, u32[]{:S(2)}) copy-start(f32[3,128,256]{2,1,0:T(8,128)} %mix_v_ref.3) | copy-start | bytes 1179652
  9.0 29.2 %all-to-all-start = ((f32[128,1,1152]{2,1,0:T(1,128)}), f32[128,1,1152]{2,1,0:T(1,128)}, u32[]{:S(2)}, u32[]{:S(2)}) async-start(f32[128,1,1152]{2,1,0:T(1,128)} %bitcast.2), calls=%async_computation | async-start | bytes 1179648 | tf_op jit(solution)/shard_map/all_to_all | solution.py:442
  20.6 10.6 %collective-permute-start = (f32[16,256]{1,0:T(8,128)S(1)}, f32[16,256]{1,0:T(8,128)S(1)}, u32[]{:S(2)}, u32[]{:S(2)}) collective-permute-start(f32[16,256]{1,0:T(8,128)S(1)} %get-tuple-element.38), channel_id=1, source_target_pairs={{0,16},{16,32},{32,48},{48,64},{64,80},{80,96},{96,112},{112,0},{1... | collective-permute-start | bytes 49160 | tf_op jit(solution)/shard_map/ppermute | solution.py:291
  20.7 10.6 %collective-permute-start.1 = (f32[16,256]{1,0:T(8,128)S(1)}, f32[16,256]{1,0:T(8,128)S(1)}, u32[]{:S(2)}, u32[]{:S(2)}) collective-permute-start(f32[16,256]{1,0:T(8,128)S(1)} %get-tuple-element.39), channel_id=1, source_target_pairs={{16,0},{32,16},{48,32},{64,48},{80,64},{96,80},{112,96},{0,112},{1... | collective-permute-start | bytes 49160 | tf_op jit(solution)/shard_map/ppermute | solution.py:291
  23.6 7.7 %collective-permute-start.2 = (f32[16,128]{1,0:T(8,128)S(1)}, f32[16,128]{1,0:T(8,128)S(1)}, u32[]{:S(2)}, u32[]{:S(2)}) collective-permute-start(f32[16,128]{1,0:T(8,128)S(1)} %get-tuple-element.40), channel_id=1, source_target_pairs={{0,1},{1,2},{2,3},{3,4},{4,5},{5,6},{6,7},{7,8},{8,9},{9,10},{10,1... | collective-permute-start | bytes 24584 | tf_op jit(solution)/shard_map/ppermute | solution.py:291
  24.7 6.6 %collective-permute-start.3 = (f32[16,128]{1,0:T(8,128)S(1)}, f32[16,128]{1,0:T(8,128)S(1)}, u32[]{:S(2)}, u32[]{:S(2)}) collective-permute-start(f32[16,128]{1,0:T(8,128)S(1)} %get-tuple-element.41), channel_id=1, source_target_pairs={{1,0},{2,1},{3,2},{4,3},{5,4},{6,5},{7,6},{8,7},{9,8},{10,9},{11,1... | collective-permute-start | bytes 24584 | tf_op jit(solution)/shard_map/ppermute | solution.py:291
  31.3 1.0 %copy-start.3 = (f32[4,128,256]{2,1,0:T(8,128)S(1)}, f32[4,128,256]{2,1,0:T(8,128)}, u32[]{:S(2)}) copy-start(f32[4,128,256]{2,1,0:T(8,128)} %mix_h_ref.3) | copy-start | bytes 1572868
  32.3 0.9 %copy-start.7 = (f32[128,256]{1,0:T(8,128)S(1)}, f32[128,256]{1,0:T(8,128)}, u32[]{:S(2)}) copy-start(f32[128,256]{1,0:T(8,128)} %turn_ref.3) | copy-start | bytes 393220
  38.2 15.7 %copy-start.1 = (f32[16,128,256]{2,1,0:T(8,128)}, f32[16,128,256]{2,1,0:T(8,128)S(1)}, u32[]{:S(2)}) copy-start(f32[16,128,256]{2,1,0:T(8,128)S(1)} %advance.2.still_ref.uv_ref) | copy-start | bytes 6291460
  47.9 14.5 %collective-permute-start.4 = (f32[16,256]{1,0:T(8,128)S(1)}, f32[16,256]{1,0:T(8,128)S(1)}, u32[]{:S(2)}, u32[]{:S(2)}) collective-permute-start(f32[16,256]{1,0:T(8,128)S(1)} %get-tuple-element.43), channel_id=1, source_target_pairs={{0,16},{16,32},{32,48},{48,64},{64,80},{80,96},{96,112},{112,0},{1... | collective-permute-start | bytes 49160 | tf_op jit(solution)/shard_map/ppermute | solution.py:291
  47.9 14.5 %collective-permute-start.5 = (f32[16,256]{1,0:T(8,128)S(1)}, f32[16,256]{1,0:T(8,128)S(1)}, u32[]{:S(2)}, u32[]{:S(2)}) collective-permute-start(f32[16,256]{1,0:T(8,128)S(1)} %get-tuple-element.44), channel_id=1, source_target_pairs={{16,0},{32,16},{48,32},{64,48},{80,64},{96,80},{112,96},{0,112},{1... | collective-permute-start | bytes 49160 | tf_op jit(solution)/shard_map/ppermute | solution.py:291
  50.8 11.5 %collective-permute-start.6 = (f32[16,128]{1,0:T(8,128)S(1)}, f32[16,128]{1,0:T(8,128)S(1)}, u32[]{:S(2)}, u32[]{:S(2)}) collective-permute-start(f32[16,128]{1,0:T(8,128)S(1)} %get-tuple-element.45), channel_id=1, source_target_pairs={{0,1},{1,2},{2,3},{3,4},{4,5},{5,6},{6,7},{7,8},{8,9},{9,10},{10,1... | collective-permute-start | bytes 24584 | tf_op jit(solution)/shard_map/ppermute | solution.py:291
  53.9 8.5 %copy-start.4 = (f32[4,128,256]{2,1,0:T(8,128)S(1)}, f32[4,128,256]{2,1,0:T(8,128)}, u32[]{:S(2)}) copy-start(f32[4,128,256]{2,1,0:T(8,128)} %mix_h_ref.3) | copy-start | bytes 1572868
  53.9 8.5 %copy-start.8 = (f32[128,256]{1,0:T(8,128)S(1)}, f32[128,256]{1,0:T(8,128)}, u32[]{:S(2)}) copy-start(f32[128,256]{1,0:T(8,128)} %turn_ref.3) | copy-start | bytes 393220
  53.9 8.5 %collective-permute-start.7 = (f32[16,128]{1,0:T(8,128)S(1)}, f32[16,128]{1,0:T(8,128)S(1)}, u32[]{:S(2)}, u32[]{:S(2)}) collective-permute-start(f32[16,128]{1,0:T(8,128)S(1)} %get-tuple-element.51), channel_id=1, source_target_pairs={{1,0},{2,1},{3,2},{4,3},{5,4},{6,5},{7,6},{8,7},{9,8},{10,9},{11,1... | collective-permute-start | bytes 24584 | tf_op jit(solution)/shard_map/ppermute | solution.py:291

commit v3 on v2

--- a/solution.py
+++ b/solution.py
@@ -7,14 +7,20 @@
 from jax.sharding import PartitionSpec as P
 
 CA, CB, LEV, STEPS, CAP = 128, 256, 4, 2, 64
+FIELDS = 4
+PLANES = FIELDS * LEV
 VALS = 2 * LEV
 WORDS = VALS + 1
+WIRE = WORDS + 1
 CHUNK = 256
 BF = jnp.bfloat16
 NT = (((1,), (1,)), ((), ()))
+LIMIT = 24
 WHOLE = pl.BlockSpec(memory_space=pltpu.VMEM)
 ANYWHERE = pl.BlockSpec(memory_space=pl.ANY)
-PARAMS = pltpu.CompilerParams(vmem_limit_bytes=48 << 20)
+PARAMS = pltpu.CompilerParams(vmem_limit_bytes=LIMIT << 20)
+STEP = pltpu.CompilerParams(vmem_limit_bytes=40 << 20)
+FULL = pltpu.CompilerParams(vmem_limit_bytes=63400000)
 
 
 def halves(x):
@@ -22,7 +28,7 @@
     return top, (x - top.astype(jnp.float32)).astype(BF)
 
 
-def slots_kernel(devices, owner_ref, place_ref):
+def slots(owner_ref, place_ref, devices):
     r = lax.broadcasted_iota(jnp.int32, (CHUNK, CHUNK), 0)
     c = lax.broadcasted_iota(jnp.int32, (CHUNK, CHUNK), 1)
     earlier = (r < c).astype(jnp.float32).astype(BF)
@@ -40,23 +46,12 @@
             place_ref[t, :, at] = (target & 3) * CAP + slot.astype(jnp.int32)
 
 
-def slots(owner, devices):
-    return pl.pallas_call(
-        functools.partial(slots_kernel, devices),
-        out_shape=jax.ShapeDtypeStruct(owner.shape, jnp.int32),
-        in_specs=[WHOLE],
-        out_specs=WHOLE,
-        compiler_params=PARAMS,
-        name="slots",
-    )(owner)
-
-
-def gather_step(t, span, owner_ref, place_ref, column_ref, misfit_ref, acc_ref):
-    groups = acc_ref.shape[0] // WORDS
+def gather(span, owner_ref, place_ref, column_ref, misfit_ref, acc_ref):
+    groups = acc_ref.shape[1] // WORDS
     group_row = lax.broadcasted_iota(jnp.int32, (groups, span), 0)
     place_row = lax.broadcasted_iota(jnp.int32, (CHUNK, span), 0)
 
-    def part(i):
+    def part(t, i):
         at = pl.ds(pl.multiple_of(i * span, span), span)
         group_hot = (group_row == (owner_ref[t, :, at] >> 2)).astype(jnp.float32).astype(BF)
         place_hot = (place_row == place_ref[t, :, at]).astype(jnp.float32).astype(BF)
@@ -70,47 +65,72 @@
         rhs = jnp.concatenate([place_hot, place_hot], axis=1)
         return lax.dot_general(lhs, rhs, NT, preferred_element_type=jnp.float32)
 
-    acc_ref[...] = part(0)
-
     def body(i, carry):
-        acc_ref[...] += part(i)
+        for t in range(STEPS):
+            acc_ref[t] += part(t, i)
         return carry
 
+    for t in range(STEPS):
+        acc_ref[t] = part(t, 0)
     lax.fori_loop(1, owner_ref.shape[2] // span, body, 0)
 
 
-def gather_first_kernel(span, owner_ref, place_ref, column_ref, misfit_ref, out_ref):
-    gather_step(0, span, owner_ref, place_ref, column_ref, misfit_ref, out_ref)
-
-
-def gather_second_kernel(span, owner_ref, place_ref, column_ref, misfit_ref, first_ref, out_ref, acc_ref):
-    gather_step(1, span, owner_ref, place_ref, column_ref, misfit_ref, acc_ref)
-    groups = acc_ref.shape[0] // WORDS
+def corner_row(first, final):
+    plane = lax.broadcasted_iota(jnp.int32, (PLANES, 128), 0)
+    lane = lax.broadcasted_iota(jnp.int32, (PLANES, 128), 1)
+    row = jnp.zeros((PLANES, 128), jnp.float32)
+    for c, x in enumerate((first[:, :1], first[:, CB - 1 :], final[:, :1], final[:, CB - 1 :])):
+        row = jnp.where(lane == plane + c * PLANES, x, row)
+    return jnp.sum(row, axis=0, keepdims=True)
+
+
+def pack_kernel(devices, span, owner_any, column_any, misfit_any, state_any, out_any, owner_ref, column_ref, misfit_ref, place_ref, acc_ref, out_ref, tile_ref, sem):
+    pairs = [(owner_any, owner_ref), (column_any, column_ref), (misfit_any, misfit_ref)]
+    pairs += [(state_any.at[:, pl.ds(at, 8)], tile_ref.at[n]) for n, at in enumerate((0, CA - 8))]
+    loads = [pltpu.make_async_copy(x, y, sem.at[n]) for n, (x, y) in enumerate(pairs)]
+    for load in loads:
+        load.start()
+    loads[0].wait()
+    slots(owner_ref, place_ref, devices)
+    for load in loads[1:]:
+        load.wait()
+    first = jnp.concatenate([tile_ref[0, p, :1, :] for p in range(PLANES)], axis=0)
+    final = jnp.concatenate([tile_ref[1, p, 7:, :] for p in range(PLANES)], axis=0)
+    out_ref[pl.ds(WORDS, devices, stride=WIRE), :] = jnp.broadcast_to(corner_row(first, final), (devices, 128))
+    gather(span, owner_ref, place_ref, column_ref, misfit_ref, acc_ref)
+    groups = devices // 4
     left = lax.broadcasted_iota(jnp.int32, (groups, 128), 1) < CAP
     for k in range(WORDS):
         for j in range(2):
-            a = first_ref[pl.ds(k * groups, groups), pl.ds(j * 128, 128)]
-            b = acc_ref[pl.ds(k * groups, groups), pl.ds(j * 128, 128)]
-            out_ref[pl.ds(2 * j * WORDS + k, groups, stride=4 * WORDS), :] = jnp.where(left, a, pltpu.roll(b, CAP, 1))
-            out_ref[pl.ds((2 * j + 1) * WORDS + k, groups, stride=4 * WORDS), :] = jnp.where(left, pltpu.roll(a, CAP, 1), b)
-
-
-def gather(records, devices, first=None, span=1024):
-    rows = WORDS * devices // 4
-    if first is None:
-        kernel, shape, extra, scratch, name = gather_first_kernel, (rows, CHUNK), (), [], "gather_first"
-    else:
-        kernel, shape, extra, name = gather_second_kernel, (devices * WORDS, 128), (first,), "gather_second"
-        scratch = [pltpu.VMEM((rows, CHUNK), jnp.float32)]
+            a = acc_ref[0, pl.ds(k * groups, groups), pl.ds(j * 128, 128)]
+            b = acc_ref[1, pl.ds(k * groups, groups), pl.ds(j * 128, 128)]
+            out_ref[pl.ds(2 * j * WIRE + k, groups, stride=4 * WIRE), :] = jnp.where(left, a, pltpu.roll(b, CAP, 1))
+            out_ref[pl.ds((2 * j + 1) * WIRE + k, groups, stride=4 * WIRE), :] = jnp.where(left, pltpu.roll(a, CAP, 1), b)
+    store = pltpu.make_async_copy(out_ref, out_any, sem.at[5])
+    store.start()
+    store.wait()
+
+
+def pack(owner, column, misfit, state, devices, span=1024):
+    sent = jax.ShapeDtypeStruct((devices * WIRE, 128), jnp.float32)
     return pl.pallas_call(
-        functools.partial(kernel, span),
-        out_shape=jax.ShapeDtypeStruct(shape, jnp.float32),
-        in_specs=[WHOLE] * (4 + len(extra)),
-        out_specs=WHOLE,
-        scratch_shapes=scratch,
-        compiler_params=PARAMS,
-        name=name,
-    )(*records, *extra)
+        functools.partial(pack_kernel, devices, span),
+        out_shape=sent,
+        in_specs=[ANYWHERE] * 4,
+        out_specs=ANYWHERE,
+        scratch_shapes=[
+            pltpu.VMEM(owner.shape, jnp.int32),
+            pltpu.VMEM(column.shape, jnp.int32),
+            pltpu.VMEM(misfit.shape, jnp.float32),
+            pltpu.VMEM(owner.shape, jnp.int32),
+            pltpu.VMEM((STEPS, WORDS * devices // 4, CHUNK), jnp.float32),
+            pltpu.VMEM(sent.shape, jnp.float32),
+            pltpu.VMEM((2, PLANES, 8, CB), jnp.float32),
+            pltpu.SemaphoreType.DMA((6,)),
+        ],
+        compiler_params=FULL,
+        name="pack",
+    )(owner, column, misfit, state)
 
 
 def exchange(keys, span, reach):
@@ -157,8 +177,8 @@
     left = lanes < CAP
 
     def list_of(k):
-        a = got_ref[pl.ds(k, 64, stride=WORDS), :]
-        b = got_ref[pl.ds(64 * WORDS + k, 64, stride=WORDS), :]
+        a = got_ref[pl.ds(k, 64, stride=WIRE), :]
+        b = got_ref[pl.ds(64 * WIRE + k, 64, stride=WIRE), :]
         first = jnp.where(left[:64], a, pltpu.roll(b, CAP, 1))
         second = jnp.where(left[:64], pltpu.roll(a, CAP, 1), b)
         return jnp.concatenate([first, second], axis=0)
@@ -245,44 +265,20 @@
     lax.fori_loop(chunks_from, chunks_to, rest, 0)
 
 
-FIELDS = 4
-PLANES = FIELDS * LEV
-
-
-def edge_lines(plane, top_ref, bottom_ref, left_ref, right_ref):
+def row_lines(plane, count, top_ref, bottom_ref):
+    for p in range(count):
+        top_ref[p : p + 1, :] = plane(p, pl.ds(0, 8), pl.ds(0, CB))[:1]
+        bottom_ref[p : p + 1, :] = plane(p, pl.ds(CA - 8, 8), pl.ds(0, CB))[7:]
+
+
+def column_lines(plane, count):
     lane = lax.broadcasted_iota(jnp.int32, (CA, 128), 1)
     picked = jnp.zeros((CA, 128), jnp.float32)
-    for p in range(PLANES):
-        top_ref[p : p + 1, :] = plane(p, pl.ds(0, 8), pl.ds(0, CB))[:1]
-        bottom_ref[p : p + 1, :] = plane(p, pl.ds(CA - 8, 8), pl.ds(0, CB))[7:]
+    for p in range(count):
         picked = jnp.where(lane == p, plane(p, pl.ds(0, CA), pl.ds(0, 128))[:, :1], picked)
-        picked = jnp.where(lane == PLANES + p, plane(p, pl.ds(0, CA), pl.ds(CB - 128, 128))[:, 127:], picked)
+        picked = jnp.where(lane == count + p, plane(p, pl.ds(0, CA), pl.ds(CB - 128, 128))[:, 127:], picked)
     lines = picked.T
-    left_ref[...] = lines[:PLANES]
-    right_ref[...] = lines[PLANES : 2 * PLANES]
-
-
-EDGES = (
-    jax.ShapeDtypeStruct((PLANES, CB), jnp.float32),
-    jax.ShapeDtypeStruct((PLANES, CB), jnp.float32),
-    jax.ShapeDtypeStruct((PLANES, CA), jnp.float32),
-    jax.ShapeDtypeStruct((PLANES, CA), jnp.float32),
-)
-
-
-def first_edges_kernel(state_ref, *edge_refs):
-    edge_lines(lambda p, rows, cols: state_ref[p, rows, cols], *edge_refs)
-
-
-def first_edges(state):
-    return pl.pallas_call(
-        first_edges_kernel,
-        out_shape=EDGES,
-        in_specs=[WHOLE],
-        out_specs=[WHOLE] * 4,
-        compiler_params=PARAMS,
-        name="first_edges",
-    )(state)
+    return lines[:count], lines[count : 2 * count]
 
 
 def moved(x, axis, forward):
@@ -295,36 +291,117 @@
     return lax.optimization_barrier((x, *others))
 
 
-def step_kernel(forced, ts_ref, uv_ref, before_ref, after_ref, prior_ref, next_ref, mix_h_ref, mix_v_ref, courant_ref, turn_ref, *rest):
-    forcing_ref, out_ref, state_ref, column_ref, sem = rest if forced else (None, *rest)
+FRAME = PLANES + 2 * LEV
+
+
+def per_plane(levels):
+    return jnp.concatenate([levels] * FIELDS, axis=0)
+
+
+def inside(ref, there):
+    return jnp.where(there, ref[...], 0.0)
+
+
+def write_frame(plane, mix_h_ref, courant_ref, frame_ref):
+    columns = column_lines(plane, PLANES)
+    mix = column_lines(lambda k, rows, cols: mix_h_ref[k, rows, cols], LEV)
+    along = column_lines(lambda k, rows, cols: courant_ref[0, k, rows, cols], LEV)
+    across = column_lines(lambda k, rows, cols: courant_ref[1, k, rows, cols], LEV)
+    place = lax.broadcasted_iota(jnp.int32, (LEV, CA), 1)
+    for n, sign in ((0, -0.5), (1, 0.5)):
+        ends = jnp.where(place == 0, mix[n] - 0.5 * along[n], jnp.where(place == CA - 1, mix[n] + 0.5 * along[n], 0.0))
+        frame_ref[2 * FRAME :, n * CA : (n + 1) * CA] = jnp.concatenate([columns[n], mix[n] + sign * across[n], ends], axis=0)
+    place = lax.broadcasted_iota(jnp.int32, (LEV, CB), 1)
+    for n, sign, at in ((0, -0.5, 0), (1, 0.5, 7)):
+        rows = pl.ds((CA - 8) * n, 8)
+
+        def line(read, count):
+            return jnp.concatenate([read(k, rows, pl.ds(0, CB))[at : at + 1] for k in range(count)], axis=0)
+
+        mix = line(lambda k, rows, cols: mix_h_ref[k, rows, cols], LEV)
+        along = line(lambda k, rows, cols: courant_ref[0, k, rows, cols], LEV)
+        across = line(lambda k, rows, cols: courant_ref[1, k, rows, cols], LEV)
+        ends = jnp.where(place == 0, mix - 0.5 * across, jnp.where(place == CB - 1, mix + 0.5 * across, 0.0))
+        frame_ref[n * FRAME : (n + 1) * FRAME, :] = jnp.concatenate([line(plane, PLANES), mix + sign * along, ends], axis=0)
+
+
+def ends_of(length, first, final):
+    place = lax.broadcasted_iota(jnp.int32, (PLANES, length), 1)
+    return jnp.where(place == 0, first, jnp.where(place == length - 1, final, 0.0))
+
+
+def beside(sent, own, corners):
+    edge, factor, ends = sent[:PLANES], sent[2 * PLANES : 2 * PLANES + LEV], sent[2 * PLANES + LEV :]
+    return edge + per_plane(factor) * own[:PLANES] + per_plane(ends) * corners
+
+
+def gained(sent, own):
+    return per_plane(own[PLANES : PLANES + LEV]) * sent[PLANES : 2 * PLANES]
+
+
+def step_kernel(last, *refs):
     half = PLANES // 2
-    loads = [
-        pltpu.make_async_copy(ts_ref.at[pl.ds(0, half)], state_ref.at[pl.ds(0, half), pl.ds(8, CA)], sem.at[0]),
-        pltpu.make_async_copy(uv_ref.at[pl.ds(half, half)], state_ref.at[pl.ds(half, half), pl.ds(8, CA)], sem.at[1]),
-    ]
+    if last:
+        ts_any, uv_any, mix_h_ref, mix_v_ref, courant_ref, turn_ref, *sent_refs, frame_ref, corner_ref, forcing_ref, out_any, state_ref, column_ref, out_ref, sem, out_sem = refs
+        uv_any_half = uv_any
+    else:
+        ts_any, mix_h_any, mix_v_any, courant_any, turn_any, ts_out, uv_out, frame_any, edge_any = refs[:9]
+        state_ref, mix_h_ref, mix_v_ref, courant_ref, turn_ref, frame_ref, edge_ref, out_ref, sem, out_sem = refs[9:]
+        uv_any_half = ts_any.at[pl.ds(half, half)]
+    pairs = [(ts_any.at[pl.ds(0, half)], state_ref.at[pl.ds(0, half), pl.ds(8, CA)]), (uv_any_half, state_ref.at[pl.ds(half, half), pl.ds(8, CA)])]
+    if not last:
+        pairs += [(mix_h_any, mix_h_ref), (mix_v_any, mix_v_ref), (courant_any, courant_ref), (turn_any, turn_ref)]
+    loads = [pltpu.make_async_copy(x, y, sem.at[n]) for n, (x, y) in enumerate(pairs)]
     for load in loads:
         load.start()
-    tx, ty = lax.axis_index("tx"), lax.axis_index("ty")
-
-    def inside(ref, there):
-        return jnp.where(there, ref[...], 0.0)
-
-    before = inside(before_ref, tx > 0)
-    after = inside(after_ref, tx < lax.axis_size("tx") - 1)
-    for p in range(PLANES):
-        state_ref[p, 0:8, :] = jnp.broadcast_to(before[p : p + 1, :], (8, CB))
-        state_ref[p, CA + 8 : CA + 16, :] = jnp.broadcast_to(after[p : p + 1, :], (8, CB))
-    sides = [inside(prior_ref, ty > 0), inside(next_ref, ty < lax.axis_size("ty") - 1)]
-    column_ref[...] = jnp.concatenate(sides + [jnp.zeros((128 - 2 * PLANES, CA), jnp.float32)], axis=0).T
+    if last:
+        tx, ty = lax.axis_index("tx"), lax.axis_index("ty")
+        there = tx > 0, tx < lax.axis_size("tx") - 1, ty > 0, ty < lax.axis_size("ty") - 1
+        before, after, prior, next_ = [inside(ref, flag) for ref, flag in zip(sent_refs, there)]
+        top, bottom = frame_ref[:FRAME], frame_ref[FRAME : 2 * FRAME]
+        left, right = frame_ref[2 * FRAME :, :CA], frame_ref[2 * FRAME :, CA:]
+        corner = [corner_ref[:, c : c + 1] for c in range(4)]
+        beside_prior = beside(prior, left, ends_of(CA, corner[3], corner[1]))
+        beside_next = beside(next_, right, ends_of(CA, corner[2], corner[0]))
+        spare = jnp.zeros((128 - 4 * PLANES, CA), jnp.float32)
+        column_ref[...] = jnp.concatenate([beside_prior, beside_next, gained(prior, left), gained(next_, right), spare], axis=0).T
+        beside_before = beside(before, top, ends_of(CB, corner[3], corner[2]))
+        beside_after = beside(after, bottom, ends_of(CB, corner[1], corner[0]))
+        gain_before, gain_after = gained(before, top), gained(after, bottom)
+        for p in range(PLANES):
+            state_ref[p, 0:8, :] = jnp.broadcast_to(beside_before[p : p + 1, :], (8, CB))
+            state_ref[p, CA + 8 : CA + 16, :] = jnp.broadcast_to(beside_after[p : p + 1, :], (8, CB))
+    else:
+        state_ref[:, 0:8, :] = jnp.zeros((PLANES, 8, CB), jnp.float32)
+        state_ref[:, CA + 8 : CA + 16, :] = jnp.zeros((PLANES, 8, CB), jnp.float32)
     for load in loads:
         load.wait()
+    if last:
+        edge = lax.broadcasted_iota(jnp.int32, (CA, 128), 1)
+        for p in range(PLANES):
+            for lanes, at, n in ((pl.ds(0, 128), 0, 2), (pl.ds(CB - 128, 128), 127, 3)):
+                gain = column_ref[:, n * PLANES + p : n * PLANES + p + 1]
+                state_ref[p, pl.ds(8, CA), lanes] += jnp.where(edge == at, gain, 0.0)
+            state_ref[p, 8:9, :] += gain_before[p : p + 1, :]
+            state_ref[p, CA + 7 : CA + 8, :] += gain_after[p : p + 1, :]
+    else:
+        write_frame(lambda p, rows, cols: state_ref[p, pl.ds(8 + rows.start, rows.size), cols], mix_h_ref, courant_ref, frame_ref)
+        frame_store = pltpu.make_async_copy(frame_ref, frame_any, sem.at[6])
+        frame_store.start()
     sub = lax.broadcasted_iota(jnp.int32, (8, CB), 0)
     lane = lax.broadcasted_iota(jnp.int32, (8, CB), 1)
+
+    def store_of(i):
+        rows = pl.ds(pl.multiple_of(i * 8, 8), 8)
+        if last:
+            return [pltpu.make_async_copy(out_ref.at[:, rows], out_any.at[:, rows], out_sem.at[0, i])]
+        parts = (pl.ds(0, half), ts_out), (pl.ds(half, half), uv_out)
+        return [pltpu.make_async_copy(out_ref.at[planes, rows], out.at[:, rows], out_sem.at[n, i]) for n, (planes, out) in enumerate(parts)]
 
     def strip(i, carry):
         at = pl.multiple_of(i * 8, 8)
         rows = pl.ds(at, 8)
-        sides = column_ref[rows, :]
+        sides = column_ref[rows, :] if last else None
         turn = turn_ref[rows, :]
         mix_v = [mix_v_ref[k, rows, :] for k in range(LEV - 1)]
         centre = [state_ref[p, pl.ds(at + 8, 8), :] for p in range(PLANES)]
@@ -339,8 +416,8 @@
                 above = state_ref[p, pl.ds(at + 16, 8), :]
                 up = jnp.where(sub == 7, pltpu.roll(above, 7, 0), pltpu.roll(a, 7, 0))
                 down = jnp.where(sub == 0, pltpu.roll(below, 1, 0), pltpu.roll(a, 1, 0))
-                right = jnp.where(lane == CB - 1, sides[:, PLANES + p : PLANES + p + 1], pltpu.roll(a, CB - 1, 1))
-                left = jnp.where(lane == 0, sides[:, p : p + 1], pltpu.roll(a, 1, 1))
+                right = jnp.where(lane == CB - 1, sides[:, PLANES + p : PLANES + p + 1] if last else 0.0, pltpu.roll(a, CB - 1, 1))
+                left = jnp.where(lane == 0, sides[:, p : p + 1] if last else 0.0, pltpu.roll(a, 1, 1))
                 new = a + mix_h * (up + down + right + left - 4.0 * a) + c0 * (up - down) + c1 * (right - left)
                 if k < LEV - 1:
                     new = new + mix_v[k] * (centre[p + 1] - a)
@@ -350,25 +427,65 @@
                     new = new + turn * centre[p + LEV]
                 if f == 3:
                     new = new - turn * centre[p - LEV]
-                if forced and f < 2:
+                if last and f < 2:
                     new = new + forcing_ref[p, rows, :]
                 out_ref[p, rows, :] = new
+        for store in store_of(i):
+            store.start()
         return carry
 
+    def finish(i, carry):
+        for store in store_of(i):
+            store.wait()
+        return carry
+
     lax.fori_loop(0, CA // 8, strip, 0)
-
-
-def step(ts, uv, halos, coefficients, forcing=None):
-    extra = () if forcing is None else (forcing,)
+    if not last:
+
+        def plane(p, rows, cols):
+            return out_ref[half + p, rows, cols]
+
+        row_lines(plane, half, edge_ref.at[pl.ds(0, half)], edge_ref.at[pl.ds(half, half)])
+        edge_ref[PLANES:, :CA], edge_ref[PLANES:, CA:] = column_lines(plane, half)
+        edge_store = pltpu.make_async_copy(edge_ref, edge_any, sem.at[7])
+        edge_store.start()
+    lax.fori_loop(0, CA // 8, finish, 0)
+    if not last:
+        frame_store.wait()
+        edge_store.wait()
+
+
+HALF = jax.ShapeDtypeStruct((PLANES // 2, CA, CB), jnp.float32)
+
+
+def first_step(state, coefficients):
+    frame = jax.ShapeDtypeStruct((3 * FRAME, CB), jnp.float32)
+    edge = jax.ShapeDtypeStruct((PLANES + PLANES // 2, CB), jnp.float32)
+    scratch = [pltpu.VMEM((PLANES, CA + 16, CB), jnp.float32)] + [pltpu.VMEM(x.shape, jnp.float32) for x in (*coefficients, frame, edge)]
+    scratch += [pltpu.VMEM((PLANES, CA, CB), jnp.float32), pltpu.SemaphoreType.DMA((8,)), pltpu.SemaphoreType.DMA((2, CA // 8))]
     return pl.pallas_call(
-        functools.partial(step_kernel, forcing is not None),
+        functools.partial(step_kernel, False),
+        out_shape=(HALF, HALF, frame, edge),
+        in_specs=[ANYWHERE] * 5,
+        out_specs=[ANYWHERE] * 4,
+        scratch_shapes=scratch,
+        compiler_params=FULL,
+        name="first_step",
+    )(state, *coefficients)
+
+
+def last_step(ts, uv, coefficients, sent, frame, corners, forcing):
+    scratch = [pltpu.VMEM((PLANES, CA + 16, CB), jnp.float32), pltpu.VMEM((CA, 128), jnp.float32)]
+    scratch += [pltpu.VMEM((PLANES, CA, CB), jnp.float32), pltpu.SemaphoreType.DMA((2,)), pltpu.SemaphoreType.DMA((1, CA // 8))]
+    return pl.pallas_call(
+        functools.partial(step_kernel, True),
         out_shape=jax.ShapeDtypeStruct((PLANES, CA, CB), jnp.float32),
-        in_specs=[ANYWHERE] * 2 + [WHOLE] * (8 + len(extra)),
-        out_specs=WHOLE,
-        scratch_shapes=[pltpu.VMEM((PLANES, CA + 16, CB), jnp.float32), pltpu.VMEM((CA, 128), jnp.float32), pltpu.SemaphoreType.DMA((2,))],
-        compiler_params=PARAMS,
-        name="advance",
-    )(ts, uv, *halos, *coefficients, *extra)
+        in_specs=[ANYWHERE] * 2 + [WHOLE] * 11,
+        out_specs=ANYWHERE,
+        scratch_shapes=scratch,
+        compiler_params=STEP,
+        name="last_step",
+    )(ts, uv, *coefficients, *sent, frame, corners, forcing)
 
 
 LISTS = (
@@ -380,29 +497,73 @@
 WINDOW, UNROLL = 40, 8
 
 
-def first_records_kernel(got_ref, still_ref, ts_ref, high_ref, low_ref, cell_ref, edge_ref, top_ref, bottom_ref, left_ref, right_ref, smem_ref, sem):
+def corner_columns(got_ref):
+    tx, ty = lax.axis_index("tx"), lax.axis_index("ty")
+    rows, columns = lax.axis_size("tx"), lax.axis_size("ty")
+    plane = lax.broadcasted_iota(jnp.int32, (PLANES, 128), 0)
+    lane = lax.broadcasted_iota(jnp.int32, (PLANES, 128), 1)
+    out = jnp.zeros((PLANES, 128), jnp.float32)
+    for c, (x, y) in enumerate(((1, 1), (1, -1), (-1, 1), (-1, -1))):
+        there = (tx + x >= 0) & (tx + x < rows) & (ty + y >= 0) & (ty + y < columns)
+        source = jnp.where(there, (tx + x) * columns + ty + y, 0)
+        row = got_ref[pl.ds(source * WIRE + WORDS, 1), :]
+        picked = jnp.sum(jnp.where(lane == plane + c * PLANES, row, 0.0), axis=1, keepdims=True)
+        out = jnp.where((lane == c) & there, picked, out)
+    return out
+
+
+def order_all_kernel(got_any, high_ref, low_ref, cell_ref, edge_ref, corner_ref, got_ref, sem):
+    load = pltpu.make_async_copy(got_any, got_ref, sem)
+    load.start()
+    load.wait()
     order_kernel(got_ref, high_ref, low_ref, cell_ref)
     bounds_of(cell_ref, edge_ref)
-    copy = pltpu.make_async_copy(edge_ref, smem_ref, sem)
-    copy.start()
-    ts_ref[...] = still_ref[: PLANES // 2]
-    copy.wait()
-    spread_step(0, 0, 32, WINDOW, UNROLL, high_ref, low_ref, cell_ref, smem_ref, ts_ref)
+    corner_ref[...] = corner_columns(got_ref)
+
+
+def order(got):
+    *lists, corners = pl.pallas_call(
+        order_all_kernel,
+        out_shape=LISTS + (jax.ShapeDtypeStruct((PLANES, 128), jnp.float32),),
+        in_specs=[ANYWHERE],
+        out_specs=[WHOLE] * 5,
+        scratch_shapes=[pltpu.VMEM(got.shape, jnp.float32), pltpu.SemaphoreType.DMA(())],
+        compiler_params=PARAMS,
+        name="order",
+    )(got)
+    return lists, corners
+
+
+def first_records_kernel(high_ref, low_ref, cell_ref, edge_ref, still_ref, frame_ref, uv_edge_ref, ts_ref, top_ref, bottom_ref, left_ref, right_ref):
     half = PLANES // 2
-    edge_lines(lambda p, rows, cols: (ts_ref if p < half else still_ref)[p, rows, cols], top_ref, bottom_ref, left_ref, right_ref)
-
-
-def first_records(got, still):
-    out = pl.pallas_call(
+    ts_ref[...] = still_ref[...]
+    spread_step(0, 0, 32, WINDOW, UNROLL, high_ref, low_ref, cell_ref, edge_ref, ts_ref)
+
+    def plane(p, rows, cols):
+        return ts_ref[p, rows, cols]
+
+    row_lines(plane, half, top_ref, bottom_ref)
+    left_ref[:half, :], right_ref[:half, :] = column_lines(plane, half)
+    for n, (line, side) in enumerate(((top_ref, left_ref), (bottom_ref, right_ref))):
+        line[half:PLANES, :] = uv_edge_ref[n * half : (n + 1) * half, :]
+        line[PLANES:, :] = frame_ref[n * FRAME : (n + 1) * FRAME, :]
+        side[half:PLANES, :] = uv_edge_ref[PLANES:, n * CA : (n + 1) * CA]
+        side[PLANES:, :] = frame_ref[2 * FRAME :, n * CA : (n + 1) * CA]
+
+
+EDGES = (jax.ShapeDtypeStruct((PLANES + FRAME, CB), jnp.float32),) * 2 + (jax.ShapeDtypeStruct((PLANES + FRAME, CA), jnp.float32),) * 2
+
+
+def first_records(lists, still, frame, uv_edges):
+    ts, *edges = pl.pallas_call(
         first_records_kernel,
-        out_shape=(jax.ShapeDtypeStruct((PLANES // 2, CA, CB), jnp.float32),) + LISTS + EDGES,
-        in_specs=[WHOLE] * 2,
-        out_specs=[WHOLE] * 9,
-        scratch_shapes=[pltpu.SMEM((8, 128), jnp.int32), pltpu.SemaphoreType.DMA(())],
+        out_shape=(HALF,) + EDGES,
+        in_specs=[WHOLE] * 3 + [pl.BlockSpec(memory_space=pltpu.SMEM)] + [WHOLE] * 3,
+        out_specs=[WHOLE] * 5,
         compiler_params=PARAMS,
         name="first_records",
-    )(got, still)
-    return out[0], out[1:5], out[5:]
+    )(*lists, still, frame, uv_edges)
+    return ts, edges
 
 
 def second_records_kernel(part, high_ref, low_ref, cell_ref, edge_ref, *rest):
@@ -427,29 +588,18 @@
     devices = lax.axis_size("tx") * lax.axis_size("ty")
     state = adjoint_start.reshape(PLANES, CA, CB)
     coefficients = (mixing_h, mixing_v, courant, coriolis)
-    owner = owner.transpose(0, 2, 1)
-    top, bottom, left, right = first_edges(state)
-    places = slots(owner, devices)
-    right, places = after(right, places)
-    prior = moved(right, "ty", True)
-    records = (owner, places, column, misfit)
-    first = gather(records, devices)
-    left, top, bottom, first = after(left, top, bottom, first)
-    next_ = moved(left, "ty", False)
-    sent = gather(records, devices, first)
-    top, bottom, sent = after(top, bottom, sent)
-    halos = moved(bottom, "tx", True), moved(top, "tx", False), prior, next_
-    got = lax.all_to_all(sent.reshape(devices, 1, WORDS * 128), ("tx", "ty"), split_axis=0, concat_axis=0, tiled=True)
-    still = step(state, state, halos, coefficients)
-
-    ts, lists, (top, bottom, left, right) = first_records(got.reshape(devices * WORDS, 128), still)
+    sent = pack(owner.transpose(0, 2, 1), column, misfit, state, devices)
+    got = lax.all_to_all(sent.reshape(devices, 1, WIRE * 128), ("tx", "ty"), split_axis=0, concat_axis=0, tiled=True)
+    still, uv, frame, uv_edges = first_step(state, coefficients)
+    lists, corners = order(got.reshape(devices * WIRE, 128))
+    ts, (top, bottom, left, right) = first_records(lists, still, frame, uv_edges)
     before, after_ = moved(bottom, "tx", True), moved(top, "tx", False)
     prior = moved(right, "ty", True)
     forcing = second_records(lists, 0)
     left, forcing = after(left, forcing)
     next_ = moved(left, "ty", False)
     forcing = second_records(lists, 1, (forcing,))
-    return step(ts, still, (before, after_, prior, next_), coefficients, forcing).reshape(FIELDS, LEV, CA, CB)
+    return last_step(ts, uv, coefficients, (before, after_, prior, next_), frame, corners, forcing).reshape(FIELDS, LEV, CA, CB)
 
 
 def solution(mesh):

time: 68.8 us -> 64.2 us (0.933)
  starting transfers between devices: 28.3 us -> 19.5 us
  waiting for transfers between devices: 2.32 us -> 7.74 us
  local copies, waits for them, and re-layouts: 3.62 us -> 2.87 us
    ppermute x8 -> x4, starting transfers between devices: 16.7 us -> 8.38 us  [moved(): return lax.ppermute(x, axis, pairs)]
    all_to_all x1, waiting for transfers between devices: 0.01 us -> 7.73 us  [local(): lax.all_to_all(sent.reshape(devices, 1, WIRE * 128), ('tx', 'ty'), split_...]
    ppermute x8 -> x4, waiting for transfers between devices: 2.32 us -> 0.01 us  [moved(): return lax.ppermute(x, axis, pairs)]
    unnamed x22 -> x18, local copies, waits for them, and re-layouts: 3.62 us -> 2.87 us
    pallas_call x7 -> x5, Pallas kernels: 28 us -> 27.4 us  [the longest x1 7.22 us: first_step(): pl.pallas_call(functools.partial(step_kernel, False), out_shape=(HALF, HA...]
  transfers between devices with their start and end apart: 9 -> 5, of which waited for: 1 -> 1; matrix products, arithmetic and copies ran while one was open for 0% -> 0% of each run, Pallas kernels for 16% -> 21%
where the time goes in v3:
time: 64.2 us; the launch traced here: 63.9 us
  Pallas kernels  33.5 us (52%)
  starting transfers between devices  19.5 us (30%)
  waiting for transfers between devices  7.74 us (12%)
  local copies, waits for them, and re-layouts  2.87 us (4%)
    all_to_all x1, starting transfers between devices, local(): lax.all_to_all(sent.reshape(devices, 1, WIRE * 128), ('tx', 'ty'), split_...  11.1 us
    ppermute x4, starting transfers between devices, moved(): return lax.ppermute(x, axis, pairs)  8.38 us
    all_to_all x1, waiting for transfers between devices, local(): lax.all_to_all(sent.reshape(devices, 1, WIRE * 128), ('tx', 'ty'), split_...  7.73 us
    pallas_call x1, Pallas kernels, first_step(): pl.pallas_call(functools.partial(step_kernel, False), out_shape=(HALF, HA...  7.22 us
    pallas_call x1, Pallas kernels, pack(): pl.pallas_call(functools.partial(pack_kernel, devices, span), out_shape=s...  6.86 us
    pallas_call x2, Pallas kernels, second_records(): pl.pallas_call(functools.partial(second_records_kernel, part), out_shape=...  6.1 us
    pallas_call x1, Pallas kernels, first_records(): pl.pallas_call(first_records_kernel, out_shape=(HALF,) + EDGES, in_specs=...  5.75 us
    pallas_call x1, Pallas kernels, last_step(): pl.pallas_call(functools.partial(step_kernel, True), out_shape=jax.ShapeD...  5.22 us
  transfers between devices with their start and end apart: 5, of which 1 were waited for; matrix products, arithmetic and copies ran while one was open for 0% of the time, Pallas kernels for 21%

profile of v3, /device:TPU:0, one launch (start us, length us, event | category | flops | bytes accessed | tf_op | source)
XLA Modules:
  0.0 63.9 jit_solution(16320114619660632885)
XLA Ops:
  0.0 6.9 %pack.1 = f32[1280,128]{1,0:T(8,128)} custom-call(s32[2,1,4096]{2,1,0:T(1,128)} %bitcast.9, s32[2,4096]{1,0:T(2,128)} %column_any.1, f32[2,8,4096]{2,1,0:T(8,128)} %misfit_any.1, f32[16,128,256]{2,1,0:T(8,128)} %bitcast.6), custom_call_target="tpu_custom_call" | custom-call | tf_op jit(solution)/shard_map/pack/pallas_call | solution.py:116
  6.9 11.1 %all-to-all-start = ((f32[128,1,1280]{2,1,0:T(1,128)}), f32[128,1,1280]{2,1,0:T(1,128)S(1)}, u32[]{:S(2)}, u32[]{:S(2)}) async-start(f32[128,1,1280]{2,1,0:T(1,128)} %bitcast.8), calls=%async_computation | async-start | bytes 1310720 | tf_op jit(solution)/shard_map/all_to_all | solution.py:592
  18.0 7.2 %first_step.1 = (f32[8,128,256]{2,1,0:T(8,128)}, f32[8,128,256]{2,1,0:T(8,128)}, f32[72,256]{1,0:T(8,128)}, f32[24,256]{1,0:T(8,128)}) custom-call(f32[16,128,256]{2,1,0:T(8,128)} %bitcast.7, f32[4,128,256]{2,1,0:T(8,128)} %refs_2_.3, f32[3,128,256]{2,1,0:T(8,128)} %refs_3_.3, f32[2,4,128,256]{3,2,1,0:T(8,128)} %refs_4_.3, f32[128,256]{1,0:T(8,128)} %refs_5_.1), custom_call_target="tpu_custom_call" | custom-call | tf_op jit(solution)/shard_map/first_step/pallas_call | solution.py:466
  25.3 7.7 %all-to-all-done = f32[128,1,1280]{2,1,0:T(1,128)S(1)} async-done(((f32[128,1,1280]{2,1,0:T(1,128)}), f32[128,1,1280]{2,1,0:T(1,128)S(1)}, u32[]{:S(2)}, u32[]{:S(2)}) %all-to-all-start) | async-done | bytes 655392 | tf_op jit(solution)/shard_map/all_to_all | solution.py:592
  33.0 2.4 %order.1 = (f32[2,8,32,256]{3,2,1,0:T(8,128)S(1)}, f32[2,8,32,256]{3,2,1,0:T(8,128)S(1)}, f32[2,1,32,256]{3,2,1,0:T(8,128)S(1)}, s32[8,128]{1,0:T(8,128)S(1)}, f32[16,128]{1,0:T(8,128)S(1)}) custom-call(f32[1280,128]{1,0:T(8,128)S(1)} %bitcast.5), custom_call_target="tpu_custom_call" | custom-call | tf_op jit(solution)/shard_map/order/pallas_call | solution.py:525
  35.4 0.0 copy-start.3
  35.4 1.2 %copy-done.3 = f32[8,128,256]{2,1,0:T(8,128)S(1)} copy-done((f32[8,128,256]{2,1,0:T(8,128)S(1)}, f32[8,128,256]{2,1,0:T(8,128)}, u32[]{:S(2)}) %copy-start.3) | copy-done | bytes 1048600
  36.6 0.9 %copy-done.6 = f32[72,256]{1,0:T(8,128)S(1)} copy-done((f32[72,256]{1,0:T(8,128)S(1)}, f32[72,256]{1,0:T(8,128)}, u32[]{:S(2)}) %copy-start.6) | copy-done | bytes 73752
  37.5 0.7 %copy-done.8 = f32[24,256]{1,0:T(8,128)S(1)} copy-done((f32[24,256]{1,0:T(8,128)S(1)}, f32[24,256]{1,0:T(8,128)}, u32[]{:S(2)}) %copy-start.8) | copy-done | bytes 24600
  38.2 5.7 %first_records.1 = (f32[8,128,256]{2,1,0:T(8,128)S(1)}, f32[40,256]{1,0:T(8,128)S(1)}, f32[40,256]{1,0:T(8,128)S(1)}, f32[40,128]{1,0:T(8,128)S(1)}, f32[40,128]{1,0:T(8,128)S(1)}) custom-call(f32[2,8,32,256]{3,2,1,0:T(8,128)S(1)} %get-tuple-element.21.high_ref, f32[2,8,32,256]{3,2,1,0:T(8,128)S(1)} %get-tuple-element.22.low_ref, ...), custom_call_target="tpu_custom_call" | custom-call | tf_op jit(solution)/shard_map/first_records/pallas_call | solution.py:558
  44.0 0.0 collective-permute-start
  44.0 3.0 %collective-permute-start.1 = (f32[40,256]{1,0:T(8,128)S(1)}, f32[40,256]{1,0:T(8,128)S(1)}, u32[]{:S(2)}, u32[]{:S(2)}) collective-permute-start(f32[40,256]{1,0:T(8,128)S(1)} %get-tuple-element.31), channel_id=1, source_target_pairs={{16,0},{32,16},{48,32},{64,48},{80,64},{96,80},{112,96},{0,112},{1... | collective-permute-start | bytes 122888 | tf_op jit(solution)/shard_map/ppermute | solution.py:287
  46.9 3.0 %second_records.2.rest_0_ = f32[8,128,256]{2,1,0:T(8,128)S(1)} custom-call(f32[2,8,32,256]{3,2,1,0:T(8,128)S(1)} %get-tuple-element.21.high_ref, f32[2,8,32,256]{3,2,1,0:T(8,128)S(1)} %get-tuple-element.22.low_ref, f32[2,1,32,256]{3,2,1,0:T(8,128)S(1)} %get-tuple-element.23.cell_ref, s32[8,128]{1,0:T(8,128)S(1)} %get-tuple-element.24.edge_ref), custom_call_target="tpu_custom_call" | custom-call | tf_op jit(solution)/shard_map/second_records/pallas_call | solution.py:576
  49.9 0.0 copy-start
  50.0 0.0 copy-start.1
  50.0 0.0 copy-start.2
  50.0 0.0 copy-start.4
  50.0 0.0 copy-start.5
  50.0 0.0 copy-start.7
  50.0 0.6 collective-permute-start.2
  50.6 4.8 %collective-permute-start.3 = (f32[40,128]{1,0:T(8,128)S(1)}, f32[40,128]{1,0:T(8,128)S(1)}, u32[]{:S(2)}, u32[]{:S(2)}) collective-permute-start(f32[40,128]{1,0:T(8,128)S(1)} %get-tuple-element.34), channel_id=1, source_target_pairs={{1,0},{2,1},{3,2},{4,3},{5,4},{6,5},{7,6},{8,7},{9,8},{10,9},{11,1... | collective-permute-start | bytes 61448 | tf_op jit(solution)/shard_map/ppermute | solution.py:287
  55.4 3.1 %second_records.3.refs_12_ = f32[8,128,256]{2,1,0:T(8,128)S(1)} custom-call(f32[2,8,32,256]{3,2,1,0:T(8,128)S(1)} %get-tuple-element.21.high_ref, f32[2,8,32,256]{3,2,1,0:T(8,128)S(1)} %get-tuple-element.22.low_ref, f32[2,1,32,256]{3,2,1,0:T(8,128)S(1)} %get-tuple-element.23.cell_ref, ...), custom_call_target="tpu_custom_call", output_to_operand_aliasing={{}: (4, {})} | custom-call | tf_op jit(solution)/shard_map/second_records/pallas_call | solution.py:576
  58.6 0.0 collective-permute-done.2.refs_8_
  58.6 0.0 collective-permute-done.3.refs_9_
  58.6 0.0 collective-permute-done.refs_6_
  58.6 0.0 collective-permute-done.1.refs_7_
  58.6 0.0 copy-done
  58.6 0.0 copy-done.1
  58.6 0.0 copy-done.2
  58.6 0.0 copy-done.4
  58.6 0.0 copy-done.5
  58.7 5.2 %last_step.1 = f32[16,128,256]{2,1,0:T(8,128)} custom-call(f32[8,128,256]{2,1,0:T(8,128)S(1)} %get-tuple-element.28.refs_0_, f32[8,128,256]{2,1,0:T(8,128)S(1)} %copy-done.4, f32[4,128,256]{2,1,0:T(8,128)S(1)} %copy-done.1, f32[3,128,256]{2,1,0:T(8,128)S(1)} %copy-done.2, f32[2,4,128,256]{3,2,1,0:T(8,128)S(1)} %copy-done, f32[128,256]{1,0:T(8,128)S(1)} %copy-done.5, ...), custom_call_target="tpu_custom_call" | custom-call | tf_op jit(solution)/shard_map/last_step/pallas_call | solution.py:480
  (3 shorter events, 0.0 us)
Async XLA Ops:
  6.9 26.1 %all-to-all-start = ((f32[128,1,1280]{2,1,0:T(1,128)}), f32[128,1,1280]{2,1,0:T(1,128)S(1)}, u32[]{:S(2)}, u32[]{:S(2)}) async-start(f32[128,1,1280]{2,1,0:T(1,128)} %bitcast.8), calls=%async_computation | async-start | bytes 1310720 | tf_op jit(solution)/shard_map/all_to_all | solution.py:592
  35.4 1.2 %copy-start.3 = (f32[8,128,256]{2,1,0:T(8,128)S(1)}, f32[8,128,256]{2,1,0:T(8,128)}, u32[]{:S(2)}) copy-start(f32[8,128,256]{2,1,0:T(8,128)} %get-tuple-element.25.still_ref) | copy-start | bytes 3145732
  36.6 0.9 %copy-start.6 = (f32[72,256]{1,0:T(8,128)S(1)}, f32[72,256]{1,0:T(8,128)}, u32[]{:S(2)}) copy-start(f32[72,256]{1,0:T(8,128)} %get-tuple-element.26.frame_ref.refs_10_) | copy-start | bytes 221188
  37.5 0.7 %copy-start.8 = (f32[24,256]{1,0:T(8,128)S(1)}, f32[24,256]{1,0:T(8,128)}, u32[]{:S(2)}) copy-start(f32[24,256]{1,0:T(8,128)} %get-tuple-element.27.uv_edge_ref) | copy-start | bytes 73732
  44.0 14.6 %collective-permute-start = (f32[40,256]{1,0:T(8,128)S(1)}, f32[40,256]{1,0:T(8,128)S(1)}, u32[]{:S(2)}, u32[]{:S(2)}) collective-permute-start(f32[40,256]{1,0:T(8,128)S(1)} %get-tuple-element.30), channel_id=1, source_target_pairs={{0,16},{16,32},{32,48},{48,64},{64,80},{80,96},{96,112},{112,0},{1... | collective-permute-start | bytes 122888 | tf_op jit(solution)/shard_map/ppermute | solution.py:287
  44.0 14.6 %collective-permute-start.1 = (f32[40,256]{1,0:T(8,128)S(1)}, f32[40,256]{1,0:T(8,128)S(1)}, u32[]{:S(2)}, u32[]{:S(2)}) collective-permute-start(f32[40,256]{1,0:T(8,128)S(1)} %get-tuple-element.31), channel_id=1, source_target_pairs={{16,0},{32,16},{48,32},{64,48},{80,64},{96,80},{112,96},{0,112},{1... | collective-permute-start | bytes 122888 | tf_op jit(solution)/shard_map/ppermute | solution.py:287
  49.9 8.7 %copy-start = (f32[2,4,128,256]{3,2,1,0:T(8,128)S(1)}, f32[2,4,128,256]{3,2,1,0:T(8,128)}, u32[]{:S(2)}) copy-start(f32[2,4,128,256]{3,2,1,0:T(8,128)} %refs_4_.3) | copy-start | bytes 3145732
  50.0 8.7 %copy-start.1 = (f32[4,128,256]{2,1,0:T(8,128)S(1)}, f32[4,128,256]{2,1,0:T(8,128)}, u32[]{:S(2)}) copy-start(f32[4,128,256]{2,1,0:T(8,128)} %refs_2_.3) | copy-start | bytes 1572868
  50.0 8.6 %copy-start.2 = (f32[3,128,256]{2,1,0:T(8,128)S(1)}, f32[3,128,256]{2,1,0:T(8,128)}, u32[]{:S(2)}) copy-start(f32[3,128,256]{2,1,0:T(8,128)} %refs_3_.3) | copy-start | bytes 1179652
  50.0 8.6 %copy-start.4 = (f32[8,128,256]{2,1,0:T(8,128)S(1)}, f32[8,128,256]{2,1,0:T(8,128)}, u32[]{:S(2)}) copy-start(f32[8,128,256]{2,1,0:T(8,128)} %get-tuple-element.29.refs_1_) | copy-start | bytes 3145732
  50.0 8.6 %copy-start.5 = (f32[128,256]{1,0:T(8,128)S(1)}, f32[128,256]{1,0:T(8,128)}, u32[]{:S(2)}) copy-start(f32[128,256]{1,0:T(8,128)} %refs_5_.1) | copy-start | bytes 393220
  50.0 8.6 %copy-start.7 = (f32[72,256]{1,0:T(8,128)S(1)}, f32[72,256]{1,0:T(8,128)}, u32[]{:S(2)}) copy-start(f32[72,256]{1,0:T(8,128)} %get-tuple-element.26.frame_ref.refs_10_) | copy-start | bytes 221188
  50.0 8.5 %collective-permute-start.2 = (f32[40,128]{1,0:T(8,128)S(1)}, f32[40,128]{1,0:T(8,128)S(1)}, u32[]{:S(2)}, u32[]{:S(2)}) collective-permute-start(f32[40,128]{1,0:T(8,128)S(1)} %get-tuple-element.32), channel_id=1, source_target_pairs={{0,1},{1,2},{2,3},{3,4},{4,5},{5,6},{6,7},{7,8},{8,9},{9,10},{10,1... | collective-permute-start | bytes 61448 | tf_op jit(solution)/shard_map/ppermute | solution.py:287
  50.6 7.9 %collective-permute-start.3 = (f32[40,128]{1,0:T(8,128)S(1)}, f32[40,128]{1,0:T(8,128)S(1)}, u32[]{:S(2)}, u32[]{:S(2)}) collective-permute-start(f32[40,128]{1,0:T(8,128)S(1)} %get-tuple-element.34), channel_id=1, source_target_pairs={{1,0},{2,1},{3,2},{4,3},{5,4},{6,5},{7,6},{8,7},{9,8},{10,9},{11,1... | collective-permute-start | bytes 61448 | tf_op jit(solution)/shard_map/ppermute | solution.py:287

commit v4 on v3

--- a/solution.py
+++ b/solution.py
@@ -17,7 +17,7 @@
 NT = (((1,), (1,)), ((), ()))
 LIMIT = 24
 WHOLE = pl.BlockSpec(memory_space=pltpu.VMEM)
-ANYWHERE = pl.BlockSpec(memory_space=pl.ANY)
+ANYWHERE = pl.BlockSpec(memory_space=pltpu.HBM)
 PARAMS = pltpu.CompilerParams(vmem_limit_bytes=LIMIT << 20)
 STEP = pltpu.CompilerParams(vmem_limit_bytes=40 << 20)
 FULL = pltpu.CompilerParams(vmem_limit_bytes=63400000)
@@ -281,10 +281,10 @@
     return lines[:count], lines[count : 2 * count]
 
 
-def moved(x, axis, forward):
+def swapped(x, axis, odd):
     count = lax.axis_size(axis)
-    pairs = [(i, (i + 1) % count) if forward else ((i + 1) % count, i) for i in range(count)]
-    return lax.ppermute(x, axis, pairs)
+    pairs = [(i, (i + 1) % count) for i in range(odd, count, 2)]
+    return lax.ppermute(x, axis, pairs + [(j, i) for i, j in pairs])
 
 
 def after(x, *others):
@@ -296,10 +296,6 @@
 
 def per_plane(levels):
     return jnp.concatenate([levels] * FIELDS, axis=0)
-
-
-def inside(ref, there):
-    return jnp.where(there, ref[...], 0.0)
 
 
 def write_frame(plane, mix_h_ref, courant_ref, frame_ref):
@@ -310,7 +306,7 @@
     place = lax.broadcasted_iota(jnp.int32, (LEV, CA), 1)
     for n, sign in ((0, -0.5), (1, 0.5)):
         ends = jnp.where(place == 0, mix[n] - 0.5 * along[n], jnp.where(place == CA - 1, mix[n] + 0.5 * along[n], 0.0))
-        frame_ref[2 * FRAME :, n * CA : (n + 1) * CA] = jnp.concatenate([columns[n], mix[n] + sign * across[n], ends], axis=0)
+        frame_ref[2 * FRAME : 3 * FRAME, n * CA : (n + 1) * CA] = jnp.concatenate([columns[n], mix[n] + sign * across[n], ends], axis=0)
     place = lax.broadcasted_iota(jnp.int32, (LEV, CB), 1)
     for n, sign, at in ((0, -0.5, 0), (1, 0.5, 7)):
         rows = pl.ds((CA - 8) * n, 8)
@@ -345,8 +341,8 @@
         ts_any, uv_any, mix_h_ref, mix_v_ref, courant_ref, turn_ref, *sent_refs, frame_ref, corner_ref, forcing_ref, out_any, state_ref, column_ref, out_ref, sem, out_sem = refs
         uv_any_half = uv_any
     else:
-        ts_any, mix_h_any, mix_v_any, courant_any, turn_any, ts_out, uv_out, frame_any, edge_any = refs[:9]
-        state_ref, mix_h_ref, mix_v_ref, courant_ref, turn_ref, frame_ref, edge_ref, out_ref, sem, out_sem = refs[9:]
+        ts_any, mix_h_any, mix_v_any, courant_any, turn_any, ts_out, uv_out, frame_any = refs[:8]
+        state_ref, mix_h_ref, mix_v_ref, courant_ref, turn_ref, frame_ref, out_ref, sem, out_sem = refs[8:]
         uv_any_half = ts_any.at[pl.ds(half, half)]
     pairs = [(ts_any.at[pl.ds(0, half)], state_ref.at[pl.ds(0, half), pl.ds(8, CA)]), (uv_any_half, state_ref.at[pl.ds(half, half), pl.ds(8, CA)])]
     if not last:
@@ -357,9 +353,14 @@
     if last:
         tx, ty = lax.axis_index("tx"), lax.axis_index("ty")
         there = tx > 0, tx < lax.axis_size("tx") - 1, ty > 0, ty < lax.axis_size("ty") - 1
-        before, after, prior, next_ = [inside(ref, flag) for ref, flag in zip(sent_refs, there)]
+        sent = []
+        for place, even_ref, odd_ref in ((tx, *sent_refs[:2]), (ty, *sent_refs[2:])):
+            even, odd = even_ref[...], odd_ref[...]
+            is_odd = lax.rem(place, 2) == 1
+            sent += [jnp.where(is_odd, even, odd), jnp.where(is_odd, odd, even)]
+        before, after, prior, next_ = [jnp.where(flag, x, 0.0) for x, flag in zip(sent, there)]
         top, bottom = frame_ref[:FRAME], frame_ref[FRAME : 2 * FRAME]
-        left, right = frame_ref[2 * FRAME :, :CA], frame_ref[2 * FRAME :, CA:]
+        left, right = frame_ref[2 * FRAME : 3 * FRAME, :CA], frame_ref[2 * FRAME : 3 * FRAME, CA:]
         corner = [corner_ref[:, c : c + 1] for c in range(4)]
         beside_prior = beside(prior, left, ends_of(CA, corner[3], corner[1]))
         beside_next = beside(next_, right, ends_of(CA, corner[2], corner[0]))
@@ -386,8 +387,6 @@
             state_ref[p, CA + 7 : CA + 8, :] += gain_after[p : p + 1, :]
     else:
         write_frame(lambda p, rows, cols: state_ref[p, pl.ds(8 + rows.start, rows.size), cols], mix_h_ref, courant_ref, frame_ref)
-        frame_store = pltpu.make_async_copy(frame_ref, frame_any, sem.at[6])
-        frame_store.start()
     sub = lax.broadcasted_iota(jnp.int32, (8, CB), 0)
     lane = lax.broadcasted_iota(jnp.int32, (8, CB), 1)
 
@@ -439,35 +438,34 @@
             store.wait()
         return carry
 
-    lax.fori_loop(0, CA // 8, strip, 0)
+    lax.fori_loop(0, CA // 8, strip, 0, unroll=2)
     if not last:
 
         def plane(p, rows, cols):
             return out_ref[half + p, rows, cols]
 
-        row_lines(plane, half, edge_ref.at[pl.ds(0, half)], edge_ref.at[pl.ds(half, half)])
-        edge_ref[PLANES:, :CA], edge_ref[PLANES:, CA:] = column_lines(plane, half)
-        edge_store = pltpu.make_async_copy(edge_ref, edge_any, sem.at[7])
-        edge_store.start()
+        at = 3 * FRAME
+        row_lines(plane, half, frame_ref.at[pl.ds(at, half)], frame_ref.at[pl.ds(at + half, half)])
+        frame_ref[at + PLANES :, :CA], frame_ref[at + PLANES :, CA:] = column_lines(plane, half)
+        frame_store = pltpu.make_async_copy(frame_ref, frame_any, sem.at[6])
+        frame_store.start()
     lax.fori_loop(0, CA // 8, finish, 0)
     if not last:
         frame_store.wait()
-        edge_store.wait()
 
 
 HALF = jax.ShapeDtypeStruct((PLANES // 2, CA, CB), jnp.float32)
 
 
 def first_step(state, coefficients):
-    frame = jax.ShapeDtypeStruct((3 * FRAME, CB), jnp.float32)
-    edge = jax.ShapeDtypeStruct((PLANES + PLANES // 2, CB), jnp.float32)
-    scratch = [pltpu.VMEM((PLANES, CA + 16, CB), jnp.float32)] + [pltpu.VMEM(x.shape, jnp.float32) for x in (*coefficients, frame, edge)]
+    frame = jax.ShapeDtypeStruct((3 * FRAME + PLANES + PLANES // 2, CB), jnp.float32)
+    scratch = [pltpu.VMEM((PLANES, CA + 16, CB), jnp.float32)] + [pltpu.VMEM(x.shape, jnp.float32) for x in (*coefficients, frame)]
     scratch += [pltpu.VMEM((PLANES, CA, CB), jnp.float32), pltpu.SemaphoreType.DMA((8,)), pltpu.SemaphoreType.DMA((2, CA // 8))]
     return pl.pallas_call(
         functools.partial(step_kernel, False),
-        out_shape=(HALF, HALF, frame, edge),
+        out_shape=(HALF, HALF, frame),
         in_specs=[ANYWHERE] * 5,
-        out_specs=[ANYWHERE] * 4,
+        out_specs=[ANYWHERE] * 3,
         scratch_shapes=scratch,
         compiler_params=FULL,
         name="first_step",
@@ -512,76 +510,76 @@
     return out
 
 
-def order_all_kernel(got_any, high_ref, low_ref, cell_ref, edge_ref, corner_ref, got_ref, sem):
-    load = pltpu.make_async_copy(got_any, got_ref, sem)
-    load.start()
-    load.wait()
+def first_records_kernel(got_any, still_any, frame_any, ts_ref, high_ref, low_ref, cell_ref, edge_ref, corner_ref, top_ref, bottom_ref, left_ref, right_ref, got_ref, frame_ref, smem_ref, sem):
+    pairs = (got_any, got_ref), (still_any, ts_ref), (frame_any, frame_ref)
+    loads = [pltpu.make_async_copy(x, y, sem.at[n]) for n, (x, y) in enumerate(pairs)]
+    for load in loads:
+        load.start()
+    loads[0].wait()
     order_kernel(got_ref, high_ref, low_ref, cell_ref)
     bounds_of(cell_ref, edge_ref)
+    copy = pltpu.make_async_copy(edge_ref, smem_ref, sem.at[3])
+    copy.start()
     corner_ref[...] = corner_columns(got_ref)
-
-
-def order(got):
-    *lists, corners = pl.pallas_call(
-        order_all_kernel,
-        out_shape=LISTS + (jax.ShapeDtypeStruct((PLANES, 128), jnp.float32),),
-        in_specs=[ANYWHERE],
-        out_specs=[WHOLE] * 5,
-        scratch_shapes=[pltpu.VMEM(got.shape, jnp.float32), pltpu.SemaphoreType.DMA(())],
-        compiler_params=PARAMS,
-        name="order",
-    )(got)
-    return lists, corners
-
-
-def first_records_kernel(high_ref, low_ref, cell_ref, edge_ref, still_ref, frame_ref, uv_edge_ref, ts_ref, top_ref, bottom_ref, left_ref, right_ref):
+    for load in loads[1:]:
+        load.wait()
+    copy.wait()
     half = PLANES // 2
-    ts_ref[...] = still_ref[...]
-    spread_step(0, 0, 32, WINDOW, UNROLL, high_ref, low_ref, cell_ref, edge_ref, ts_ref)
+    spread_step(0, 0, 32, WINDOW, UNROLL, high_ref, low_ref, cell_ref, smem_ref, ts_ref)
 
     def plane(p, rows, cols):
         return ts_ref[p, rows, cols]
 
-    row_lines(plane, half, top_ref, bottom_ref)
-    left_ref[:half, :], right_ref[:half, :] = column_lines(plane, half)
-    for n, (line, side) in enumerate(((top_ref, left_ref), (bottom_ref, right_ref))):
-        line[half:PLANES, :] = uv_edge_ref[n * half : (n + 1) * half, :]
-        line[PLANES:, :] = frame_ref[n * FRAME : (n + 1) * FRAME, :]
-        side[half:PLANES, :] = uv_edge_ref[PLANES:, n * CA : (n + 1) * CA]
-        side[PLANES:, :] = frame_ref[2 * FRAME :, n * CA : (n + 1) * CA]
+    at = 3 * FRAME
+    lines, sides = [], []
+    columns = column_lines(plane, half)
+    for n in range(2):
+        rows = pl.ds((CA - 8) * n, 8)
+        edge = [plane(p, rows, pl.ds(0, CB))[7 * n : 7 * n + 1] for p in range(half)]
+        lines.append(jnp.concatenate(edge + [frame_ref[at + n * half : at + (n + 1) * half, :], frame_ref[n * FRAME : (n + 1) * FRAME, :]], axis=0))
+        lanes = slice(n * CA, (n + 1) * CA)
+        sides.append(jnp.concatenate([columns[n], frame_ref[at + PLANES :, lanes], frame_ref[2 * FRAME : 3 * FRAME, lanes]], axis=0))
+    for axis, (first, final), even_ref, odd_ref in (("tx", lines, top_ref, bottom_ref), ("ty", sides, left_ref, right_ref)):
+        odd = lax.rem(lax.axis_index(axis), 2) == 1
+        even_ref[...] = jnp.where(odd, first, final)
+        odd_ref[...] = jnp.where(odd, final, first)
 
 
 EDGES = (jax.ShapeDtypeStruct((PLANES + FRAME, CB), jnp.float32),) * 2 + (jax.ShapeDtypeStruct((PLANES + FRAME, CA), jnp.float32),) * 2
 
 
-def first_records(lists, still, frame, uv_edges):
-    ts, *edges = pl.pallas_call(
+def first_records(got, still, frame):
+    out = pl.pallas_call(
         first_records_kernel,
-        out_shape=(HALF,) + EDGES,
-        in_specs=[WHOLE] * 3 + [pl.BlockSpec(memory_space=pltpu.SMEM)] + [WHOLE] * 3,
-        out_specs=[WHOLE] * 5,
+        out_shape=(HALF,) + LISTS + (jax.ShapeDtypeStruct((PLANES, 128), jnp.float32),) + EDGES,
+        in_specs=[ANYWHERE] * 3,
+        out_specs=[WHOLE] * 10,
+        scratch_shapes=[
+            pltpu.VMEM(got.shape, jnp.float32),
+            pltpu.VMEM(frame.shape, jnp.float32),
+            pltpu.SMEM((8, 128), jnp.int32),
+            pltpu.SemaphoreType.DMA((4,)),
+        ],
         compiler_params=PARAMS,
         name="first_records",
-    )(*lists, still, frame, uv_edges)
-    return ts, edges
-
-
-def second_records_kernel(part, high_ref, low_ref, cell_ref, edge_ref, *rest):
-    out_ref = rest[-1]
-    out_ref[...] = rest[0][...] if part else jnp.zeros_like(out_ref)
-    spread_step(1, 16 * part, 16 * part + 16, WINDOW, UNROLL, high_ref, low_ref, cell_ref, edge_ref, out_ref)
-
-
-def second_records(lists, part, earlier=()):
+    )(got, still, frame)
+    return out[0], out[1:5], out[5], out[6:]
+
+
+def second_records_kernel(high_ref, low_ref, cell_ref, edge_ref, out_ref):
+    out_ref[...] = jnp.zeros_like(out_ref)
+    spread_step(1, 0, 32, WINDOW, UNROLL, high_ref, low_ref, cell_ref, edge_ref, out_ref)
+
+
+def second_records(lists):
     return pl.pallas_call(
-        functools.partial(second_records_kernel, part),
-        out_shape=jax.ShapeDtypeStruct((PLANES // 2, CA, CB), jnp.float32),
-        in_specs=[WHOLE] * 3 + [pl.BlockSpec(memory_space=pltpu.SMEM)] + [WHOLE] * len(earlier),
+        second_records_kernel,
+        out_shape=HALF,
+        in_specs=[WHOLE] * 3 + [pl.BlockSpec(memory_space=pltpu.SMEM)],
         out_specs=WHOLE,
-        input_output_aliases={4: 0} if earlier else {},
         compiler_params=PARAMS,
         name="second_records",
-    )(*lists, *earlier)
+    )(*lists)
 
 
 def local(adjoint_start, mixing_h, mixing_v, courant, coriolis, misfit, owner, column):
@@ -590,16 +588,14 @@
     coefficients = (mixing_h, mixing_v, courant, coriolis)
     sent = pack(owner.transpose(0, 2, 1), column, misfit, state, devices)
     got = lax.all_to_all(sent.reshape(devices, 1, WIRE * 128), ("tx", "ty"), split_axis=0, concat_axis=0, tiled=True)
-    still, uv, frame, uv_edges = first_step(state, coefficients)
-    lists, corners = order(got.reshape(devices * WIRE, 128))
-    ts, (top, bottom, left, right) = first_records(lists, still, frame, uv_edges)
-    before, after_ = moved(bottom, "tx", True), moved(top, "tx", False)
-    prior = moved(right, "ty", True)
-    forcing = second_records(lists, 0)
-    left, forcing = after(left, forcing)
-    next_ = moved(left, "ty", False)
-    forcing = second_records(lists, 1, (forcing,))
-    return last_step(ts, uv, coefficients, (before, after_, prior, next_), frame, corners, forcing).reshape(FIELDS, LEV, CA, CB)
+    still, uv, frame = first_step(state, coefficients)
+    ts, lists, corners, edges = first_records(got.reshape(devices * WIRE, 128), still, frame)
+    x0 = swapped(edges[0], "tx", 0)
+    x1 = swapped(edges[1], "tx", 1)
+    y0 = swapped(edges[2], "ty", 0)
+    y1 = swapped(edges[3], "ty", 1)
+    forcing = second_records(lists)
+    return last_step(ts, uv, coefficients, (x0, x1, y0, y1), frame, corners, forcing).reshape(FIELDS, LEV, CA, CB)
 
 
 def solution(mesh):

time: 64.2 us -> 57.2 us (0.89)
  starting transfers between devices: 19.5 us -> 14.1 us
  Pallas kernels: 33.5 us -> 32.1 us
  waiting for transfers between devices: 7.74 us -> 8.55 us
  local copies, waits for them, and re-layouts: 2.87 us -> 2.15 us
    ppermute x4, starting transfers between devices: 8.38 us -> 2.92 us  [swapped(): return lax.ppermute(x, axis, pairs + [(j, i) for i, j in pairs])]
    unnamed x18 -> x16, local copies, waits for them, and re-layouts: 2.87 us -> 2.15 us
    pallas_call x4 -> x2, Pallas kernels: 14.2 us -> 13.6 us  [the longest x1 8.24 us: first_records(): pl.pallas_call(first_records_kernel, out_shape=(HALF,) + LISTS + (jax.Sha...]
  transfers between devices with their start and end apart: 5 -> 5, of which waited for: 1 -> 2; matrix products, arithmetic and copies ran while one was open for 0% -> 0% of each run, Pallas kernels for 21% -> 21%
where the time goes in v4:
time: 57.2 us; the launch traced here: 57 us
  Pallas kernels  32.1 us (56%)
  starting transfers between devices  14.1 us (25%)
  waiting for transfers between devices  8.55 us (15%)
  local copies, waits for them, and re-layouts  2.15 us (4%)
    all_to_all x1, starting transfers between devices, local(): lax.all_to_all(sent.reshape(devices, 1, WIRE * 128), ('tx', 'ty'), split_...  11.1 us
    pallas_call x1, Pallas kernels, first_records(): pl.pallas_call(first_records_kernel, out_shape=(HALF,) + LISTS + (jax.Sha...  8.24 us
    all_to_all x1, waiting for transfers between devices, local(): lax.all_to_all(sent.reshape(devices, 1, WIRE * 128), ('tx', 'ty'), split_...  8 us
    pallas_call x1, Pallas kernels, first_step(): pl.pallas_call(functools.partial(step_kernel, False), out_shape=(HALF, HA...  6.91 us
    pallas_call x1, Pallas kernels, pack(): pl.pallas_call(functools.partial(pack_kernel, devices, span), out_shape=s...  6.85 us
    pallas_call x1, Pallas kernels, second_records(): pl.pallas_call(second_records_kernel, out_shape=HALF, in_specs=[WHOLE] *...  5.33 us
    pallas_call x1, Pallas kernels, last_step(): pl.pallas_call(functools.partial(step_kernel, True), out_shape=jax.ShapeD...  4.76 us
    ppermute x4, starting transfers between devices, swapped(): return lax.ppermute(x, axis, pairs + [(j, i) for i, j in pairs])  2.92 us
  transfers between devices with their start and end apart: 5, of which 2 were waited for; matrix products, arithmetic and copies ran while one was open for 0% of the time, Pallas kernels for 21%

profile of v4, /device:TPU:0, one launch (start us, length us, event | category | flops | bytes accessed | tf_op | source)
XLA Modules:
  0.0 57.0 jit_solution(1289803989145552554)
XLA Ops:
  0.0 6.8 %pack.1 = f32[1280,128]{1,0:T(8,128)} custom-call(s32[2,1,4096]{2,1,0:T(1,128)} %bitcast.9, s32[2,4096]{1,0:T(2,128)} %column_any.1, f32[2,8,4096]{2,1,0:T(8,128)} %misfit_any.1, f32[16,128,256]{2,1,0:T(8,128)} %bitcast.6), custom_call_target="tpu_custom_call" | custom-call | tf_op jit(solution)/shard_map/pack/pallas_call | solution.py:116
  6.9 11.1 %all-to-all-start = ((f32[128,1,1280]{2,1,0:T(1,128)}), f32[128,1,1280]{2,1,0:T(1,128)S(1)}, u32[]{:S(2)}, u32[]{:S(2)}) async-start(f32[128,1,1280]{2,1,0:T(1,128)} %bitcast.8), calls=%async_computation | async-start | bytes 1310720 | tf_op jit(solution)/shard_map/all_to_all | solution.py:590
  18.0 0.0 copy-start.5
  18.0 6.9 %first_step.1 = (f32[8,128,256]{2,1,0:T(8,128)}, f32[8,128,256]{2,1,0:T(8,128)}, f32[96,256]{1,0:T(8,128)}) custom-call(f32[16,128,256]{2,1,0:T(8,128)} %bitcast.7, f32[4,128,256]{2,1,0:T(8,128)} %refs_2_.3, f32[3,128,256]{2,1,0:T(8,128)} %refs_3_.3, f32[2,4,128,256]{3,2,1,0:T(8,128)} %refs_4_.3, f32[128,256]{1,0:T(8,128)} %refs_5_.1), custom_call_target="tpu_custom_call" | custom-call | tf_op jit(solution)/shard_map/first_step/pallas_call | solution.py:464
  24.9 0.0 copy-start
  25.0 0.0 copy-start.1
  25.0 0.0 copy-start.2
  25.0 8.0 %all-to-all-done = f32[128,1,1280]{2,1,0:T(1,128)S(1)} async-done(((f32[128,1,1280]{2,1,0:T(1,128)}), f32[128,1,1280]{2,1,0:T(1,128)S(1)}, u32[]{:S(2)}, u32[]{:S(2)}) %all-to-all-start) | async-done | bytes 655392 | tf_op jit(solution)/shard_map/all_to_all | solution.py:590
  33.0 0.0 copy-start.3
  33.0 1.2 %copy-done.3 = f32[8,128,256]{2,1,0:T(8,128)S(1)} copy-done((f32[8,128,256]{2,1,0:T(8,128)S(1)}, f32[8,128,256]{2,1,0:T(8,128)}, u32[]{:S(2)}) %copy-start.3) | copy-done | bytes 1048600
  34.2 0.0 copy-start.6
  34.2 0.9 %copy-done.6 = f32[96,256]{1,0:T(8,128)S(1)} copy-done((f32[96,256]{1,0:T(8,128)S(1)}, f32[96,256]{1,0:T(8,128)}, u32[]{:S(2)}) %copy-start.6) | copy-done | bytes 98328
  35.1 0.0 copy-start.4
  35.1 0.0 copy-start.7
  35.1 8.2 %first_records.1 = (f32[8,128,256]{2,1,0:T(8,128)S(1)}, f32[2,8,32,256]{3,2,1,0:T(8,128)S(1)}, f32[2,8,32,256]{3,2,1,0:T(8,128)S(1)}, f32[2,1,32,256]{3,2,1,0:T(...) custom-call(f32[1280,128]{1,0:T(8,128)S(1)} %bitcast.5, ...), custom_call_target="tpu_custom_call" | custom-call | tf_op jit(solution)/shard_map/first_records/pallas_call | solution.py:552
  43.4 0.1 collective-permute-start
  43.4 1.0 %collective-permute-start.1 = (f32[40,256]{1,0:T(8,128)S(1)}, f32[40,256]{1,0:T(8,128)S(1)}, u32[]{:S(2)}, u32[]{:S(2)}) collective-permute-start(f32[40,256]{1,0:T(8,128)S(1)} %get-tuple-element.23), channel_id=1, source_target_pairs={{16,32},{48,64},{80,96},{112,0},{32,16},{64,48},{96,80},{0,112},{1... | collective-permute-start | bytes 122888 | tf_op jit(solution)/shard_map/ppermute | solution.py:287
  44.4 0.7 %collective-permute-start.2 = (f32[40,128]{1,0:T(8,128)S(1)}, f32[40,128]{1,0:T(8,128)S(1)}, u32[]{:S(2)}, u32[]{:S(2)}) collective-permute-start(f32[40,128]{1,0:T(8,128)S(1)} %get-tuple-element.24), channel_id=1, source_target_pairs={{0,1},{2,3},{4,5},{6,7},{8,9},{10,11},{12,13},{14,15},{1,0},{3,2},... | collective-permute-start | bytes 61448 | tf_op jit(solution)/shard_map/ppermute | solution.py:287
  45.1 1.2 %collective-permute-start.3 = (f32[40,128]{1,0:T(8,128)S(1)}, f32[40,128]{1,0:T(8,128)S(1)}, u32[]{:S(2)}, u32[]{:S(2)}) collective-permute-start(f32[40,128]{1,0:T(8,128)S(1)} %get-tuple-element.25), channel_id=1, source_target_pairs={{1,2},{3,4},{5,6},{7,8},{9,10},{11,12},{13,14},{15,0},{2,1},{4,3},... | collective-permute-start | bytes 61448 | tf_op jit(solution)/shard_map/ppermute | solution.py:287
  46.3 5.3 %second_records.1.refs_12_ = f32[8,128,256]{2,1,0:T(8,128)S(1)} custom-call(f32[2,8,32,256]{3,2,1,0:T(8,128)S(1)} %get-tuple-element.27.high_ref, f32[2,8,32,256]{3,2,1,0:T(8,128)S(1)} %get-tuple-element.28.low_ref, f32[2,1,32,256]{3,2,1,0:T(8,128)S(1)} %get-tuple-element.29.cell_ref, s32[8,128]{1,0:T(8,128)S(1)} %get-tuple-element.30.edge_ref), custom_call_target="tpu_custom_call" | custom-call | tf_op jit(solution)/shard_map/second_records/pallas_call | solution.py:575
  51.6 0.0 collective-permute-done.2.refs_8_
  51.6 0.5 collective-permute-done.3.refs_9_
  52.2 0.0 collective-permute-done.refs_6_
  52.2 0.0 collective-permute-done.1.refs_7_
  52.2 0.0 copy-done.5
  52.2 0.0 copy-done
  52.2 0.0 copy-done.1
  52.2 0.0 copy-done.2
  52.2 0.0 copy-done.4
  52.2 0.0 copy-done.7
  52.2 4.8 %last_step.1 = f32[16,128,256]{2,1,0:T(8,128)} custom-call(f32[8,128,256]{2,1,0:T(8,128)S(1)} %get-tuple-element.20.refs_0_, f32[8,128,256]{2,1,0:T(8,128)S(1)} %copy-done.4, f32[4,128,256]{2,1,0:T(8,128)S(1)} %copy-done.1, f32[3,128,256]{2,1,0:T(8,128)S(1)} %copy-done.2, f32[2,4,128,256]{3,2,1,0:T(8,128)S(1)} %copy-done, f32[128,256]{1,0:T(8,128)S(1)} %copy-done.5, ...), custom_call_target="tpu_custom_call" | custom-call | tf_op jit(solution)/shard_map/last_step/pallas_call | solution.py:478
Async XLA Ops:
  6.9 26.1 %all-to-all-start = ((f32[128,1,1280]{2,1,0:T(1,128)}), f32[128,1,1280]{2,1,0:T(1,128)S(1)}, u32[]{:S(2)}, u32[]{:S(2)}) async-start(f32[128,1,1280]{2,1,0:T(1,128)} %bitcast.8), calls=%async_computation | async-start | bytes 1310720 | tf_op jit(solution)/shard_map/all_to_all | solution.py:590
  18.0 34.2 %copy-start.5 = (f32[128,256]{1,0:T(8,128)S(1)}, f32[128,256]{1,0:T(8,128)}, u32[]{:S(2)}) copy-start(f32[128,256]{1,0:T(8,128)} %refs_5_.1) | copy-start | bytes 393220
  24.9 27.3 %copy-start = (f32[2,4,128,256]{3,2,1,0:T(8,128)S(1)}, f32[2,4,128,256]{3,2,1,0:T(8,128)}, u32[]{:S(2)}) copy-start(f32[2,4,128,256]{3,2,1,0:T(8,128)} %refs_4_.3) | copy-start | bytes 3145732
  25.0 27.2 %copy-start.1 = (f32[4,128,256]{2,1,0:T(8,128)S(1)}, f32[4,128,256]{2,1,0:T(8,128)}, u32[]{:S(2)}) copy-start(f32[4,128,256]{2,1,0:T(8,128)} %refs_2_.3) | copy-start | bytes 1572868
  25.0 27.2 %copy-start.2 = (f32[3,128,256]{2,1,0:T(8,128)S(1)}, f32[3,128,256]{2,1,0:T(8,128)}, u32[]{:S(2)}) copy-start(f32[3,128,256]{2,1,0:T(8,128)} %refs_3_.3) | copy-start | bytes 1179652
  33.0 1.2 %copy-start.3 = (f32[8,128,256]{2,1,0:T(8,128)S(1)}, f32[8,128,256]{2,1,0:T(8,128)}, u32[]{:S(2)}) copy-start(f32[8,128,256]{2,1,0:T(8,128)} %get-tuple-element.18.still_any) | copy-start | bytes 3145732
  34.2 0.9 %copy-start.6 = (f32[96,256]{1,0:T(8,128)S(1)}, f32[96,256]{1,0:T(8,128)}, u32[]{:S(2)}) copy-start(f32[96,256]{1,0:T(8,128)} %get-tuple-element.19.frame_any.refs_10_) | copy-start | bytes 294916
  35.1 17.1 %copy-start.4 = (f32[8,128,256]{2,1,0:T(8,128)S(1)}, f32[8,128,256]{2,1,0:T(8,128)}, u32[]{:S(2)}) copy-start(f32[8,128,256]{2,1,0:T(8,128)} %get-tuple-element.21.refs_1_) | copy-start | bytes 3145732
  35.1 17.1 %copy-start.7 = (f32[96,256]{1,0:T(8,128)S(1)}, f32[96,256]{1,0:T(8,128)}, u32[]{:S(2)}) copy-start(f32[96,256]{1,0:T(8,128)} %get-tuple-element.19.frame_any.refs_10_) | copy-start | bytes 294916
  43.4 8.8 %collective-permute-start = (f32[40,256]{1,0:T(8,128)S(1)}, f32[40,256]{1,0:T(8,128)S(1)}, u32[]{:S(2)}, u32[]{:S(2)}) collective-permute-start(f32[40,256]{1,0:T(8,128)S(1)} %get-tuple-element.22), channel_id=1, source_target_pairs={{0,16},{32,48},{64,80},{96,112},{16,0},{48,32},{80,64},{112,96},{1... | collective-permute-start | bytes 122888 | tf_op jit(solution)/shard_map/ppermute | solution.py:287
  43.4 8.7 %collective-permute-start.1 = (f32[40,256]{1,0:T(8,128)S(1)}, f32[40,256]{1,0:T(8,128)S(1)}, u32[]{:S(2)}, u32[]{:S(2)}) collective-permute-start(f32[40,256]{1,0:T(8,128)S(1)} %get-tuple-element.23), channel_id=1, source_target_pairs={{16,32},{48,64},{80,96},{112,0},{32,16},{64,48},{96,80},{0,112},{1... | collective-permute-start | bytes 122888 | tf_op jit(solution)/shard_map/ppermute | solution.py:287
  44.4 7.2 %collective-permute-start.2 = (f32[40,128]{1,0:T(8,128)S(1)}, f32[40,128]{1,0:T(8,128)S(1)}, u32[]{:S(2)}, u32[]{:S(2)}) collective-permute-start(f32[40,128]{1,0:T(8,128)S(1)} %get-tuple-element.24), channel_id=1, source_target_pairs={{0,1},{2,3},{4,5},{6,7},{8,9},{10,11},{12,13},{14,15},{1,0},{3,2},... | collective-permute-start | bytes 61448 | tf_op jit(solution)/shard_map/ppermute | solution.py:287
  45.1 7.1 %collective-permute-start.3 = (f32[40,128]{1,0:T(8,128)S(1)}, f32[40,128]{1,0:T(8,128)S(1)}, u32[]{:S(2)}, u32[]{:S(2)}) collective-permute-start(f32[40,128]{1,0:T(8,128)S(1)} %get-tuple-element.25), channel_id=1, source_target_pairs={{1,2},{3,4},{5,6},{7,8},{9,10},{11,12},{13,14},{15,0},{2,1},{4,3},... | collective-permute-start | bytes 61448 | tf_op jit(solution)/shard_map/ppermute | solution.py:287

commit v5 on v4

--- a/solution.py
+++ b/solution.py
@@ -111,7 +111,7 @@
     store.wait()
 
 
-def pack(owner, column, misfit, state, devices, span=1024):
+def pack(owner, column, misfit, state, devices, span=2048):
     sent = jax.ShapeDtypeStruct((devices * WIRE, 128), jnp.float32)
     return pl.pallas_call(
         functools.partial(pack_kernel, devices, span),
@@ -133,47 +133,55 @@
     )(owner, column, misfit, state)
 
 
-def exchange(keys, span, reach):
+def exchange(keys, span, reach, flip=None):
     sub = lax.broadcasted_iota(jnp.int32, (8, 128), 0)
     count = len(keys)
     keys = list(keys)
+    if span < 8 * count:
+        flip = (sub & (span // count)) != 0 if span >= count else None
     if reach < count:
         for v in range(count):
             w = v ^ reach
             if v > w:
                 continue
             low, high = jnp.minimum(keys[v], keys[w]), jnp.maximum(keys[v], keys[w])
-            if span < count:
-                keys[v], keys[w] = (high, low) if v & span else (low, high)
-            elif span < 8 * count:
-                down = (sub & (span // count)) != 0
-                keys[v], keys[w] = jnp.where(down, high, low), jnp.where(down, low, high)
-            else:
-                keys[v], keys[w] = low, high
+            if flip is not None:
+                low, high = jnp.where(flip, high, low), jnp.where(flip, low, high)
+            elif span < count and v & span:
+                low, high = high, low
+            keys[v], keys[w] = low, high
         return keys
     step = reach // count
-    upper = (sub & step) != 0
-    if span < 8 * count:
-        upper = upper != ((sub & (span // count)) != 0)
+    second = (sub & step) != 0
+    upper = second if flip is None else second != flip
     for v in range(count):
-        other = jnp.where((sub & step) != 0, pltpu.roll(keys[v], step, 0), pltpu.roll(keys[v], 8 - step, 0))
+        other = jnp.where(second, pltpu.roll(keys[v], step, 0), pltpu.roll(keys[v], 8 - step, 0))
         keys[v] = jnp.where(upper, jnp.maximum(keys[v], other), jnp.minimum(keys[v], other))
     return keys
 
 
 def sort_rows(keys):
+    length = 8 * len(keys)
+    beyond = (lax.broadcasted_iota(jnp.int32, (8, 128), 1) & 32) != 0
     span = 2
-    while span <= 8 * len(keys):
+    while span <= length:
         reach = span // 2
         while reach:
-            keys = exchange(keys, span, reach)
+            keys = exchange(keys, span, reach, beyond)
             reach //= 2
         span *= 2
+    other = [jnp.where(beyond, pltpu.roll(x, 32, 1), pltpu.roll(x, 96, 1)) for x in keys]
+    keys = [jnp.where(beyond, jnp.maximum(x, y), jnp.minimum(x, y)) for x, y in zip(keys, other)]
+    reach = length // 2
+    while reach:
+        keys = exchange(keys, length, reach)
+        reach //= 2
     return keys
 
 
 def order_kernel(got_ref, high_ref, low_ref, cell_ref):
     lanes = lax.broadcasted_iota(jnp.int32, (128, 128), 1)
+    rows = lax.broadcasted_iota(jnp.int32, (128, 128), 0)
     left = lanes < CAP
 
     def list_of(k):
@@ -187,38 +195,55 @@
     slot = lanes & (CAP - 1)
     spread = ((slot & 1) << 5) | ((slot & 2) << 3) | ((slot & 4) << 1) | ((slot & 8) >> 1) | ((slot & 16) >> 3) | ((slot & 32) >> 5)
     idle = ((spread << 1) | (lanes >> 6)) << 8
-    key = (jnp.where(ids > 0, ids - 1, idle) << 7) | lanes
+    key = (jnp.where(ids > 0, ids - 1, idle) << 8) | ((rows & 32) << 2) | lanes
     turned = key.astype(jnp.float32).T
     keys = sort_rows([turned[8 * v : 8 * v + 8] for v in range(16)])
     keys = jnp.concatenate(keys, axis=0).astype(jnp.int32)
-    source = (keys & 127).astype(jnp.float32).T.astype(jnp.int32)
-
-    def place(ref, k, x):
-        for v in range(0, 16, 2):
-            a, b = x[8 * v : 8 * v + 8], x[8 * v + 8 : 8 * v + 16]
-            g, h = v // 4, (v // 2) % 2
-            l8 = left[:8]
-            ref[0, k, pl.ds(8 * g, 8), pl.ds(128 * h, 128)] = jnp.where(l8, a, pltpu.roll(b, CAP, 1))
-            ref[1, k, pl.ds(8 * g, 8), pl.ds(128 * h, 128)] = jnp.where(l8, pltpu.roll(a, CAP, 1), b)
-
-    place(cell_ref, 0, (keys >> 7).astype(jnp.float32))
+    source = (keys & 255).astype(jnp.float32).T.astype(jnp.int32)
+    lane_of, beyond = source & 127, source >= 128
+    block = lanes[:8] >> 5
+
+    def place(x, store):
+        for h in range(2):
+            for u in range(2):
+                parts = [x[8 * v : 8 * v + 8] for v in range(8 * h + 4 * u, 8 * h + 4 * u + 4)]
+                for group in range(4):
+                    moved = [part if j == group else pltpu.roll(part, (j - group) % 4 * 32, 1) for j, part in enumerate(parts)]
+                    tile = jnp.where(block < 2, jnp.where(block == 0, moved[0], moved[1]), jnp.where(block == 2, moved[2], moved[3]))
+                    store(group // 2, pl.ds(16 * (group % 2) + 8 * h, 8), pl.ds(128 * u, 128), tile)
+
+    def store_cell(t, at, cols, tile):
+        cell_ref[t, 0, at, cols] = tile
+
+    place((keys >> 8).astype(jnp.float32), store_cell)
     for k in range(VALS):
-        moved = jnp.take_along_axis(list_of(k), source, axis=1).T
-        top = moved.astype(BF).astype(jnp.float32)
-        place(high_ref, k, top)
-        place(low_ref, k, moved - top)
+        x = list_of(k)
+        near = jnp.concatenate([x[:32], x[:32], x[64:96], x[64:96]], axis=0)
+        far = jnp.concatenate([x[32:64], x[32:64], x[96:], x[96:]], axis=0)
+        picked = jnp.where(beyond, jnp.take_along_axis(far, lane_of, axis=1), jnp.take_along_axis(near, lane_of, axis=1))
+
+        def store_value(t, at, cols, tile, k=k):
+            top = tile.astype(BF).astype(jnp.float32)
+            high_ref[t, k, at, cols] = top
+            low_ref[t, k, at, cols] = tile - top
+
+        place(picked.T, store_value)
 
 
 def bounds_of(cell_ref, edge_ref):
     chunk = lax.broadcasted_iota(jnp.int32, (32, 128), 0)
     lane = lax.broadcasted_iota(jnp.int32, (32, 128), 1)
-    lines = []
+    lines, beyond = [], []
     for t in range(STEPS):
         row = cell_ref[t, 0].astype(jnp.int32) >> 8
         least = jnp.min(jnp.minimum(row[:, :128], row[:, 128:]).astype(jnp.float32), axis=1, keepdims=True)
         most = jnp.max(jnp.maximum(row[:, :128], row[:, 128:]).astype(jnp.float32), axis=1, keepdims=True)
         lines += [jnp.sum(jnp.where(chunk == lane, e, 0.0), axis=0, keepdims=True) for e in (least, most)]
-    edge_ref[...] = jnp.concatenate(lines + [jnp.zeros((4, 128), jnp.float32)], axis=0).astype(jnp.int32)
+        base = jnp.minimum((least.astype(jnp.int32) >> 3) << 3, CA - WINDOW)
+        over = jnp.max((most.astype(jnp.int32) >= base + WINDOW).astype(jnp.float32), axis=0, keepdims=True)
+        beyond.append(jnp.broadcast_to(over, (1, 128)))
+    spare = jnp.zeros((8 - 3 * STEPS, 128), jnp.float32)
+    edge_ref[...] = jnp.concatenate(lines + beyond + [spare], axis=0).astype(jnp.int32)
 
 
 def products(t, i, base, window, keep, high_ref, low_ref, cell_ref):
@@ -262,7 +287,8 @@
         lax.while_loop(lambda start: start <= edge_ref[2 * t + 1, i], more, first(i) + window)
         return carry
 
-    lax.fori_loop(chunks_from, chunks_to, rest, 0)
+    last = jnp.where(edge_ref[2 * STEPS + t, 0] > 0, chunks_to, chunks_from)
+    lax.fori_loop(chunks_from, last, rest, 0)
 
 
 def row_lines(plane, count, top_ref, bottom_ref):
@@ -438,7 +464,7 @@
             store.wait()
         return carry
 
-    lax.fori_loop(0, CA // 8, strip, 0, unroll=2)
+    lax.fori_loop(0, CA // 8, strip, 0, unroll=4)
     if not last:
 
         def plane(p, rows, cols):
@@ -492,7 +518,7 @@
     jax.ShapeDtypeStruct((STEPS, 1, 32, CHUNK), jnp.float32),
     jax.ShapeDtypeStruct((8, 128), jnp.int32),
 )
-WINDOW, UNROLL = 40, 8
+WINDOW, UNROLL = 32, 16
 
 
 def corner_columns(got_ref):
@@ -510,18 +536,17 @@
     return out
 
 
-def first_records_kernel(got_any, still_any, frame_any, ts_ref, high_ref, low_ref, cell_ref, edge_ref, corner_ref, top_ref, bottom_ref, left_ref, right_ref, got_ref, frame_ref, smem_ref, sem):
-    pairs = (got_any, got_ref), (still_any, ts_ref), (frame_any, frame_ref)
+def first_records_kernel(got_ref, still_any, frame_any, ts_ref, high_ref, low_ref, cell_ref, edge_ref, corner_ref, top_ref, bottom_ref, left_ref, right_ref, frame_ref, smem_ref, sem):
+    pairs = (still_any, ts_ref), (frame_any, frame_ref)
     loads = [pltpu.make_async_copy(x, y, sem.at[n]) for n, (x, y) in enumerate(pairs)]
     for load in loads:
         load.start()
-    loads[0].wait()
     order_kernel(got_ref, high_ref, low_ref, cell_ref)
     bounds_of(cell_ref, edge_ref)
-    copy = pltpu.make_async_copy(edge_ref, smem_ref, sem.at[3])
+    copy = pltpu.make_async_copy(edge_ref, smem_ref, sem.at[2])
     copy.start()
     corner_ref[...] = corner_columns(got_ref)
-    for load in loads[1:]:
+    for load in loads:
         load.wait()
     copy.wait()
     half = PLANES // 2
@@ -552,13 +577,12 @@
     out = pl.pallas_call(
         first_records_kernel,
         out_shape=(HALF,) + LISTS + (jax.ShapeDtypeStruct((PLANES, 128), jnp.float32),) + EDGES,
-        in_specs=[ANYWHERE] * 3,
+        in_specs=[WHOLE, ANYWHERE, ANYWHERE],
         out_specs=[WHOLE] * 10,
         scratch_shapes=[
-            pltpu.VMEM(got.shape, jnp.float32),
             pltpu.VMEM(frame.shape, jnp.float32),
             pltpu.SMEM((8, 128), jnp.int32),
-            pltpu.SemaphoreType.DMA((4,)),
+            pltpu.SemaphoreType.DMA((3,)),
         ],
         compiler_params=PARAMS,
         name="first_records",

time: 57.2 us -> 55.6 us (0.972)
  Pallas kernels: 32.1 us -> 28.1 us
  waiting for transfers between devices: 8.55 us -> 10.5 us
    pallas_call x1, Pallas kernels: 5.33 us -> 3.51 us  [second_records(): pl.pallas_call(second_records_kernel, out_shape=HALF, in_specs=[WHOLE] *...]
    ppermute x4, waiting for transfers between devices: 0.55 us -> 2.35 us  [swapped(): return lax.ppermute(x, axis, pairs + [(j, i) for i, j in pairs])]
    pallas_call x1, Pallas kernels: 8.24 us -> 6.94 us  [first_records(): pl.pallas_call(first_records_kernel, out_shape=(HALF,) + LISTS + (jax.Sha...]
  transfers between devices with their start and end apart: 5 -> 5, of which waited for: 2 -> 2; matrix products, arithmetic and copies ran while one was open for 0% -> 0% of each run, Pallas kernels for 21% -> 19%
where the time goes in v5:
time: 55.6 us; the launch traced here: 55.1 us
  Pallas kernels  28.1 us (51%)
  starting transfers between devices  14.1 us (25%)
  waiting for transfers between devices  10.5 us (19%)
  local copies, waits for them, and re-layouts  2.15 us (4%)
    all_to_all x1, starting transfers between devices, local(): lax.all_to_all(sent.reshape(devices, 1, WIRE * 128), ('tx', 'ty'), split_...  11.1 us
    all_to_all x1, waiting for transfers between devices, local(): lax.all_to_all(sent.reshape(devices, 1, WIRE * 128), ('tx', 'ty'), split_...  8.16 us
    pallas_call x1, Pallas kernels, first_records(): pl.pallas_call(first_records_kernel, out_shape=(HALF,) + LISTS + (jax.Sha...  6.94 us
    pallas_call x1, Pallas kernels, first_step(): pl.pallas_call(functools.partial(step_kernel, False), out_shape=(HALF, HA...  6.75 us
    pallas_call x1, Pallas kernels, pack(): pl.pallas_call(functools.partial(pack_kernel, devices, span), out_shape=s...  6.3 us
    pallas_call x1, Pallas kernels, last_step(): pl.pallas_call(functools.partial(step_kernel, True), out_shape=jax.ShapeD...  4.57 us
    pallas_call x1, Pallas kernels, second_records(): pl.pallas_call(second_records_kernel, out_shape=HALF, in_specs=[WHOLE] *...  3.51 us
    ppermute x4, starting transfers between devices, swapped(): return lax.ppermute(x, axis, pairs + [(j, i) for i, j in pairs])  2.96 us
  transfers between devices with their start and end apart: 5, of which 2 were waited for; matrix products, arithmetic and copies ran while one was open for 0% of the time, Pallas kernels for 19%

profile of v5, /device:TPU:0, one launch (start us, length us, event | category | flops | bytes accessed | tf_op | source)
XLA Modules:
  0.0 55.1 jit_solution(10276255474750241258)
XLA Ops:
  0.0 6.3 %pack.1 = f32[1280,128]{1,0:T(8,128)} custom-call(s32[2,1,4096]{2,1,0:T(1,128)} %bitcast.9, s32[2,4096]{1,0:T(2,128)} %column_any.1, f32[2,8,4096]{2,1,0:T(8,128)} %misfit_any.1, f32[16,128,256]{2,1,0:T(8,128)} %bitcast.6), custom_call_target="tpu_custom_call" | custom-call | tf_op jit(solution)/shard_map/pack/pallas_call | solution.py:116
  6.3 11.1 %all-to-all-start = ((f32[128,1,1280]{2,1,0:T(1,128)}), f32[128,1,1280]{2,1,0:T(1,128)S(1)}, u32[]{:S(2)}, u32[]{:S(2)}) async-start(f32[128,1,1280]{2,1,0:T(1,128)} %bitcast.8), calls=%async_computation | async-start | bytes 1310720 | tf_op jit(solution)/shard_map/all_to_all | solution.py:614
  17.5 0.0 copy-start.5
  17.5 6.8 %first_step.1 = (f32[8,128,256]{2,1,0:T(8,128)}, f32[8,128,256]{2,1,0:T(8,128)}, f32[96,256]{1,0:T(8,128)}) custom-call(f32[16,128,256]{2,1,0:T(8,128)} %bitcast.7, f32[4,128,256]{2,1,0:T(8,128)} %refs_2_.3, f32[3,128,256]{2,1,0:T(8,128)} %refs_3_.3, f32[2,4,128,256]{3,2,1,0:T(8,128)} %refs_4_.3, f32[128,256]{1,0:T(8,128)} %refs_5_.1), custom_call_target="tpu_custom_call" | custom-call | tf_op jit(solution)/shard_map/first_step/pallas_call | solution.py:490
  24.2 0.0 copy-start
  24.3 0.0 copy-start.1
  24.3 0.0 copy-start.2
  24.3 8.2 %all-to-all-done = f32[128,1,1280]{2,1,0:T(1,128)S(1)} async-done(((f32[128,1,1280]{2,1,0:T(1,128)}), f32[128,1,1280]{2,1,0:T(1,128)S(1)}, u32[]{:S(2)}, u32[]{:S(2)}) %all-to-all-start) | async-done | bytes 655392 | tf_op jit(solution)/shard_map/all_to_all | solution.py:614
  32.4 0.0 copy-start.3
  32.4 1.2 %copy-done.3 = f32[8,128,256]{2,1,0:T(8,128)S(1)} copy-done((f32[8,128,256]{2,1,0:T(8,128)S(1)}, f32[8,128,256]{2,1,0:T(8,128)}, u32[]{:S(2)}) %copy-start.3) | copy-done | bytes 1048600
  33.7 0.0 copy-start.6
  33.7 0.9 %copy-done.6 = f32[96,256]{1,0:T(8,128)S(1)} copy-done((f32[96,256]{1,0:T(8,128)S(1)}, f32[96,256]{1,0:T(8,128)}, u32[]{:S(2)}) %copy-start.6) | copy-done | bytes 98328
  34.6 0.0 copy-start.4
  34.6 0.0 copy-start.7
  34.6 6.9 %first_records.1 = (f32[8,128,256]{2,1,0:T(8,128)S(1)}, f32[2,8,32,256]{3,2,1,0:T(8,128)S(1)}, f32[2,8,32,256]{3,2,1,0:T(8,128)S(1)}, f32[2,1,32,256]{3,2,1,0:T(...) custom-call(f32[1280,128]{1,0:T(8,128)S(1)} %bitcast.5, ...), custom_call_target="tpu_custom_call" | custom-call | tf_op jit(solution)/shard_map/first_records/pallas_call | solution.py:577
  41.5 0.1 collective-permute-start
  41.6 1.0 %collective-permute-start.1 = (f32[40,256]{1,0:T(8,128)S(1)}, f32[40,256]{1,0:T(8,128)S(1)}, u32[]{:S(2)}, u32[]{:S(2)}) collective-permute-start(f32[40,256]{1,0:T(8,128)S(1)} %get-tuple-element.23), channel_id=1, source_target_pairs={{16,32},{48,64},{80,96},{112,0},{32,16},{64,48},{96,80},{0,112},{1... | collective-permute-start | bytes 122888 | tf_op jit(solution)/shard_map/ppermute | solution.py:313
  42.6 0.6 %collective-permute-start.2 = (f32[40,128]{1,0:T(8,128)S(1)}, f32[40,128]{1,0:T(8,128)S(1)}, u32[]{:S(2)}, u32[]{:S(2)}) collective-permute-start(f32[40,128]{1,0:T(8,128)S(1)} %get-tuple-element.24), channel_id=1, source_target_pairs={{0,1},{2,3},{4,5},{6,7},{8,9},{10,11},{12,13},{14,15},{1,0},{3,2},... | collective-permute-start | bytes 61448 | tf_op jit(solution)/shard_map/ppermute | solution.py:313
  43.2 1.2 %collective-permute-start.3 = (f32[40,128]{1,0:T(8,128)S(1)}, f32[40,128]{1,0:T(8,128)S(1)}, u32[]{:S(2)}, u32[]{:S(2)}) collective-permute-start(f32[40,128]{1,0:T(8,128)S(1)} %get-tuple-element.25), channel_id=1, source_target_pairs={{1,2},{3,4},{5,6},{7,8},{9,10},{11,12},{13,14},{15,0},{2,1},{4,3},... | collective-permute-start | bytes 61448 | tf_op jit(solution)/shard_map/ppermute | solution.py:313
  44.5 3.5 %second_records.1.refs_12_ = f32[8,128,256]{2,1,0:T(8,128)S(1)} custom-call(f32[2,8,32,256]{3,2,1,0:T(8,128)S(1)} %get-tuple-element.27.high_ref, f32[2,8,32,256]{3,2,1,0:T(8,128)S(1)} %get-tuple-element.28.low_ref, f32[2,1,32,256]{3,2,1,0:T(8,128)S(1)} %get-tuple-element.29.cell_ref, s32[8,128]{1,0:T(8,128)S(1)} %get-tuple-element.30.edge_ref), custom_call_target="tpu_custom_call" | custom-call | tf_op jit(solution)/shard_map/second_records/pallas_call | solution.py:599
  48.0 0.0 collective-permute-done.2.refs_8_
  48.0 2.3 %collective-permute-done.3.refs_9_ = f32[40,128]{1,0:T(8,128)S(1)} collective-permute-done((f32[40,128]{1,0:T(8,128)S(1)}, f32[40,128]{1,0:T(8,128)S(1)}, u32[]{:S(2)}, u32[]{:S(2)}) %collective-permute-start.3) | collective-permute-done | bytes 20512 | tf_op jit(solution)/shard_map/ppermute | solution.py:313
  50.3 0.0 collective-permute-done.refs_6_
  50.4 0.0 collective-permute-done.1.refs_7_
  50.4 0.0 copy-done.5
  50.4 0.0 copy-done
  50.4 0.0 copy-done.1
  50.4 0.0 copy-done.2
  50.4 0.0 copy-done.4
  50.4 0.0 copy-done.7
  50.4 4.6 %last_step.1 = f32[16,128,256]{2,1,0:T(8,128)} custom-call(f32[8,128,256]{2,1,0:T(8,128)S(1)} %get-tuple-element.20.refs_0_, f32[8,128,256]{2,1,0:T(8,128)S(1)} %copy-done.4, f32[4,128,256]{2,1,0:T(8,128)S(1)} %copy-done.1, f32[3,128,256]{2,1,0:T(8,128)S(1)} %copy-done.2, f32[2,4,128,256]{3,2,1,0:T(8,128)S(1)} %copy-done, f32[128,256]{1,0:T(8,128)S(1)} %copy-done.5, ...), custom_call_target="tpu_custom_call" | custom-call | tf_op jit(solution)/shard_map/last_step/pallas_call | solution.py:504
Async XLA Ops:
  6.3 26.1 %all-to-all-start = ((f32[128,1,1280]{2,1,0:T(1,128)}), f32[128,1,1280]{2,1,0:T(1,128)S(1)}, u32[]{:S(2)}, u32[]{:S(2)}) async-start(f32[128,1,1280]{2,1,0:T(1,128)} %bitcast.8), calls=%async_computation | async-start | bytes 1310720 | tf_op jit(solution)/shard_map/all_to_all | solution.py:614
  17.5 32.9 %copy-start.5 = (f32[128,256]{1,0:T(8,128)S(1)}, f32[128,256]{1,0:T(8,128)}, u32[]{:S(2)}) copy-start(f32[128,256]{1,0:T(8,128)} %refs_5_.1) | copy-start | bytes 393220
  24.2 26.1 %copy-start = (f32[2,4,128,256]{3,2,1,0:T(8,128)S(1)}, f32[2,4,128,256]{3,2,1,0:T(8,128)}, u32[]{:S(2)}) copy-start(f32[2,4,128,256]{3,2,1,0:T(8,128)} %refs_4_.3) | copy-start | bytes 3145732
  24.3 26.1 %copy-start.1 = (f32[4,128,256]{2,1,0:T(8,128)S(1)}, f32[4,128,256]{2,1,0:T(8,128)}, u32[]{:S(2)}) copy-start(f32[4,128,256]{2,1,0:T(8,128)} %refs_2_.3) | copy-start | bytes 1572868
  24.3 26.1 %copy-start.2 = (f32[3,128,256]{2,1,0:T(8,128)S(1)}, f32[3,128,256]{2,1,0:T(8,128)}, u32[]{:S(2)}) copy-start(f32[3,128,256]{2,1,0:T(8,128)} %refs_3_.3) | copy-start | bytes 1179652
  32.4 1.2 %copy-start.3 = (f32[8,128,256]{2,1,0:T(8,128)S(1)}, f32[8,128,256]{2,1,0:T(8,128)}, u32[]{:S(2)}) copy-start(f32[8,128,256]{2,1,0:T(8,128)} %get-tuple-element.18.still_any) | copy-start | bytes 3145732
  33.7 0.9 %copy-start.6 = (f32[96,256]{1,0:T(8,128)S(1)}, f32[96,256]{1,0:T(8,128)}, u32[]{:S(2)}) copy-start(f32[96,256]{1,0:T(8,128)} %get-tuple-element.19.frame_any.refs_10_) | copy-start | bytes 294916
  34.6 15.8 %copy-start.4 = (f32[8,128,256]{2,1,0:T(8,128)S(1)}, f32[8,128,256]{2,1,0:T(8,128)}, u32[]{:S(2)}) copy-start(f32[8,128,256]{2,1,0:T(8,128)} %get-tuple-element.21.refs_1_) | copy-start | bytes 3145732
  34.6 15.8 %copy-start.7 = (f32[96,256]{1,0:T(8,128)S(1)}, f32[96,256]{1,0:T(8,128)}, u32[]{:S(2)}) copy-start(f32[96,256]{1,0:T(8,128)} %get-tuple-element.19.frame_any.refs_10_) | copy-start | bytes 294916
  41.5 8.8 %collective-permute-start = (f32[40,256]{1,0:T(8,128)S(1)}, f32[40,256]{1,0:T(8,128)S(1)}, u32[]{:S(2)}, u32[]{:S(2)}) collective-permute-start(f32[40,256]{1,0:T(8,128)S(1)} %get-tuple-element.22), channel_id=1, source_target_pairs={{0,16},{32,48},{64,80},{96,112},{16,0},{48,32},{80,64},{112,96},{1... | collective-permute-start | bytes 122888 | tf_op jit(solution)/shard_map/ppermute | solution.py:313
  41.6 8.8 %collective-permute-start.1 = (f32[40,256]{1,0:T(8,128)S(1)}, f32[40,256]{1,0:T(8,128)S(1)}, u32[]{:S(2)}, u32[]{:S(2)}) collective-permute-start(f32[40,256]{1,0:T(8,128)S(1)} %get-tuple-element.23), channel_id=1, source_target_pairs={{16,32},{48,64},{80,96},{112,0},{32,16},{64,48},{96,80},{0,112},{1... | collective-permute-start | bytes 122888 | tf_op jit(solution)/shard_map/ppermute | solution.py:313
  42.6 5.4 %collective-permute-start.2 = (f32[40,128]{1,0:T(8,128)S(1)}, f32[40,128]{1,0:T(8,128)S(1)}, u32[]{:S(2)}, u32[]{:S(2)}) collective-permute-start(f32[40,128]{1,0:T(8,128)S(1)} %get-tuple-element.24), channel_id=1, source_target_pairs={{0,1},{2,3},{4,5},{6,7},{8,9},{10,11},{12,13},{14,15},{1,0},{3,2},... | collective-permute-start | bytes 61448 | tf_op jit(solution)/shard_map/ppermute | solution.py:313
  43.2 7.1 %collective-permute-start.3 = (f32[40,128]{1,0:T(8,128)S(1)}, f32[40,128]{1,0:T(8,128)S(1)}, u32[]{:S(2)}, u32[]{:S(2)}) collective-permute-start(f32[40,128]{1,0:T(8,128)S(1)} %get-tuple-element.25), channel_id=1, source_target_pairs={{1,2},{3,4},{5,6},{7,8},{9,10},{11,12},{13,14},{15,0},{2,1},{4,3},... | collective-permute-start | bytes 61448 | tf_op jit(solution)/shard_map/ppermute | solution.py:313

commit v6 on v5

--- a/solution.py
+++ b/solution.py
@@ -99,16 +99,22 @@
     out_ref[pl.ds(WORDS, devices, stride=WIRE), :] = jnp.broadcast_to(corner_row(first, final), (devices, 128))
     gather(span, owner_ref, place_ref, column_ref, misfit_ref, acc_ref)
     groups = devices // 4
-    left = lax.broadcasted_iota(jnp.int32, (groups, 128), 1) < CAP
-    for k in range(WORDS):
-        for j in range(2):
-            a = acc_ref[0, pl.ds(k * groups, groups), pl.ds(j * 128, 128)]
-            b = acc_ref[1, pl.ds(k * groups, groups), pl.ds(j * 128, 128)]
-            out_ref[pl.ds(2 * j * WIRE + k, groups, stride=4 * WIRE), :] = jnp.where(left, a, pltpu.roll(b, CAP, 1))
-            out_ref[pl.ds((2 * j + 1) * WIRE + k, groups, stride=4 * WIRE), :] = jnp.where(left, pltpu.roll(a, CAP, 1), b)
-    store = pltpu.make_async_copy(out_ref, out_any, sem.at[5])
-    store.start()
-    store.wait()
+    left = lax.broadcasted_iota(jnp.int32, (groups // 2, 128), 1) < CAP
+    half = groups // 2
+    stores = []
+    for part in range(2):
+        start = part * half * 4 * WIRE
+        for k in range(WORDS):
+            for j in range(2):
+                a = acc_ref[0, pl.ds(k * groups + part * half, half), pl.ds(j * 128, 128)]
+                b = acc_ref[1, pl.ds(k * groups + part * half, half), pl.ds(j * 128, 128)]
+                out_ref[pl.ds(start + 2 * j * WIRE + k, half, stride=4 * WIRE), :] = jnp.where(left, a, pltpu.roll(b, CAP, 1))
+                out_ref[pl.ds(start + (2 * j + 1) * WIRE + k, half, stride=4 * WIRE), :] = jnp.where(left, pltpu.roll(a, CAP, 1), b)
+        rows = pl.ds(start, half * 4 * WIRE)
+        stores.append(pltpu.make_async_copy(out_ref.at[rows], out_any.at[rows], sem.at[5 + part]))
+        stores[part].start()
+    for store in stores:
+        store.wait()
 
 
 def pack(owner, column, misfit, state, devices, span=2048):
@@ -126,7 +132,7 @@
             pltpu.VMEM((STEPS, WORDS * devices // 4, CHUNK), jnp.float32),
             pltpu.VMEM(sent.shape, jnp.float32),
             pltpu.VMEM((2, PLANES, 8, CB), jnp.float32),
-            pltpu.SemaphoreType.DMA((6,)),
+            pltpu.SemaphoreType.DMA((7,)),
         ],
         compiler_params=FULL,
         name="pack",

time: 55.6 us -> 55.4 us (level)
  no operation moved by 1% of the time
where the time goes in v6:
time: 55.4 us; the launch traced here: 55.2 us
  Pallas kernels  28.1 us (51%)
  starting transfers between devices  14.1 us (25%)
  waiting for transfers between devices  10.5 us (19%)
  local copies, waits for them, and re-layouts  2.15 us (4%)
    all_to_all x1, starting transfers between devices, local(): lax.all_to_all(sent.reshape(devices, 1, WIRE * 128), ('tx', 'ty'), split_...  11.1 us
    all_to_all x1, waiting for transfers between devices, local(): lax.all_to_all(sent.reshape(devices, 1, WIRE * 128), ('tx', 'ty'), split_...  8.16 us
    pallas_call x1, Pallas kernels, first_records(): pl.pallas_call(first_records_kernel, out_shape=(HALF,) + LISTS + (jax.Sha...  6.96 us
    pallas_call x1, Pallas kernels, first_step(): pl.pallas_call(functools.partial(step_kernel, False), out_shape=(HALF, HA...  6.75 us
    pallas_call x1, Pallas kernels, pack(): pl.pallas_call(functools.partial(pack_kernel, devices, span), out_shape=s...  6.31 us
    pallas_call x1, Pallas kernels, last_step(): pl.pallas_call(functools.partial(step_kernel, True), out_shape=jax.ShapeD...  4.57 us
    pallas_call x1, Pallas kernels, second_records(): pl.pallas_call(second_records_kernel, out_shape=HALF, in_specs=[WHOLE] *...  3.5 us
    ppermute x4, starting transfers between devices, swapped(): return lax.ppermute(x, axis, pairs + [(j, i) for i, j in pairs])  2.93 us
  transfers between devices with their start and end apart: 5, of which 2 were waited for; matrix products, arithmetic and copies ran while one was open for 0% of the time, Pallas kernels for 19%

profile of v6, /device:TPU:0, one launch (start us, length us, event | category | flops | bytes accessed | tf_op | source)
XLA Modules:
  0.0 55.2 jit_solution(1801919242443758045)
XLA Ops:
  0.0 6.3 %pack.1 = f32[1280,128]{1,0:T(8,128)} custom-call(s32[2,1,4096]{2,1,0:T(1,128)} %bitcast.9, s32[2,4096]{1,0:T(2,128)} %column_any.1, f32[2,8,4096]{2,1,0:T(8,128)} %misfit_any.1, f32[16,128,256]{2,1,0:T(8,128)} %bitcast.6), custom_call_target="tpu_custom_call" | custom-call | tf_op jit(solution)/shard_map/pack/pallas_call | solution.py:122
  6.3 11.1 %all-to-all-start = ((f32[128,1,1280]{2,1,0:T(1,128)}), f32[128,1,1280]{2,1,0:T(1,128)S(1)}, u32[]{:S(2)}, u32[]{:S(2)}) async-start(f32[128,1,1280]{2,1,0:T(1,128)} %bitcast.8), calls=%async_computation | async-start | bytes 1310720 | tf_op jit(solution)/shard_map/all_to_all | solution.py:620
  17.5 0.0 copy-start.5
  17.5 6.8 %first_step.1 = (f32[8,128,256]{2,1,0:T(8,128)}, f32[8,128,256]{2,1,0:T(8,128)}, f32[96,256]{1,0:T(8,128)}) custom-call(f32[16,128,256]{2,1,0:T(8,128)} %bitcast.7, f32[4,128,256]{2,1,0:T(8,128)} %refs_2_.3, f32[3,128,256]{2,1,0:T(8,128)} %refs_3_.3, f32[2,4,128,256]{3,2,1,0:T(8,128)} %refs_4_.3, f32[128,256]{1,0:T(8,128)} %refs_5_.1), custom_call_target="tpu_custom_call" | custom-call | tf_op jit(solution)/shard_map/first_step/pallas_call | solution.py:496
  24.2 0.0 copy-start
  24.3 0.0 copy-start.1
  24.3 0.0 copy-start.2
  24.3 8.2 %all-to-all-done = f32[128,1,1280]{2,1,0:T(1,128)S(1)} async-done(((f32[128,1,1280]{2,1,0:T(1,128)}), f32[128,1,1280]{2,1,0:T(1,128)S(1)}, u32[]{:S(2)}, u32[]{:S(2)}) %all-to-all-start) | async-done | bytes 655392 | tf_op jit(solution)/shard_map/all_to_all | solution.py:620
  32.4 0.0 copy-start.3
  32.4 1.2 %copy-done.3 = f32[8,128,256]{2,1,0:T(8,128)S(1)} copy-done((f32[8,128,256]{2,1,0:T(8,128)S(1)}, f32[8,128,256]{2,1,0:T(8,128)}, u32[]{:S(2)}) %copy-start.3) | copy-done | bytes 1048600
  33.7 0.0 copy-start.6
  33.7 0.9 %copy-done.6 = f32[96,256]{1,0:T(8,128)S(1)} copy-done((f32[96,256]{1,0:T(8,128)S(1)}, f32[96,256]{1,0:T(8,128)}, u32[]{:S(2)}) %copy-start.6) | copy-done | bytes 98328
  34.6 0.0 copy-start.4
  34.6 0.0 copy-start.7
  34.6 7.0 %first_records.1 = (f32[8,128,256]{2,1,0:T(8,128)S(1)}, f32[2,8,32,256]{3,2,1,0:T(8,128)S(1)}, f32[2,8,32,256]{3,2,1,0:T(8,128)S(1)}, f32[2,1,32,256]{3,2,1,0:T(...) custom-call(f32[1280,128]{1,0:T(8,128)S(1)} %bitcast.5, ...), custom_call_target="tpu_custom_call" | custom-call | tf_op jit(solution)/shard_map/first_records/pallas_call | solution.py:583
  41.5 0.1 collective-permute-start
  41.6 1.0 %collective-permute-start.1 = (f32[40,256]{1,0:T(8,128)S(1)}, f32[40,256]{1,0:T(8,128)S(1)}, u32[]{:S(2)}, u32[]{:S(2)}) collective-permute-start(f32[40,256]{1,0:T(8,128)S(1)} %get-tuple-element.23), channel_id=1, source_target_pairs={{16,32},{48,64},{80,96},{112,0},{32,16},{64,48},{96,80},{0,112},{1... | collective-permute-start | bytes 122888 | tf_op jit(solution)/shard_map/ppermute | solution.py:319
  42.6 0.7 %collective-permute-start.2 = (f32[40,128]{1,0:T(8,128)S(1)}, f32[40,128]{1,0:T(8,128)S(1)}, u32[]{:S(2)}, u32[]{:S(2)}) collective-permute-start(f32[40,128]{1,0:T(8,128)S(1)} %get-tuple-element.24), channel_id=1, source_target_pairs={{0,1},{2,3},{4,5},{6,7},{8,9},{10,11},{12,13},{14,15},{1,0},{3,2},... | collective-permute-start | bytes 61448 | tf_op jit(solution)/shard_map/ppermute | solution.py:319
  43.3 1.2 %collective-permute-start.3 = (f32[40,128]{1,0:T(8,128)S(1)}, f32[40,128]{1,0:T(8,128)S(1)}, u32[]{:S(2)}, u32[]{:S(2)}) collective-permute-start(f32[40,128]{1,0:T(8,128)S(1)} %get-tuple-element.25), channel_id=1, source_target_pairs={{1,2},{3,4},{5,6},{7,8},{9,10},{11,12},{13,14},{15,0},{2,1},{4,3},... | collective-permute-start | bytes 61448 | tf_op jit(solution)/shard_map/ppermute | solution.py:319
  44.5 3.5 %second_records.1.refs_12_ = f32[8,128,256]{2,1,0:T(8,128)S(1)} custom-call(f32[2,8,32,256]{3,2,1,0:T(8,128)S(1)} %get-tuple-element.27.high_ref, f32[2,8,32,256]{3,2,1,0:T(8,128)S(1)} %get-tuple-element.28.low_ref, f32[2,1,32,256]{3,2,1,0:T(8,128)S(1)} %get-tuple-element.29.cell_ref, s32[8,128]{1,0:T(8,128)S(1)} %get-tuple-element.30.edge_ref), custom_call_target="tpu_custom_call" | custom-call | tf_op jit(solution)/shard_map/second_records/pallas_call | solution.py:605
  48.0 0.0 collective-permute-done.2.refs_8_
  48.0 2.4 %collective-permute-done.3.refs_9_ = f32[40,128]{1,0:T(8,128)S(1)} collective-permute-done((f32[40,128]{1,0:T(8,128)S(1)}, f32[40,128]{1,0:T(8,128)S(1)}, u32[]{:S(2)}, u32[]{:S(2)}) %collective-permute-start.3) | collective-permute-done | bytes 20512 | tf_op jit(solution)/shard_map/ppermute | solution.py:319
  50.4 0.0 collective-permute-done.refs_6_
  50.4 0.0 collective-permute-done.1.refs_7_
  50.4 0.0 copy-done.5
  50.4 0.0 copy-done
  50.4 0.0 copy-done.1
  50.4 0.0 copy-done.2
  50.4 0.0 copy-done.4
  50.4 0.0 copy-done.7
  50.4 4.6 %last_step.1 = f32[16,128,256]{2,1,0:T(8,128)} custom-call(f32[8,128,256]{2,1,0:T(8,128)S(1)} %get-tuple-element.20.refs_0_, f32[8,128,256]{2,1,0:T(8,128)S(1)} %copy-done.4, f32[4,128,256]{2,1,0:T(8,128)S(1)} %copy-done.1, f32[3,128,256]{2,1,0:T(8,128)S(1)} %copy-done.2, f32[2,4,128,256]{3,2,1,0:T(8,128)S(1)} %copy-done, f32[128,256]{1,0:T(8,128)S(1)} %copy-done.5, ...), custom_call_target="tpu_custom_call" | custom-call | tf_op jit(solution)/shard_map/last_step/pallas_call | solution.py:510
Async XLA Ops:
  6.3 26.1 %all-to-all-start = ((f32[128,1,1280]{2,1,0:T(1,128)}), f32[128,1,1280]{2,1,0:T(1,128)S(1)}, u32[]{:S(2)}, u32[]{:S(2)}) async-start(f32[128,1,1280]{2,1,0:T(1,128)} %bitcast.8), calls=%async_computation | async-start | bytes 1310720 | tf_op jit(solution)/shard_map/all_to_all | solution.py:620
  17.5 32.9 %copy-start.5 = (f32[128,256]{1,0:T(8,128)S(1)}, f32[128,256]{1,0:T(8,128)}, u32[]{:S(2)}) copy-start(f32[128,256]{1,0:T(8,128)} %refs_5_.1) | copy-start | bytes 393220
  24.2 26.1 %copy-start = (f32[2,4,128,256]{3,2,1,0:T(8,128)S(1)}, f32[2,4,128,256]{3,2,1,0:T(8,128)}, u32[]{:S(2)}) copy-start(f32[2,4,128,256]{3,2,1,0:T(8,128)} %refs_4_.3) | copy-start | bytes 3145732
  24.3 26.1 %copy-start.1 = (f32[4,128,256]{2,1,0:T(8,128)S(1)}, f32[4,128,256]{2,1,0:T(8,128)}, u32[]{:S(2)}) copy-start(f32[4,128,256]{2,1,0:T(8,128)} %refs_2_.3) | copy-start | bytes 1572868
  24.3 26.1 %copy-start.2 = (f32[3,128,256]{2,1,0:T(8,128)S(1)}, f32[3,128,256]{2,1,0:T(8,128)}, u32[]{:S(2)}) copy-start(f32[3,128,256]{2,1,0:T(8,128)} %refs_3_.3) | copy-start | bytes 1179652
  32.4 1.2 %copy-start.3 = (f32[8,128,256]{2,1,0:T(8,128)S(1)}, f32[8,128,256]{2,1,0:T(8,128)}, u32[]{:S(2)}) copy-start(f32[8,128,256]{2,1,0:T(8,128)} %get-tuple-element.18.still_any) | copy-start | bytes 3145732
  33.7 0.9 %copy-start.6 = (f32[96,256]{1,0:T(8,128)S(1)}, f32[96,256]{1,0:T(8,128)}, u32[]{:S(2)}) copy-start(f32[96,256]{1,0:T(8,128)} %get-tuple-element.19.frame_any.refs_10_) | copy-start | bytes 294916
  34.6 15.8 %copy-start.4 = (f32[8,128,256]{2,1,0:T(8,128)S(1)}, f32[8,128,256]{2,1,0:T(8,128)}, u32[]{:S(2)}) copy-start(f32[8,128,256]{2,1,0:T(8,128)} %get-tuple-element.21.refs_1_) | copy-start | bytes 3145732
  34.6 15.9 %copy-start.7 = (f32[96,256]{1,0:T(8,128)S(1)}, f32[96,256]{1,0:T(8,128)}, u32[]{:S(2)}) copy-start(f32[96,256]{1,0:T(8,128)} %get-tuple-element.19.frame_any.refs_10_) | copy-start | bytes 294916
  41.5 8.8 %collective-permute-start = (f32[40,256]{1,0:T(8,128)S(1)}, f32[40,256]{1,0:T(8,128)S(1)}, u32[]{:S(2)}, u32[]{:S(2)}) collective-permute-start(f32[40,256]{1,0:T(8,128)S(1)} %get-tuple-element.22), channel_id=1, source_target_pairs={{0,16},{32,48},{64,80},{96,112},{16,0},{48,32},{80,64},{112,96},{1... | collective-permute-start | bytes 122888 | tf_op jit(solution)/shard_map/ppermute | solution.py:319
  41.6 8.7 %collective-permute-start.1 = (f32[40,256]{1,0:T(8,128)S(1)}, f32[40,256]{1,0:T(8,128)S(1)}, u32[]{:S(2)}, u32[]{:S(2)}) collective-permute-start(f32[40,256]{1,0:T(8,128)S(1)} %get-tuple-element.23), channel_id=1, source_target_pairs={{16,32},{48,64},{80,96},{112,0},{32,16},{64,48},{96,80},{0,112},{1... | collective-permute-start | bytes 122888 | tf_op jit(solution)/shard_map/ppermute | solution.py:319
  42.6 5.4 %collective-permute-start.2 = (f32[40,128]{1,0:T(8,128)S(1)}, f32[40,128]{1,0:T(8,128)S(1)}, u32[]{:S(2)}, u32[]{:S(2)}) collective-permute-start(f32[40,128]{1,0:T(8,128)S(1)} %get-tuple-element.24), channel_id=1, source_target_pairs={{0,1},{2,3},{4,5},{6,7},{8,9},{10,11},{12,13},{14,15},{1,0},{3,2},... | collective-permute-start | bytes 61448 | tf_op jit(solution)/shard_map/ppermute | solution.py:319
  43.3 7.1 %collective-permute-start.3 = (f32[40,128]{1,0:T(8,128)S(1)}, f32[40,128]{1,0:T(8,128)S(1)}, u32[]{:S(2)}, u32[]{:S(2)}) collective-permute-start(f32[40,128]{1,0:T(8,128)S(1)} %get-tuple-element.25), channel_id=1, source_target_pairs={{1,2},{3,4},{5,6},{7,8},{9,10},{11,12},{13,14},{15,0},{2,1},{4,3},... | collective-permute-start | bytes 61448 | tf_op jit(solution)/shard_map/ppermute | solution.py:319
